TPU v7x, 512 devices: a whole 4x8x8 slice. The times are simulated.
512 devices in a mesh: ba: 32 (over z, y_lo), dev: 16 (over y_hi, x, core).
Axes of the slice: x: 4, y: 8 (y_hi: 2, y_lo: 4; y = y_hi * 4 + y_lo), z: 8, core: 2. Of those that a mesh axis runs over, the one named last changes fastest.
Arguments:
- factors: bfloat16 [64, 512, 1024], P('ba', 'dev'), may hold values from -0.1875 to 0.1875
- amplitudes: bfloat16 [64, 512, 512], P(None, 'dev'), may hold values from -0.375 to 0.375
- pair_order: int32 [64], replicated, may hold values from 0 to 63, each once
- occ_bin: int32 [8], replicated, may hold values from 0 to 127
- vir_bin: int32 [64], replicated, may hold values from 0 to 127
- levels: float32 [128], replicated, may hold values from 0.1 to 0.8
Outputs:
- update: float32 [64, 4096], P('ba', 'dev')
Inputs may be any that keep to these rules, and one draw needn't show every extreme that they name: `pair_order`: each value appears once; entry k names the ordered occupied pair (value // 8, value % 8). `occ_bin`: orbital i has energy minus levels at its bin. `vir_bin`: window virtual a has energy levels at its bin.
All inputs are finite; a program needn't handle non-finite values.
Results may differ from a plain program's by a relative error of at most 0.0029.
Values may be sent and summed in bfloat16 or wider, within the bound.
No kernel may reach another device: no remote copies, remote signals or barrier semaphores. Data moves between devices by JAX's collectives and lax.ppermute only.
A program may use at most 64 MiB of HBM per device.

v0:
```python
import jax
import jax.numpy as jnp
from jax import lax
from jax.sharding import Mesh
from jax.sharding import PartitionSpec as P

NOCC = 8
BA = ("ba_0", "ba_1")


level_shift = 0.3


def copy_for_each(x, axis):
    copies = jnp.broadcast_to(x, (lax.axis_size(axis), *x.shape))
    return lax.all_to_all(copies, axis, split_axis=0, concat_axis=0, tiled=True)


def in_order(parts, dim):
    dims = list(parts.shape[1:])
    dims[dim] *= parts.shape[0]
    return jnp.moveaxis(parts, 0, dim).reshape(dims)


def gathered_copies(x, axis, dim):
    parts = copy_for_each(x, axis)
    return in_order(parts, dim)


def gathered_by_axis(x, axes, dim):
    out = x
    for number in range(len(axes) - 1, -1, -1):
        out = lax.all_gather(out, axes[number], axis=dim, tiled=True)
    return out


def split_up(x, dim, size):
    dims = x.shape
    parts = x.reshape(*dims[:dim], size, dims[dim] // size, *dims[dim + 1 :])
    return jnp.moveaxis(parts, dim, 0)


def sent_and_summed(x, axis, dim):
    parts = split_up(x, dim, lax.axis_size(axis))
    arrived = lax.all_to_all(parts, axis, split_axis=0, concat_axis=0, tiled=True)
    return arrived.sum(axis=0)


def integral_block(left_side, right_side, contracts):
    left_count, cblock, fitting = left_side.shape
    flat_left = left_side.reshape(left_count * cblock, fitting)
    flat_amps = contracts.reshape(contracts.shape[0], -1)
    results = []
    for position in range(right_side.shape[0]):
        integrals = lax.dot_general(
            flat_left,
            right_side[position],
            (((1,), (1,)), ((), ())),
            preferred_element_type=jnp.float32,
        )
        integrals = integrals.astype(jnp.bfloat16).reshape(left_count, -1)
        results.append(
            lax.dot_general(
                integrals, flat_amps, (((1,), (1,)), ((), ())), preferred_element_type=jnp.float32
            )
        )
    return jnp.stack(results)


def lookup(indices, table):
    choices_range = jnp.arange(table.shape[0], dtype=jnp.int32)
    return jnp.sum(
        jnp.where(indices[:, None] == choices_range[None, :], table[None, :], 0.0), axis=1
    )


def per_device(factors, amplitudes, pair_order, occ_bin, vir_bin, levels):
    owned = factors.shape[0]
    window = owned * lax.axis_size(BA)
    pair_count = amplitudes.shape[0]
    split_rows = window // lax.axis_size("dev")
    swapped = pair_order % NOCC * NOCC + pair_order // NOCC
    matches = swapped[:, None] == pair_order[None, :]
    right_side = gathered_copies(factors, "dev", 1)
    left_side = gathered_by_axis(factors, BA, 0)
    ladder = integral_block(left_side, right_side, amplitudes)
    moved = lax.all_to_all(ladder, BA, split_axis=1, concat_axis=0, tiled=True)
    flipped = jnp.transpose(moved, (1, 0, 2))
    permuter = matches.astype(jnp.float32)
    combined = ladder + jnp.matmul(flipped, permuter.T, precision=lax.Precision.HIGHEST)
    summed = sent_and_summed(combined, "dev", 1)
    virtual_energy = lookup(vir_bin, levels)
    occupied_energy = -lookup(occ_bin, levels)
    pair_energy = lookup(pair_order // NOCC, occupied_energy) + lookup(
        pair_order % NOCC, occupied_energy
    )
    left_energy = lax.dynamic_slice_in_dim(
        virtual_energy, lax.axis_index("dev") * split_rows, split_rows
    )
    right_energy = lax.dynamic_slice_in_dim(virtual_energy, lax.axis_index(BA) * owned, owned)
    denominator = (
        right_energy[:, None, None]
        + left_energy[None, :, None]
        - pair_energy[None, None, :]
        + level_shift
    )
    return (summed / denominator).reshape(owned, split_rows * pair_count)


def solution(mesh):
    finer = Mesh(mesh.devices.reshape(8, 4, mesh.shape["dev"]), ("ba_0", "ba_1", "dev"))
    return jax.shard_map(
        per_device,
        mesh=finer,
        in_specs=(P(BA, "dev", None), P(None, "dev", None), P(), P(), P(), P()),
        out_specs=P(BA, "dev"),
        check_vma=False,
    )
```

profile of v0, /device:TPU:1, one launch (start us, length us, event | category | flops | bytes accessed | tf_op | source)
XLA Modules:
  0.0 163.9 jit_solution(10252828465435802927)
XLA Ops:
  6.5 0.0 all-gather.2.cloned.1.call-start
  6.5 15.2 %all_gather.6 = bf16[8,32,1024]{2,1,0:T(8,128)(2,1)} all-gather(bf16[2,32,1024]{2,1,0:T(8,128)(2,1)} %param.6), channel_id=1, replica_groups=mesh['ba_0'=8,'ba_1'=4,'dev'=16] {'ba_1'}, dimensions={0}, use_global_device_ids=true | all-gather | bytes 655360 | tf_op jit(solution)/shard_map/all_gather | solution.py:33
  21.8 0.0 all-gather.2.cloned.1.call-update
  21.8 2.5 %broadcast_in_dim.60 = bf16[16,2,32,1024]{3,2,1,0:T(8,128)(2,1)} broadcast(bf16[2,32,1024]{2,1,0:T(8,128)(2,1)} %param.6), dimensions={1,2,3} | broadcast | bytes 2228224 | tf_op jit(solution)/shard_map/broadcast_in_dim | solution.py:15
  24.3 12.2 %all-to-all-start = ((bf16[16,2,32,1024]{3,2,1,0:T(8,128)(2,1)}), bf16[16,2,32,1024]{3,2,1,0:T(8,128)(2,1)}, u32[]{:S(2)}, u32[]{:S(2)}) async-start(bf16[16,2,32,1024]{3,2,1,0:T(8,128)(2,1)} %broadcast_in_dim.60), calls=%async_computation | async-start | bytes 4194304 | tf_op jit(solution)/shard_map/all_to_all | solution.py:16
  36.5 0.0 copy-start.2
  36.5 0.0 copy-start.3
  36.6 0.0 copy-start.1
  36.6 2.8 %copy.14 = bf16[8,8,32,512]{3,1,2,0:T(8,128)(2,1)S(1)} copy(bf16[8,8,32,512]{3,2,1,0:T(8,128)(2,1)} %bitcast.38) | data formatting | bytes 4194304
  39.4 0.0 copy-done.2
  39.4 0.0 copy-done.3
  39.4 0.2 select_reduce_fusion
  39.6 0.1 dynamic_slice.7
  39.7 0.1 dynamic_slice.6
  39.8 0.1 broadcast_add_fusion
  39.8 0.1 sub.29
  39.9 0.1 sub.30
  40.0 0.0 copy-done.1
  40.0 39.9 %all-to-all-done = bf16[16,2,32,1024]{3,2,1,0:T(8,128)(2,1)} async-done(((bf16[16,2,32,1024]{3,2,1,0:T(8,128)(2,1)}), bf16[16,2,32,1024]{3,2,1,0:T(8,128)(2,1)}, u32[]{:S(2)}, u32[]{:S(2)}) %all-to-all-start) | async-done | bytes 2097184 | tf_op jit(solution)/shard_map/all_to_all | solution.py:16
  80.0 2.9 %fusion.4 = (bf16[1,16,32,1024]{3,2,0,1:T(8,128)(2,1)S(1)}, bf16[1,16,32,1024]{3,2,0,1:T(8,128)(2,1)}) fusion(bf16[2,16,32,1024]{3,2,0,1:T(8,128)(2,1)} %bitcast.1), kind=kLoop, calls=%fused_computation.27 | loop fusion | bytes 4194304 | tf_op jit(solution)/shard_map/slice | solution.py:57
  82.9 4.0 %all-gather.2.cloned.1.call-done = bf16[64,32,1024]{2,1,0:T(8,128)(2,1)} async-done(((bf16[8,32,1024]{2,1,0:T(8,128)(2,1)}), bf16[64,32,1024]{2,1,0:T(8,128)(2,1)}) %all-gather.2.cloned.1.call-update) | async-done | bytes 4194320 | tf_op jit(solution)/shard_map/all_gather | solution.py:33
  86.8 6.2 %convolution_convert_fusion = bf16[2048,512]{1,0:T(8,128)(2,1)} fusion(bf16[2048,1024]{1,0:T(8,128)(2,1)} %bitcast.46, bf16[512,1024]{1,0:T(8,128)(2,1)} %bitcast.40), kind=kOutput, calls=%fused_computation | convolution fusion | flops 2148532224 | bytes 7340032 | tf_op jit(solution)/shard_map/dot_general | solution.py:55
  93.1 4.2 %reshape.74 = bf16[64,16384]{1,0:T(8,128)(2,1)} reshape(bf16[2048,512]{1,0:T(8,128)(2,1)} %convolution_convert_fusion) | data formatting | bytes 4194304 | tf_op jit(solution)/shard_map/reshape | solution.py:61
  97.3 5.9 %convolution_convert_fusion.1 = bf16[2048,512]{1,0:T(8,128)(2,1)} fusion(bf16[2048,1024]{1,0:T(8,128)(2,1)} %bitcast.47, bf16[512,1024]{1,0:T(8,128)(2,1)S(1)} %bitcast.39), kind=kOutput, calls=%fused_computation.1 | convolution fusion | flops 2148532224 | bytes 7340032 | tf_op jit(solution)/shard_map/dot_general | solution.py:55
  103.2 4.2 %reshape.72 = bf16[64,16384]{1,0:T(8,128)(2,1)} reshape(bf16[2048,512]{1,0:T(8,128)(2,1)} %convolution_convert_fusion.1) | data formatting | bytes 4194304 | tf_op jit(solution)/shard_map/reshape | solution.py:61
  107.4 0.0 copy-start
  107.4 2.4 %convolution_bitcast_fusion = f32[1,64,64]{2,1,0:T(8,128)S(1)} fusion(bf16[64,16384]{1,0:T(8,128)(2,1)} %reshape.74, bf16[64,16384]{1,0:T(8,128)(2,1)S(1)} %bitcast.36), kind=kOutput, calls=%fused_computation.3 | convolution fusion | flops 134217728 | bytes 4210688 | tf_op jit(solution)/shard_map/dot_general | solution.py:63
  109.8 0.0 copy-done
  109.8 0.0 copy-start.4
  109.8 0.7 convolution_bitcast_fusion.1
  110.6 0.1 copy.18
  110.6 0.7 reshape.77
  111.3 16.6 %all-to-all-start.1 = ((f32[32,1,256]{2,1,0:T(1,128)}), f32[32,1,256]{2,1,0:T(1,128)S(1)}, u32[]{:S(2)}, u32[]{:S(2)}) async-start(f32[32,1,256]{2,1,0:T(1,128)} %reshape.77), calls=%async_computation.1 | async-start | bytes 65536 | tf_op jit(solution)/shard_map/all_to_all | solution.py:87
  127.9 0.0 copy-done.4
  127.9 0.2 select_reduce_fusion.3
  128.1 8.9 %all-to-all-done.1 = f32[32,1,256]{2,1,0:T(1,128)S(1)} async-done(((f32[32,1,256]{2,1,0:T(1,128)}), f32[32,1,256]{2,1,0:T(1,128)S(1)}, u32[]{:S(2)}, u32[]{:S(2)}) %all-to-all-start.1) | async-done | bytes 32800 | tf_op jit(solution)/shard_map/all_to_all | solution.py:87
  137.0 0.5 broadcast.61
  137.5 0.7 reduce
  138.3 0.1 reshape.78
  138.4 0.2 convolution_add_fusion
  138.7 0.7 reshape.79
  139.4 6.5 %all-to-all-start.2 = ((f32[16,1,512]{2,1,0:T(1,128)}), f32[16,1,512]{2,1,0:T(1,128)S(1)}, u32[]{:S(2)}, u32[]{:S(2)}) async-start(f32[16,1,512]{2,1,0:T(1,128)} %reshape.79), calls=%async_computation.2 | async-start | bytes 65536 | tf_op jit(solution)/shard_map/all_to_all | solution.py:45
  145.9 0.1 select_reduce_fusion.1
  146.0 0.1 sub.32
  146.0 9.5 %all-to-all-done.2 = f32[16,1,512]{2,1,0:T(1,128)S(1)} async-done(((f32[16,1,512]{2,1,0:T(1,128)}), f32[16,1,512]{2,1,0:T(1,128)S(1)}, u32[]{:S(2)}, u32[]{:S(2)}) %all-to-all-start.2) | async-done | bytes 32800 | tf_op jit(solution)/shard_map/all_to_all | solution.py:45
  155.6 0.7 reduce.1
  156.3 0.1 reshape.80
  156.4 0.1 reduce_sum.48
  156.5 0.6 add_divide_fusion
  (8 shorter events, 0.1 us)
Async XLA Ops:
  6.5 80.3 %all-gather.2.cloned.1.call-start = ((), (), s32[]{:S(2)}) async-start(), calls=%async_computation.3 | async-start | bytes 4718592 | tf_op jit(solution)/shard_map/all_gather | solution.py:33
  24.3 55.7 %all-to-all-start = ((bf16[16,2,32,1024]{3,2,1,0:T(8,128)(2,1)}), bf16[16,2,32,1024]{3,2,1,0:T(8,128)(2,1)}, u32[]{:S(2)}, u32[]{:S(2)}) async-start(bf16[16,2,32,1024]{3,2,1,0:T(8,128)(2,1)} %broadcast_in_dim.60), calls=%async_computation | async-start | bytes 4194304 | tf_op jit(solution)/shard_map/all_to_all | solution.py:16
  36.5 2.9 %copy-start.2 = (s32[64]{0:T(128)S(1)}, s32[64]{0:T(128)}, u32[]{:S(2)}) copy-start(s32[64]{0:T(128)} %param.10) | copy-start | bytes 772
  36.5 2.9 %copy-start.3 = (f32[128]{0:T(128)S(1)}, f32[128]{0:T(128)}, u32[]{:S(2)}) copy-start(f32[128]{0:T(128)} %param.11) | copy-start | bytes 1540
  36.6 3.4 %copy-start.1 = (s32[64]{0:T(128)S(1)}, s32[64]{0:T(128)}, u32[]{:S(2)}) copy-start(s32[64]{0:T(128)} %param.8) | copy-start | bytes 772
  107.4 2.4 %copy-start = (bf16[64,16384]{1,0:T(8,128)(2,1)S(1)}, bf16[64,16384]{1,0:T(8,128)(2,1)}, u32[]{:S(2)}) copy-start(bf16[64,16384]{1,0:T(8,128)(2,1)} %reshape.72) | copy-start | bytes 6291460
  109.8 18.1 %copy-start.4 = (s32[8]{0:T(128)S(1)}, s32[8]{0:T(128)}, u32[]{:S(2)}) copy-start(s32[8]{0:T(128)} %param.9) | copy-start | bytes 100
  111.3 25.7 %all-to-all-start.1 = ((f32[32,1,256]{2,1,0:T(1,128)}), f32[32,1,256]{2,1,0:T(1,128)S(1)}, u32[]{:S(2)}, u32[]{:S(2)}) async-start(f32[32,1,256]{2,1,0:T(1,128)} %reshape.77), calls=%async_computation.1 | async-start | bytes 65536 | tf_op jit(solution)/shard_map/all_to_all | solution.py:87
  139.4 16.2 %all-to-all-start.2 = ((f32[16,1,512]{2,1,0:T(1,128)}), f32[16,1,512]{2,1,0:T(1,128)S(1)}, u32[]{:S(2)}, u32[]{:S(2)}) async-start(f32[16,1,512]{2,1,0:T(1,128)} %reshape.79), calls=%async_computation.2 | async-start | bytes 65536 | tf_op jit(solution)/shard_map/all_to_all | solution.py:45
Sparse Core Ops, SparseCore 0:
  21.9 64.8 all-gather.1
where the time goes:
time: 165 us; the launch traced here: 164 us
  waiting for transfers between devices  62.4 us (38%)
  starting transfers between devices  35.3 us (21%)
  local copies, waits for them, and re-layouts  19.4 us (12%)
  matrix products  15.5 us (9%)
  blocking collectives  15.2 us (9%)
  between operations  13.6 us (8%)
  other arithmetic  2.61 us (2%)
    all_to_all x1, waiting for transfers between devices, copy_for_each(): return lax.all_to_all(copies, axis, split_axis=0, concat_axis=0, tiled=True)  39.9 us
    all_to_all x1, starting transfers between devices, per_device(): moved = lax.all_to_all(ladder, BA, split_axis=1, concat_axis=0, tiled=True)  16.6 us
    all_gather x1, blocking collectives, gathered_by_axis(): out = lax.all_gather(out, axes[number], axis=dim, tiled=True)  15.2 us
    all_to_all x1, starting transfers between devices, copy_for_each(): return lax.all_to_all(copies, axis, split_axis=0, concat_axis=0, tiled=True)  12.2 us
    dot_general x2, matrix products, integral_block(): lax.dot_general(flat_left, right_side[position], (((1,), (1,)), ((), ()))...  12.1 us
    all_to_all x1, waiting for transfers between devices, sent_and_summed(): lax.all_to_all(parts, axis, split_axis=0, concat_axis=0, tiled=True)  9.53 us
    all_to_all x1, waiting for transfers between devices, per_device(): moved = lax.all_to_all(ladder, BA, split_axis=1, concat_axis=0, tiled=True)  8.92 us
    reshape x2, local copies, waits for them, and re-layouts, integral_block(): integrals = integrals.astype(jnp.bfloat16).reshape(left_count, -1)  8.41 us
  transfers between devices with their start and end apart: 4, of which 4 were waited for; matrix products, arithmetic and copies ran while one was open for 6% of the time, Pallas kernels for 0%

commit v1 on v0

v1 whole, which is shorter than its diff:
```python
import functools

import jax
import jax.numpy as jnp
from jax import lax
from jax.experimental import pallas as pl
from jax.experimental.pallas import tpu as pltpu
from jax.sharding import Mesh
from jax.sharding import PartitionSpec as P

NOCC = 8
AXES = ("z", "yl", "yh", "x", "c")
SIZES = (8, 4, 2, 4, 2)
BA = ("z", "yl")
DEV = ("yh", "x", "c")
GROUP = ("yl", "yh", "x", "c")
level_shift = 0.3
CSTEP = 4


def lookup(indices, table):
    choices_range = jnp.arange(table.shape[0], dtype=jnp.int32)
    return jnp.sum(
        jnp.where(indices[:, None] == choices_range[None, :], table[None, :], 0.0), axis=1
    )


def ladder_kernel(amps_ref, right_ref, left_ref, out_ref, bmat, xs, acc):
    step = pl.program_id(0)

    @pl.when(step == 0)
    def _():
        acc[...] = jnp.zeros_like(acc)
        for yl in range(4):
            for r in range(2):
                for yh in range(2):
                    for x in range(4):
                        for c in range(2):
                            d = ((yh * 4 + x) * 2 + c) * 32
                            b = yl * 2 + r
                            bmat[d : d + 32, b * 256 : (b + 1) * 256] = right_ref[c, x, yh, yl, r]

    amps = amps_ref[...].reshape(CSTEP * 64, 512)
    for b in range(8):
        prod = jnp.dot(
            amps, bmat[:, b * 256 : (b + 1) * 256], preferred_element_type=jnp.float32
        ).astype(jnp.bfloat16)
        for cc in range(CSTEP):
            xs[cc, b * 64 : (b + 1) * 64, :] = prod[cc * 64 : (cc + 1) * 64]
    total = acc[...]
    for cc in range(CSTEP):
        total += lax.dot_general(
            xs[cc], left_ref[cc], (((1,), (1,)), ((), ())), preferred_element_type=jnp.float32
        )
    acc[...] = total

    @pl.when(step == pl.num_programs(0) - 1)
    def _():
        for yl in range(4):
            w = acc[yl * 128 : (yl + 1) * 128, :].T
            for ac in range(16):
                out_ref[yl * 16 + ac, 0:4, :] = w[ac * 4 : ac * 4 + 4, :]
            c1, i2 = yl // 2, yl % 2
            for big in range(8):
                for yl1 in range(4):
                    out_ref[(yl1 * 8 + big) * 2 + c1, 4 + 2 * i2 : 6 + 2 * i2, :] = w[
                        8 * big + 2 * yl1 : 8 * big + 2 * yl1 + 2, :
                    ]


def ladder_parts(amps, right, left):
    return pl.pallas_call(
        ladder_kernel,
        grid=(32 // CSTEP,),
        in_specs=[
            pl.BlockSpec((CSTEP, 64, 512), lambda i: (i, 0, 0)),
            pl.BlockSpec((2, 4, 2, 4, 2, 32, 256), lambda i: (0,) * 7),
            pl.BlockSpec((CSTEP, 64, 256), lambda i: (i, 0, 0)),
        ],
        out_specs=pl.BlockSpec((64, 8, 128), lambda i: (0, 0, 0)),
        out_shape=jax.ShapeDtypeStruct((64, 8, 128), jnp.float32),
        scratch_shapes=[
            pltpu.VMEM((512, 2048), jnp.bfloat16),
            pltpu.VMEM((CSTEP, 512, 256), jnp.bfloat16),
            pltpu.VMEM((512, 64), jnp.float32),
        ],
        compiler_params=pltpu.CompilerParams(
            dimension_semantics=("arbitrary",), vmem_limit_bytes=32 * 1024 * 1024
        ),
        cost_estimate=pl.CostEstimate(
            flops=2 * 2048 * 512 * 2048 + 2 * 64 * 64 * 8 * 8192,
            bytes_accessed=6 * 1024 * 1024,
            transcendentals=0,
        ),
    )(amps, right, left)


def swap_pairs():
    pairs = []
    for z in range(8):
        for yl in range(4):
            for big in range(8):
                for c in range(2):
                    pairs.append((((z * 4 + yl) * 8 + big) * 2 + c, ((big * 4 + yl) * 8 + z) * 2 + c))
    return pairs


def per_device(factors, amplitudes, pair_order, occ_bin, vir_bin, levels):
    quarters = factors.reshape(64, 4, 256).transpose(1, 0, 2)
    quarters = jnp.broadcast_to(quarters[None], (2, 4, 64, 256)).reshape(8, 64, 256)
    rows = lax.all_to_all(quarters, ("yh", "yl"), 0, 0, tiled=True)
    own = lax.dynamic_slice_in_dim(rows, lax.axis_index("yh") * 4, 4)
    everyone = jnp.broadcast_to(rows.reshape(1, 512, 256), (4, 512, 256))
    right = lax.all_to_all(everyone, "x", 0, 0, tiled=True)
    right = lax.all_gather(right, "c", axis=0, tiled=False)
    right = right.reshape(2, 4, 2, 4, 2, 32, 256)
    own = jnp.broadcast_to(own.reshape(1, 256, 256), (8, 256, 256))
    left = lax.all_to_all(own, "z", 0, 0, tiled=True)
    left = left.reshape(64, 32, 256).transpose(1, 0, 2)
    amps = amplitudes.transpose(1, 0, 2)
    parts = ladder_parts(amps, right, left)
    parts = lax.all_to_all(parts, GROUP, 0, 0, tiled=True)
    summed = parts.sum(axis=0)
    direct = summed[:4].reshape(4, 2, 64)
    flipped = lax.ppermute(summed[4:], AXES, swap_pairs())
    flipped = flipped.reshape(2, 2, 2, 64).transpose(0, 2, 1, 3).reshape(4, 2, 64)

    swapped = pair_order % NOCC * NOCC + pair_order // NOCC
    matches = swapped[:, None] == pair_order[None, :]
    partnered = jnp.sum(
        jnp.where(matches[None, None], flipped[:, :, None, :], 0.0), axis=-1
    )
    total = (direct + partnered).transpose(1, 0, 2)

    virtual_energy = lookup(vir_bin, levels)
    occupied_energy = -lookup(occ_bin, levels)
    pair_energy = lookup(pair_order // NOCC, occupied_energy) + lookup(
        pair_order % NOCC, occupied_energy
    )
    left_energy = lax.dynamic_slice_in_dim(virtual_energy, lax.axis_index(DEV) * 4, 4)
    right_energy = lax.dynamic_slice_in_dim(virtual_energy, lax.axis_index(BA) * 2, 2)
    denominator = (
        right_energy[:, None, None]
        + left_energy[None, :, None]
        - pair_energy[None, None, :]
        + level_shift
    )
    return (total / denominator).reshape(2, 256)


def solution(mesh):
    finer = Mesh(mesh.devices.reshape(SIZES), AXES)
    return jax.shard_map(
        per_device,
        mesh=finer,
        in_specs=(P(BA, DEV, None), P(None, DEV, None), P(), P(), P(), P()),
        out_specs=P(BA, DEV),
        check_vma=False,
    )
```

time: 165 us -> 133 us (0.81)
  the two profiles are of different devices: /device:TPU:1 before, /device:TPU:56 now
where the time goes in v1:
time: 133 us
  waiting for transfers between devices  41.6 us (31%)
  blocking collectives  31.1 us (23%)
  starting transfers between devices  26.4 us (20%)
  between operations  13.5 us (10%)
  local copies, waits for them, and re-layouts  10.3 us (8%)
  Pallas kernels  9.07 us (7%)
    all_to_all x1, waiting for transfers between devices, per_device(): left = lax.all_to_all(own, 'z', 0, 0, tiled=True)  22.4 us
    all_to_all x1, blocking collectives, per_device(): right = lax.all_to_all(everyone, 'x', 0, 0, tiled=True)  15.7 us
    all_to_all x1, blocking collectives, per_device(): rows = lax.all_to_all(quarters, ('yh', 'yl'), 0, 0, tiled=True)  15.4 us
    all_to_all x1, starting transfers between devices, per_device(): parts = lax.all_to_all(parts, GROUP, 0, 0, tiled=True)  10.8 us
    all_to_all x1, waiting for transfers between devices, per_device(): parts = lax.all_to_all(parts, GROUP, 0, 0, tiled=True)  10.4 us
    all_to_all x1, starting transfers between devices, per_device(): left = lax.all_to_all(own, 'z', 0, 0, tiled=True)  10.3 us
    pallas_call x1, Pallas kernels, ladder_parts(): pl.pallas_call(ladder_kernel, grid=(32 // CSTEP,), in_specs=[pl.BlockSpec...  9.07 us
    ppermute x1, waiting for transfers between devices, per_device(): flipped = lax.ppermute(summed[4:], AXES, swap_pairs())  8.78 us
  transfers between devices with their start and end apart: 4, of which 3 were waited for; matrix products, arithmetic and copies ran while one was open for 5% of the time, Pallas kernels for 0%

profile of v1, /device:TPU:56, one launch (start us, length us, event | category | flops | bytes accessed | tf_op | source)
XLA Modules:
  0.0 132.8 jit_solution(12777356475223925553)
XLA Ops:
  6.5 0.0 all-gather.3.cloned.1.call-start
  6.5 1.0 reshape.99
  7.6 15.4 %all_to_all.20 = bf16[8,64,256]{2,1,0:T(8,128)(2,1)S(1)} all-to-all(bf16[8,64,256]{2,1,0:T(8,128)(2,1)S(1)} %bitcast.21), channel_id=1, replica_groups=mesh['z'=8,'yl'=4,'yh'=2,'x'=4,'c'=2] {'yh','yl'}, dimensions={0} | all-to-all | bytes 524288 | tf_op jit(solution)/shard_map/all_to_all | solution.py:111
  22.9 0.1 broadcast_in_dim.102
  23.0 15.7 %all_to_all.21 = bf16[4,512,256]{2,1,0:T(8,128)(2,1)} all-to-all(bf16[4,512,256]{2,1,0:T(8,128)(2,1)S(1)} %broadcast_in_dim.102), channel_id=1, replica_groups=mesh['z'=8,'yl'=4,'yh'=2,'x'=4,'c'=2] {'x'}, dimensions={0} | all-to-all | bytes 2097152 | tf_op jit(solution)/shard_map/all_to_all | solution.py:114
  38.7 0.0 copy-start.3
  38.7 0.0 copy-start.4
  38.7 0.0 all-gather.3.cloned.1.call-update
  38.8 1.1 broadcast_in_dim.104
  39.8 10.3 %all-to-all-start.2 = ((bf16[8,256,256]{2,1,0:T(8,128)(2,1)}), bf16[8,256,256]{2,1,0:T(8,128)(2,1)S(1)}, u32[]{:S(2)}, u32[]{:S(2)}) async-start(bf16[8,256,256]{2,1,0:T(8,128)(2,1)} %broadcast_in_dim.104), calls=%async_computation.2 | async-start | bytes 2097152 | tf_op jit(solution)/shard_map/all_to_all | solution.py:118
  50.1 0.0 copy-done.3
  50.1 0.0 copy-done.4
  50.1 0.2 select_reduce_fusion.1
  50.3 0.1 dynamic_slice.11
  50.4 0.1 dynamic_slice.10
  50.5 0.0 copy-start.2
  50.5 2.8 %copy.29 = bf16[64,32,512]{2,0,1:T(8,128)(2,1)S(1)} copy(bf16[64,32,512]{2,1,0:T(8,128)(2,1)} %param.7) | data formatting | bytes 4194304 | tf_op args[1]
  53.2 0.0 copy-done.2
  53.3 22.4 %all-to-all-done.2 = bf16[8,256,256]{2,1,0:T(8,128)(2,1)S(1)} async-done(((bf16[8,256,256]{2,1,0:T(8,128)(2,1)}), bf16[8,256,256]{2,1,0:T(8,128)(2,1)S(1)}, u32[]{:S(2)}, u32[]{:S(2)}) %all-to-all-start.2) | async-done | bytes 1048608 | tf_op jit(solution)/shard_map/all_to_all | solution.py:118
  75.6 0.0 copy-start.1
  75.6 1.0 copy-done.1
  76.6 1.8 %copy.30 = bf16[64,32,256]{2,0,1:T(8,128)(2,1)S(1)} copy(bf16[64,32,256]{2,1,0:T(8,128)(2,1)} %bitcast.19) | data formatting | bytes 2097152 | tf_op jit(solution)/shard_map/reshape | solution.py:119
  78.4 0.0 all-gather.3.cloned.1.call-done
  78.5 0.0 copy-start
  78.5 1.6 %copy-done = bf16[8,512,256]{2,1,0:T(8,128)(2,1)S(1)} copy-done((bf16[8,512,256]{2,1,0:T(8,128)(2,1)S(1)}, bf16[8,512,256]{2,1,0:T(8,128)(2,1)}, u32[]{:S(2)}) %copy-start) | copy-done | bytes 2097176
  80.1 0.0 copy-start.5
  80.1 9.1 %shard_map.64 = f32[64,8,128]{2,1,0:T(8,128)} custom-call(bf16[32,64,512]{2,1,0:T(8,128)(2,1)S(1)} %bitcast.16, bf16[2,4,2,4,2,32,256]{6,5,4,3,2,1,0:T(8,128)(2,1)S(1)} %bitcast.18, bf16[32,64,256]{2,1,0:T(8,128)(2,1)S(1)} %bitcast.17), custom_call_target="tpu_custom_call" | custom-call | flops 4831838208 | bytes 6291456 | tf_op jit(solution)/shard_map/pallas_call | solution.py:72
  89.1 10.8 %all-to-all-start.3 = ((f32[64,8,128]{2,1,0:T(8,128)}), f32[64,8,128]{2,1,0:T(8,128)S(1)}, u32[]{:S(2)}, u32[]{:S(2)}) async-start(f32[64,8,128]{2,1,0:T(8,128)} %shard_map.64), calls=%async_computation.3 | async-start | bytes 524288 | tf_op jit(solution)/shard_map/all_to_all | solution.py:122
  100.0 0.0 copy-done.5
  100.0 0.2 select_reduce_fusion.4
  100.2 0.1 broadcast_add_fusion
  100.2 0.1 broadcast_compare_fusion
  100.3 10.4 %all-to-all-done.3 = f32[64,8,128]{2,1,0:T(8,128)S(1)} async-done(((f32[64,8,128]{2,1,0:T(8,128)}), f32[64,8,128]{2,1,0:T(8,128)S(1)}, u32[]{:S(2)}, u32[]{:S(2)}) %all-to-all-start.3) | async-done | bytes 262176 | tf_op jit(solution)/shard_map/all_to_all | solution.py:122
  110.7 0.1 reduce_sum.54
  110.8 5.2 %collective-permute-start = (f32[4,128]{1,0:T(4,128)S(1)}, f32[4,128]{1,0:T(4,128)S(1)}, u32[]{:S(2)}, u32[]{:S(2)}) collective-permute-start(f32[4,128]{1,0:T(4,128)S(1)} %get-tuple-element.10), channel_id=1, source_target_pairs={{0,0},{1,1},{2,64},{3,65},{4,128},{5,129},{6,192},{7,193},{8,256},... | collective-permute-start | bytes 6152 | tf_op jit(solution)/shard_map/ppermute | solution.py:125
  116.0 0.1 select_reduce_fusion.2
  116.1 0.1 reshape.103
  116.2 8.8 %collective-permute-done = f32[4,128]{1,0:T(4,128)S(1)} collective-permute-done((f32[4,128]{1,0:T(4,128)S(1)}, f32[4,128]{1,0:T(4,128)S(1)}, u32[]{:S(2)}, u32[]{:S(2)}) %collective-permute-start) | collective-permute-done | bytes 2080 | tf_op jit(solution)/shard_map/ppermute | solution.py:125
  125.0 0.1 reshape.104
  125.1 0.2 select_reduce_fusion
  125.2 0.1 bitcast_divide_fusion
  125.3 0.7 reshape.105
  (9 shorter events, 0.1 us)
Async XLA Ops:
  6.5 71.9 %all-gather.3.cloned.1.call-start = ((), (), s32[]{:S(2)}) async-start(), calls=%async_computation.4 | async-start | bytes 3145728 | tf_op jit(solution)/shard_map/all_gather | solution.py:115
  38.7 11.4 %copy-start.3 = (s32[64]{0:T(128)S(1)}, s32[64]{0:T(128)}, u32[]{:S(2)}) copy-start(s32[64]{0:T(128)} %param.10) | copy-start | bytes 772
  38.7 11.4 %copy-start.4 = (f32[128]{0:T(128)S(1)}, f32[128]{0:T(128)}, u32[]{:S(2)}) copy-start(f32[128]{0:T(128)} %param.11) | copy-start | bytes 1540
  39.8 35.8 %all-to-all-start.2 = ((bf16[8,256,256]{2,1,0:T(8,128)(2,1)}), bf16[8,256,256]{2,1,0:T(8,128)(2,1)S(1)}, u32[]{:S(2)}, u32[]{:S(2)}) async-start(bf16[8,256,256]{2,1,0:T(8,128)(2,1)} %broadcast_in_dim.104), calls=%async_computation.2 | async-start | bytes 2097152 | tf_op jit(solution)/shard_map/all_to_all | solution.py:118
  50.5 2.8 %copy-start.2 = (s32[64]{0:T(128)S(1)}, s32[64]{0:T(128)}, u32[]{:S(2)}) copy-start(s32[64]{0:T(128)} %param.8) | copy-start | bytes 772
  75.6 1.0 copy-start.1
  78.5 1.6 %copy-start = (bf16[8,512,256]{2,1,0:T(8,128)(2,1)S(1)}, bf16[8,512,256]{2,1,0:T(8,128)(2,1)}, u32[]{:S(2)}) copy-start(bf16[8,512,256]{2,1,0:T(8,128)(2,1)} %all-gather.3.cloned.1.call-done) | copy-start | bytes 6291460
  80.1 19.9 %copy-start.5 = (s32[8]{0:T(128)S(1)}, s32[8]{0:T(128)}, u32[]{:S(2)}) copy-start(s32[8]{0:T(128)} %param.9) | copy-start | bytes 100
  89.1 21.6 %all-to-all-start.3 = ((f32[64,8,128]{2,1,0:T(8,128)}), f32[64,8,128]{2,1,0:T(8,128)S(1)}, u32[]{:S(2)}, u32[]{:S(2)}) async-start(f32[64,8,128]{2,1,0:T(8,128)} %shard_map.64), calls=%async_computation.3 | async-start | bytes 524288 | tf_op jit(solution)/shard_map/all_to_all | solution.py:122
  110.8 14.2 %collective-permute-start = (f32[4,128]{1,0:T(4,128)S(1)}, f32[4,128]{1,0:T(4,128)S(1)}, u32[]{:S(2)}, u32[]{:S(2)}) collective-permute-start(f32[4,128]{1,0:T(4,128)S(1)} %get-tuple-element.10), channel_id=1, source_target_pairs={{0,0},{1,1},{2,64},{3,65},{4,128},{5,129},{6,192},{7,193},{8,256},... | collective-permute-start | bytes 6152 | tf_op jit(solution)/shard_map/ppermute | solution.py:125
Sparse Core Ops, SparseCore 0:
  38.8 22.1 all-gather.2

commit v2 on v1

v2 whole, which is shorter than its diff:
```python
import functools

import jax
import jax.numpy as jnp
from jax import lax
from jax.experimental import pallas as pl
from jax.experimental.pallas import tpu as pltpu
from jax.sharding import Mesh
from jax.sharding import PartitionSpec as P

NOCC = 8
AXES = ("z", "yl", "yh", "x", "c")
SIZES = (8, 4, 2, 4, 2)
BA = ("z", "yl")
DEV = ("yh", "x", "c")
GROUP = ("yl", "yh", "x", "c")
level_shift = 0.3
DSTEP = 4
LSTEP = 8


def lookup(indices, table):
    choices_range = jnp.arange(table.shape[0], dtype=jnp.int32)
    return jnp.sum(
        jnp.where(indices[:, None] == choices_range[None, :], table[None, :], 0.0), axis=1
    )


def product_kernel(where_ref, own_ref, other_ref, r0_ref, rp_ref, rm_ref, rt_ref, out_ref, bmat):
    x, c = where_ref[0], where_ref[1]

    @pl.when(pl.program_id(0) == 0)
    def _():
        for ref, shift in ((r0_ref, 0), (rp_ref, 3), (rm_ref, 1), (rt_ref, 2)):
            source = (x + shift) & 3
            for yh in range(2):
                for yl in range(4):
                    for cc in range(2):
                        for r in range(2):
                            d = pl.multiple_of((yh * 4 + source) * 64 + cc * 32, 32)
                            b = yl * 2 + r
                            bmat[pl.ds(d, 32), b * 128 : (b + 1) * 128] = ref[
                                (yh * 4 + yl) * 2 + cc, r * 32 : r * 32 + 32, :
                            ]

    for amps_ref, cc in ((own_ref, c), (other_ref, 1 - c)):
        amps = amps_ref[...].reshape(DSTEP * 64, 512)
        lanes = pl.ds(pl.multiple_of(cc * 128, 128), 128)
        for bb in range(4):
            prod = jnp.dot(
                amps, bmat[:, bb * 256 : (bb + 1) * 256], preferred_element_type=jnp.float32
            ).astype(jnp.bfloat16)
            for dd in range(DSTEP):
                for r in range(2):
                    b = bb * 2 + r
                    out_ref[dd, b * 64 : (b + 1) * 64, lanes] = prod[
                        dd * 64 : (dd + 1) * 64, r * 128 : (r + 1) * 128
                    ]


def products(where, own, other, rights):
    block = pl.BlockSpec((DSTEP, 64, 512), lambda i, w: (i, 0, 0))
    whole = pl.BlockSpec((16, 64, 128), lambda i, w: (0, 0, 0))
    return pl.pallas_call(
        product_kernel,
        grid_spec=pltpu.PrefetchScalarGridSpec(
            num_scalar_prefetch=1,
            grid=(32 // DSTEP,),
            in_specs=[block, block, whole, whole, whole, whole],
            out_specs=pl.BlockSpec((DSTEP, 512, 256), lambda i, w: (i, 0, 0)),
            scratch_shapes=[pltpu.VMEM((512, 1024), jnp.bfloat16)],
        ),
        out_shape=jax.ShapeDtypeStruct((32, 512, 256), jnp.bfloat16),
        compiler_params=pltpu.CompilerParams(
            dimension_semantics=("arbitrary",), vmem_limit_bytes=56 * 1024 * 1024
        ),
        cost_estimate=pl.CostEstimate(
            flops=2 * 4096 * 512 * 1024, bytes_accessed=14 * 1024 * 1024, transcendentals=0
        ),
    )(where, own, other, *rights)


def ladder_kernel(prod_ref, left_ref, out_ref, acc):
    step = pl.program_id(0)

    @pl.when(step == 0)
    def _():
        acc[...] = jnp.zeros_like(acc)

    total = acc[...]
    for dd in range(LSTEP):
        total += lax.dot_general(
            prod_ref[dd], left_ref[dd], (((1,), (1,)), ((), ())), preferred_element_type=jnp.float32
        )
    acc[...] = total

    @pl.when(step == pl.num_programs(0) - 1)
    def _():
        for yl in range(4):
            w = acc[yl * 128 : (yl + 1) * 128, :].T
            for ac in range(16):
                out_ref[yl * 16 + ac, 0:4, :] = w[ac * 4 : ac * 4 + 4, :]
            c1, i2 = yl // 2, yl % 2
            for big in range(8):
                for yl1 in range(4):
                    out_ref[(yl1 * 8 + big) * 2 + c1, 4 + 2 * i2 : 6 + 2 * i2, :] = w[
                        8 * big + 2 * yl1 : 8 * big + 2 * yl1 + 2, :
                    ]


def ladder_parts(prods, left):
    return pl.pallas_call(
        ladder_kernel,
        grid=(32 // LSTEP,),
        in_specs=[
            pl.BlockSpec((LSTEP, 512, 256), lambda i: (i, 0, 0)),
            pl.BlockSpec((LSTEP, 64, 256), lambda i: (i, 0, 0)),
        ],
        out_specs=pl.BlockSpec((64, 8, 128), lambda i: (0, 0, 0)),
        out_shape=jax.ShapeDtypeStruct((64, 8, 128), jnp.float32),
        scratch_shapes=[pltpu.VMEM((512, 64), jnp.float32)],
        compiler_params=pltpu.CompilerParams(
            dimension_semantics=("arbitrary",), vmem_limit_bytes=56 * 1024 * 1024
        ),
        cost_estimate=pl.CostEstimate(
            flops=2 * 64 * 64 * 8 * 8192, bytes_accessed=9 * 1024 * 1024, transcendentals=0
        ),
    )(prods, left)


def swap_pairs():
    pairs = []
    for z in range(8):
        for yl in range(4):
            for big in range(8):
                for c in range(2):
                    pairs.append((((z * 4 + yl) * 8 + big) * 2 + c, ((big * 4 + yl) * 8 + z) * 2 + c))
    return pairs


def per_device(factors, amplitudes, pair_order, occ_bin, vir_bin, levels):
    eighths = factors.reshape(64, 8, 128).transpose(1, 0, 2)
    eighths = jnp.broadcast_to(eighths[None], (2, 8, 64, 128)).reshape(16, 64, 128)
    rows = lax.all_to_all(eighths, ("yh", "yl", "c"), 0, 0, tiled=True)
    amps = amplitudes.transpose(1, 0, 2)
    amps_other = lax.ppermute(amps, "c", [(0, 1), (1, 0)])
    own = lax.dynamic_slice_in_dim(rows, lax.axis_index("yh") * 8, 8)
    own = jnp.broadcast_to(own.reshape(1, 512, 128), (8, 512, 128))
    left = lax.all_to_all(own, "z", 0, 0, tiled=True)
    left = left.reshape(8, 4, 2, 2, 32, 128).transpose(4, 0, 1, 3, 2, 5).reshape(32, 64, 256)
    rights = [rows] + [
        lax.ppermute(rows, "x", [(i, (i + s) % 4) for i in range(4)]) for s in (1, 3, 2)
    ]
    where = jnp.stack([lax.axis_index("x"), lax.axis_index("c")]).astype(jnp.int32)
    prods = products(where, amps, amps_other, rights)
    parts = ladder_parts(prods, left)
    parts = lax.all_to_all(parts, GROUP, 0, 0, tiled=True)
    summed = parts.sum(axis=0)
    direct = summed[:4].reshape(4, 2, 64)
    flipped = lax.ppermute(summed[4:], AXES, swap_pairs())
    flipped = flipped.reshape(2, 2, 2, 64).transpose(0, 2, 1, 3).reshape(4, 2, 64)

    swapped = pair_order % NOCC * NOCC + pair_order // NOCC
    matches = swapped[:, None] == pair_order[None, :]
    partnered = jnp.sum(
        jnp.where(matches[None, None], flipped[:, :, None, :], 0.0), axis=-1
    )
    total = (direct + partnered).transpose(1, 0, 2)

    virtual_energy = lookup(vir_bin, levels)
    occupied_energy = -lookup(occ_bin, levels)
    pair_energy = lookup(pair_order // NOCC, occupied_energy) + lookup(
        pair_order % NOCC, occupied_energy
    )
    left_energy = lax.dynamic_slice_in_dim(virtual_energy, lax.axis_index(DEV) * 4, 4)
    right_energy = lax.dynamic_slice_in_dim(virtual_energy, lax.axis_index(BA) * 2, 2)
    denominator = (
        right_energy[:, None, None]
        + left_energy[None, :, None]
        - pair_energy[None, None, :]
        + level_shift
    )
    return (total / denominator).reshape(2, 256)


def solution(mesh):
    finer = Mesh(mesh.devices.reshape(SIZES), AXES)
    return jax.shard_map(
        per_device,
        mesh=finer,
        in_specs=(P(BA, DEV, None), P(None, DEV, None), P(), P(), P(), P()),
        out_specs=P(BA, DEV),
        check_vma=False,
    )
```

time: 133 us -> 108 us (0.81)
  blocking collectives: 31.1 us -> 0 us
  starting transfers between devices: 26.4 us -> 50.6 us
  between operations: 13.5 us -> 0.15 us
  waiting for transfers between devices: 41.6 us -> 28.8 us
  Pallas kernels: 9.07 us -> 17.5 us
  local copies, waits for them, and re-layouts: 10.3 us -> 8.4 us
    all_to_all x2 -> x0, blocking collectives: 31.1 us -> none  [the longest x1 15.7 us: per_device(): right = lax.all_to_all(everyone, 'x', 0, 0, tiled=True)]
    all_to_all x1, waiting for transfers between devices: 22.4 us -> 0.01 us  [per_device(): left = lax.all_to_all(own, 'z', 0, 0, tiled=True)]
    ppermute x0 -> x4, starting transfers between devices: none -> 12.7 us  [the longest x3 10.8 us: per_device(): lax.ppermute(rows, 'x', [(i, (i + s) % 4) for i in range(4)])]
    all_to_all x0 -> x1, starting transfers between devices: none -> 8.68 us  [per_device(): rows = lax.all_to_all(eighths, ('yh', 'yl', 'c'), 0, 0, tiled=True)]
    pallas_call x1 -> x2, Pallas kernels: 9.07 us -> 17.5 us  [the longest x1 11.2 us: products(): pl.pallas_call(product_kernel, grid_spec=pltpu.PrefetchScalarGridSpec(num...]
    all_to_all x0 -> x1, waiting for transfers between devices: none -> 8.04 us  [per_device(): rows = lax.all_to_all(eighths, ('yh', 'yl', 'c'), 0, 0, tiled=True)]
    ppermute x0 -> x4, waiting for transfers between devices: none -> 6.9 us  [the longest x3 6.9 us: per_device(): lax.ppermute(rows, 'x', [(i, (i + s) % 4) for i in range(4)])]
    ppermute x1, starting transfers between devices: 5.23 us -> 10.3 us  [per_device(): flipped = lax.ppermute(summed[4:], AXES, swap_pairs())]
  transfers between devices with their start and end apart: 4 -> 8, of which waited for: 3 -> 6; matrix products, arithmetic and copies ran while one was open for 5% -> 3% of each run, Pallas kernels for 0% -> 10%
where the time goes in v2:
time: 108 us; the launch traced here: 107 us
  starting transfers between devices  50.6 us (47%)
  waiting for transfers between devices  28.8 us (27%)
  Pallas kernels  17.5 us (16%)
  local copies, waits for them, and re-layouts  8.4 us (8%)
  other arithmetic  1.57 us (1%)
    pallas_call x1, Pallas kernels, products(): pl.pallas_call(product_kernel, grid_spec=pltpu.PrefetchScalarGridSpec(num...  11.2 us
    ppermute x3, starting transfers between devices, per_device(): lax.ppermute(rows, 'x', [(i, (i + s) % 4) for i in range(4)])  10.8 us
    ppermute x1, starting transfers between devices, per_device(): flipped = lax.ppermute(summed[4:], AXES, swap_pairs())  10.3 us
    all_to_all x1, waiting for transfers between devices, per_device(): parts = lax.all_to_all(parts, GROUP, 0, 0, tiled=True)  10.2 us
    all_to_all x1, starting transfers between devices, per_device(): parts = lax.all_to_all(parts, GROUP, 0, 0, tiled=True)  10.1 us
    all_to_all x1, starting transfers between devices, per_device(): left = lax.all_to_all(own, 'z', 0, 0, tiled=True)  8.88 us
    all_to_all x1, starting transfers between devices, per_device(): rows = lax.all_to_all(eighths, ('yh', 'yl', 'c'), 0, 0, tiled=True)  8.68 us
    all_to_all x1, waiting for transfers between devices, per_device(): rows = lax.all_to_all(eighths, ('yh', 'yl', 'c'), 0, 0, tiled=True)  8.04 us
  transfers between devices with their start and end apart: 8, of which 6 were waited for; matrix products, arithmetic and copies ran while one was open for 3% of the time, Pallas kernels for 10%

profile of v2, /device:TPU:56, one launch (start us, length us, event | category | flops | bytes accessed | tf_op | source)
XLA Modules:
  0.0 107.1 jit_solution(666844107399667238)
XLA Ops:
  0.0 0.0 copy-start.2
  0.0 2.8 %copy.24 = bf16[64,32,512]{2,0,1:T(8,128)(2,1)S(1)} copy(bf16[64,32,512]{2,1,0:T(8,128)(2,1)} %param.7) | data formatting | bytes 4194304 | tf_op args[1]
  2.8 0.0 copy-start
  2.8 1.9 %collective-permute-start = (bf16[32,64,512]{2,1,0:T(8,128)(2,1)S(1)}, bf16[32,64,512]{2,1,0:T(8,128)(2,1)}, u32[]{:S(2)}, u32[]{:S(2)}) collective-permute-start(bf16[32,64,512]{2,1,0:T(8,128)(2,1)S(1)} %bitcast.20), channel_id=1, source_target_pairs={{0,1},{1,0},{2,3},{3,2},{4,5},{5,4},{6,7},{7,6},{8,9},{9,8},{10,11... | collective-permute-start | bytes 6291464 | tf_op jit(solution)/shard_map/ppermute | solution.py:146
  4.7 0.0 copy-done.2
  4.8 0.7 broadcast_in_dim.93
  5.5 0.0 copy-start.4
  5.5 0.0 copy-start.5
  5.5 0.0 copy-start.3
  5.5 8.7 %all-to-all-start = ((bf16[16,64,128]{2,1,0:T(8,128)(2,1)}), bf16[16,64,128]{2,1,0:T(8,128)(2,1)S(1)}, u32[]{:S(2)}, u32[]{:S(2)}) async-start(bf16[16,64,128]{2,1,0:T(8,128)(2,1)} %bitcast.4), calls=%async_computation | async-start | bytes 524288 | tf_op jit(solution)/shard_map/all_to_all | solution.py:144
  14.2 8.0 %all-to-all-done.r0_ref = bf16[16,64,128]{2,1,0:T(8,128)(2,1)S(1)} async-done(((bf16[16,64,128]{2,1,0:T(8,128)(2,1)}), bf16[16,64,128]{2,1,0:T(8,128)(2,1)S(1)}, u32[]{:S(2)}, u32[]{:S(2)}) %all-to-all-start) | async-done | bytes 262176 | tf_op jit(solution)/shard_map/all_to_all | solution.py:144
  22.3 0.0 copy-start.1
  22.3 1.2 %broadcast_in_dim.95 = bf16[8,512,128]{2,1,0:T(8,128)(2,1)} broadcast(bf16[512,128]{1,0:T(8,128)(2,1)S(1)} %bitcast.22), dimensions={1,2} | broadcast | bytes 1179648 | tf_op jit(solution)/shard_map/broadcast_in_dim | solution.py:148
  23.5 0.0 copy-done
  23.5 8.9 %all-to-all-start.1 = ((bf16[8,512,128]{2,1,0:T(8,128)(2,1)}), bf16[8,512,128]{2,1,0:T(8,128)(2,1)S(1)}, u32[]{:S(2)}, u32[]{:S(2)}) async-start(bf16[8,512,128]{2,1,0:T(8,128)(2,1)} %broadcast_in_dim.95), calls=%async_computation.1 | async-start | bytes 2097152 | tf_op jit(solution)/shard_map/all_to_all | solution.py:149
  32.3 0.0 copy-done.4
  32.3 0.0 copy-done.5
  32.4 0.2 select_reduce_fusion.4
  32.5 3.4 %collective-permute-start.1 = (bf16[16,64,128]{2,1,0:T(8,128)(2,1)S(1)}, bf16[16,64,128]{2,1,0:T(8,128)(2,1)}, u32[]{:S(2)}, u32[]{:S(2)}) collective-permute-start(bf16[16,64,128]{2,1,0:T(8,128)(2,1)S(1)} %all-to-all-done.r0_ref), channel_id=1, source_target_pairs={{0,2},{2,4},{4,6},{6,0},{1,3},{3,5},{5,7},{7,1},{8,10},{10,12},{12... | collective-permute-start | bytes 786440 | tf_op jit(solution)/shard_map/ppermute | solution.py:152
  35.9 3.7 %collective-permute-start.2 = (bf16[16,64,128]{2,1,0:T(8,128)(2,1)S(1)}, bf16[16,64,128]{2,1,0:T(8,128)(2,1)}, u32[]{:S(2)}, u32[]{:S(2)}) collective-permute-start(bf16[16,64,128]{2,1,0:T(8,128)(2,1)S(1)} %all-to-all-done.r0_ref), channel_id=1, source_target_pairs={{0,6},{2,0},{4,2},{6,4},{1,7},{3,1},{5,3},{7,5},{8,14},{10,8},{12,... | collective-permute-start | bytes 786440 | tf_op jit(solution)/shard_map/ppermute | solution.py:152
  39.6 3.7 %collective-permute-start.3 = (bf16[16,64,128]{2,1,0:T(8,128)(2,1)S(1)}, bf16[16,64,128]{2,1,0:T(8,128)(2,1)}, u32[]{:S(2)}, u32[]{:S(2)}) collective-permute-start(bf16[16,64,128]{2,1,0:T(8,128)(2,1)S(1)} %all-to-all-done.r0_ref), channel_id=1, source_target_pairs={{0,4},{2,6},{4,0},{6,2},{1,5},{3,7},{5,1},{7,3},{8,12},{10,14},{12... | collective-permute-start | bytes 786440 | tf_op jit(solution)/shard_map/ppermute | solution.py:152
  43.3 0.7 pad_add_fusion.where_ref
  44.0 0.0 copy-done.3
  44.0 0.1 collective-permute-done.1.rp_ref
  44.1 6.7 %collective-permute-done.2.rm_ref = bf16[16,64,128]{2,1,0:T(8,128)(2,1)} collective-permute-done((bf16[16,64,128]{2,1,0:T(8,128)(2,1)S(1)}, bf16[16,64,128]{2,1,0:T(8,128)(2,1)}, u32[]{:S(2)}, u32[]{:S(2)}) %collective-permute-start.2) | collective-permute-done | bytes 262176 | tf_op jit(solution)/shard_map/ppermute | solution.py:152
  50.8 0.1 collective-permute-done.3.rt_ref
  50.9 0.0 collective-permute-done.other_ref
  50.9 0.0 copy-done.1
  50.9 11.2 %shard_map.64.prod_ref = bf16[32,512,256]{2,1,0:T(8,128)(2,1)} custom-call(s32[2]{0:T(128)} %pad_add_fusion.where_ref, bf16[32,64,512]{2,1,0:T(8,128)(2,1)} %bitcast.21, bf16[32,64,512]{2,1,0:T(8,128)(2,1)} %collective-permute-done.other_ref, bf16[16,64,128]{2,1,0:T(8,128)(2,1)} %copy-done.1, bf16[16,64,128]{2,1,0:T(8,128)(2,1)} %collective-permute-done.1.rp_ref, ...), custom_call_target="tpu_custom_call" | custom-call | flops 4294967296 | bytes 14680064 | tf_op jit(solution)/shard_map/pallas_call | solution.py:64
  62.1 0.0 all-to-all-done.1
  62.1 1.1 %copy.19 = bf16[32,8,4,2,2,128]{5,4,3,2,1,0:T(2,128)(2,1)S(1)} copy(bf16[32,8,4,2,2,128]{5,0,3,4,2,1:T(8,128)(2,1)S(1)} %bitcast.19) | data formatting | bytes 2097152 | tf_op jit(solution)/shard_map/transpose | solution.py:150
  63.2 1.5 %reshape.100.left_ref = bf16[32,64,256]{2,1,0:T(8,128)(2,1)} reshape(bf16[32,8,4,2,2,128]{5,4,3,2,1,0:T(2,128)(2,1)S(1)} %copy.19) | data formatting | bytes 2097152 | tf_op jit(solution)/shard_map/reshape | solution.py:150
  64.7 0.0 copy-start.6
  64.7 6.3 %shard_map.65 = f32[64,8,128]{2,1,0:T(8,128)} custom-call(bf16[32,512,256]{2,1,0:T(8,128)(2,1)} %shard_map.64.prod_ref, bf16[32,64,256]{2,1,0:T(8,128)(2,1)} %reshape.100.left_ref), custom_call_target="tpu_custom_call" | custom-call | flops 536870912 | bytes 9437184 | tf_op jit(solution)/shard_map/pallas_call | solution.py:112
  71.0 10.1 %all-to-all-start.2 = ((f32[64,8,128]{2,1,0:T(8,128)}), f32[64,8,128]{2,1,0:T(8,128)S(1)}, u32[]{:S(2)}, u32[]{:S(2)}) async-start(f32[64,8,128]{2,1,0:T(8,128)} %shard_map.65), calls=%async_computation.2 | async-start | bytes 524288 | tf_op jit(solution)/shard_map/all_to_all | solution.py:157
  81.1 0.0 copy-done.6
  81.1 0.2 select_reduce_fusion.1
  81.3 0.1 dynamic_slice.11
  81.3 0.1 dynamic_slice.10
  81.4 0.1 broadcast_add_fusion
  81.5 0.1 broadcast_compare_fusion
  81.6 10.2 %all-to-all-done.2 = f32[64,8,128]{2,1,0:T(8,128)S(1)} async-done(((f32[64,8,128]{2,1,0:T(8,128)}), f32[64,8,128]{2,1,0:T(8,128)S(1)}, u32[]{:S(2)}, u32[]{:S(2)}) %all-to-all-start.2) | async-done | bytes 262176 | tf_op jit(solution)/shard_map/all_to_all | solution.py:157
  91.8 0.1 reduce_sum.54
  91.9 10.3 %collective-permute-start.4 = (f32[4,128]{1,0:T(4,128)S(1)}, f32[4,128]{1,0:T(4,128)S(1)}, u32[]{:S(2)}, u32[]{:S(2)}) collective-permute-start(f32[4,128]{1,0:T(4,128)S(1)} %get-tuple-element.10), channel_id=1, source_target_pairs={{0,0},{1,1},{2,64},{3,65},{4,128},{5,129},{6,192},{7,193},{8,256},... | collective-permute-start | bytes 6152 | tf_op jit(solution)/shard_map/ppermute | solution.py:160
  102.2 0.1 select_reduce_fusion.2
  102.3 0.1 reshape.101
  102.4 3.7 %collective-permute-done.4 = f32[4,128]{1,0:T(4,128)S(1)} collective-permute-done((f32[4,128]{1,0:T(4,128)S(1)}, f32[4,128]{1,0:T(4,128)S(1)}, u32[]{:S(2)}, u32[]{:S(2)}) %collective-permute-start.4) | collective-permute-done | bytes 2080 | tf_op jit(solution)/shard_map/ppermute | solution.py:160
  106.1 0.1 reshape.102
  106.2 0.2 select_reduce_fusion
  106.3 0.1 bitcast_divide_fusion
  106.4 0.7 reshape.103
  (9 shorter events, 0.1 us)
Async XLA Ops:
  0.0 4.7 %copy-start.2 = (bf16[2,32,1024]{2,1,0:T(8,128)(2,1)S(1)}, bf16[2,32,1024]{2,1,0:T(8,128)(2,1)}, u32[]{:S(2)}) copy-start(bf16[2,32,1024]{2,1,0:T(8,128)(2,1)} %param.6) | copy-start | bytes 393220
  2.8 20.7 %copy-start = (bf16[64,32,512]{2,0,1:T(8,128)(2,1)}, bf16[64,32,512]{2,0,1:T(8,128)(2,1)S(1)}, u32[]{:S(2)}) copy-start(bf16[64,32,512]{2,0,1:T(8,128)(2,1)S(1)} %copy.24) | copy-start | bytes 6291460
  2.8 48.1 %collective-permute-start = (bf16[32,64,512]{2,1,0:T(8,128)(2,1)S(1)}, bf16[32,64,512]{2,1,0:T(8,128)(2,1)}, u32[]{:S(2)}, u32[]{:S(2)}) collective-permute-start(bf16[32,64,512]{2,1,0:T(8,128)(2,1)S(1)} %bitcast.20), channel_id=1, source_target_pairs={{0,1},{1,0},{2,3},{3,2},{4,5},{5,4},{6,7},{7,6},{8,9},{9,8},{10,11... | collective-permute-start | bytes 6291464 | tf_op jit(solution)/shard_map/ppermute | solution.py:146
  5.5 26.8 %copy-start.4 = (s32[8]{0:T(128)S(1)}, s32[8]{0:T(128)}, u32[]{:S(2)}) copy-start(s32[8]{0:T(128)} %param.9) | copy-start | bytes 100
  5.5 26.8 %copy-start.5 = (f32[128]{0:T(128)S(1)}, f32[128]{0:T(128)}, u32[]{:S(2)}) copy-start(f32[128]{0:T(128)} %param.11) | copy-start | bytes 1540
  5.5 38.5 %copy-start.3 = (s32[64]{0:T(128)S(1)}, s32[64]{0:T(128)}, u32[]{:S(2)}) copy-start(s32[64]{0:T(128)} %param.8) | copy-start | bytes 772
  5.5 16.7 %all-to-all-start = ((bf16[16,64,128]{2,1,0:T(8,128)(2,1)}), bf16[16,64,128]{2,1,0:T(8,128)(2,1)S(1)}, u32[]{:S(2)}, u32[]{:S(2)}) async-start(bf16[16,64,128]{2,1,0:T(8,128)(2,1)} %bitcast.4), calls=%async_computation | async-start | bytes 524288 | tf_op jit(solution)/shard_map/all_to_all | solution.py:144
  22.3 28.7 %copy-start.1 = (bf16[16,64,128]{2,1,0:T(8,128)(2,1)}, bf16[16,64,128]{2,1,0:T(8,128)(2,1)S(1)}, u32[]{:S(2)}) copy-start(bf16[16,64,128]{2,1,0:T(8,128)(2,1)S(1)} %all-to-all-done.r0_ref) | copy-start | bytes 786436
  23.5 38.6 %all-to-all-start.1 = ((bf16[8,512,128]{2,1,0:T(8,128)(2,1)}), bf16[8,512,128]{2,1,0:T(8,128)(2,1)S(1)}, u32[]{:S(2)}, u32[]{:S(2)}) async-start(bf16[8,512,128]{2,1,0:T(8,128)(2,1)} %broadcast_in_dim.95), calls=%async_computation.1 | async-start | bytes 2097152 | tf_op jit(solution)/shard_map/all_to_all | solution.py:149
  32.5 11.6 %collective-permute-start.1 = (bf16[16,64,128]{2,1,0:T(8,128)(2,1)S(1)}, bf16[16,64,128]{2,1,0:T(8,128)(2,1)}, u32[]{:S(2)}, u32[]{:S(2)}) collective-permute-start(bf16[16,64,128]{2,1,0:T(8,128)(2,1)S(1)} %all-to-all-done.r0_ref), channel_id=1, source_target_pairs={{0,2},{2,4},{4,6},{6,0},{1,3},{3,5},{5,7},{7,1},{8,10},{10,12},{12... | collective-permute-start | bytes 786440 | tf_op jit(solution)/shard_map/ppermute | solution.py:152
  35.9 14.9 %collective-permute-start.2 = (bf16[16,64,128]{2,1,0:T(8,128)(2,1)S(1)}, bf16[16,64,128]{2,1,0:T(8,128)(2,1)}, u32[]{:S(2)}, u32[]{:S(2)}) collective-permute-start(bf16[16,64,128]{2,1,0:T(8,128)(2,1)S(1)} %all-to-all-done.r0_ref), channel_id=1, source_target_pairs={{0,6},{2,0},{4,2},{6,4},{1,7},{3,1},{5,3},{7,5},{8,14},{10,8},{12,... | collective-permute-start | bytes 786440 | tf_op jit(solution)/shard_map/ppermute | solution.py:152
  39.6 11.3 %collective-permute-start.3 = (bf16[16,64,128]{2,1,0:T(8,128)(2,1)S(1)}, bf16[16,64,128]{2,1,0:T(8,128)(2,1)}, u32[]{:S(2)}, u32[]{:S(2)}) collective-permute-start(bf16[16,64,128]{2,1,0:T(8,128)(2,1)S(1)} %all-to-all-done.r0_ref), channel_id=1, source_target_pairs={{0,4},{2,6},{4,0},{6,2},{1,5},{3,7},{5,1},{7,3},{8,12},{10,14},{12... | collective-permute-start | bytes 786440 | tf_op jit(solution)/shard_map/ppermute | solution.py:152
  64.7 16.3 %copy-start.6 = (s32[64]{0:T(128)S(1)}, s32[64]{0:T(128)}, u32[]{:S(2)}) copy-start(s32[64]{0:T(128)} %param.10) | copy-start | bytes 772
  71.0 20.8 %all-to-all-start.2 = ((f32[64,8,128]{2,1,0:T(8,128)}), f32[64,8,128]{2,1,0:T(8,128)S(1)}, u32[]{:S(2)}, u32[]{:S(2)}) async-start(f32[64,8,128]{2,1,0:T(8,128)} %shard_map.65), calls=%async_computation.2 | async-start | bytes 524288 | tf_op jit(solution)/shard_map/all_to_all | solution.py:157
  91.9 14.2 %collective-permute-start.4 = (f32[4,128]{1,0:T(4,128)S(1)}, f32[4,128]{1,0:T(4,128)S(1)}, u32[]{:S(2)}, u32[]{:S(2)}) collective-permute-start(f32[4,128]{1,0:T(4,128)S(1)} %get-tuple-element.10), channel_id=1, source_target_pairs={{0,0},{1,1},{2,64},{3,65},{4,128},{5,129},{6,192},{7,193},{8,256},... | collective-permute-start | bytes 6152 | tf_op jit(solution)/shard_map/ppermute | solution.py:160

commit v3 on v2

v3 whole, which is shorter than its diff:
```python
import functools

import jax
import jax.numpy as jnp
from jax import lax
from jax.experimental import pallas as pl
from jax.experimental.pallas import tpu as pltpu
from jax.sharding import Mesh
from jax.sharding import PartitionSpec as P

NOCC = 8
AXES = ("z", "yl", "yh", "x", "c")
SIZES = (8, 4, 2, 4, 2)
BA = ("z", "yl")
DEV = ("yh", "x", "c")
GROUP = ("yl", "yh", "x", "c")
level_shift = 0.3
DSTEP = 8


def lookup(indices, table):
    choices_range = jnp.arange(table.shape[0], dtype=jnp.int32)
    return jnp.sum(
        jnp.where(indices[:, None] == choices_range[None, :], table[None, :], 0.0), axis=1
    )


def ladder_kernel(
    where_ref, own_ref, other_ref, r0_ref, rp_ref, rm_ref, rt_ref, left_ref, out_ref, bmat, xs, wide, lefts, acc
):
    x, c = where_ref[0], where_ref[1]
    step = pl.program_id(0)

    @pl.when(step == 0)
    def _():
        acc[...] = jnp.zeros_like(acc)
        wide[...] = left_ref[...].astype(jnp.float32)
        for ref, shift in ((r0_ref, 0), (rp_ref, 3), (rm_ref, 1), (rt_ref, 2)):
            source = (x + shift) & 3
            for yh in range(2):
                for yl in range(4):
                    for cc in range(2):
                        for r in range(2):
                            d = pl.multiple_of((yh * 4 + source) * 64 + cc * 32, 32)
                            b = yl * 2 + r
                            bmat[pl.ds(d, 32), b * 128 : (b + 1) * 128] = ref[
                                (yh * 4 + yl) * 2 + cc, r * 32 : r * 32 + 32, :
                            ]

    for dd in range(DSTEP):
        for cc in range(2):
            for r in range(2):
                start = cc * 64 + r * 32 + step * DSTEP + dd
                lefts[dd, r * 32 : (r + 1) * 32, cc * 128 : (cc + 1) * 128] = wide[
                    pl.ds(start, 32, stride=128), :
                ].astype(jnp.bfloat16)

    for amps_ref, cc in ((own_ref, c), (other_ref, 1 - c)):
        amps = amps_ref[...].reshape(DSTEP * 64, 512)
        lanes = pl.ds(pl.multiple_of(cc * 128, 128), 128)
        for bb in range(4):
            prod = jnp.dot(
                amps, bmat[:, bb * 256 : (bb + 1) * 256], preferred_element_type=jnp.float32
            ).astype(jnp.bfloat16)
            for dd in range(DSTEP):
                for r in range(2):
                    b = bb * 2 + r
                    xs[dd, b * 64 : (b + 1) * 64, lanes] = prod[
                        dd * 64 : (dd + 1) * 64, r * 128 : (r + 1) * 128
                    ]
    total = acc[...]
    for dd in range(DSTEP):
        total += lax.dot_general(
            xs[dd], lefts[dd], (((1,), (1,)), ((), ())), preferred_element_type=jnp.float32
        )
    acc[...] = total

    @pl.when(step == pl.num_programs(0) - 1)
    def _():
        for yl in range(4):
            w = acc[yl * 128 : (yl + 1) * 128, :].T
            for r in range(2):
                for z in range(8):
                    out_ref[pl.ds(z * 32 + yl * 8 + r, 4, stride=2), :] = w[
                        r * 32 + z * 4 : r * 32 + z * 4 + 4, :
                    ]


def ladder_parts(where, own, other, rights, left):
    block = pl.BlockSpec((DSTEP, 64, 512), lambda i, w: (i, 0, 0))
    whole = pl.BlockSpec((16, 64, 128), lambda i, w: (0, 0, 0))
    return pl.pallas_call(
        ladder_kernel,
        grid_spec=pltpu.PrefetchScalarGridSpec(
            num_scalar_prefetch=1,
            grid=(32 // DSTEP,),
            in_specs=[block, block, whole, whole, whole, whole]
            + [pl.BlockSpec((4096, 128), lambda i, w: (0, 0))],
            out_specs=pl.BlockSpec((256, 128), lambda i, w: (0, 0)),
            scratch_shapes=[
                pltpu.VMEM((512, 1024), jnp.bfloat16),
                pltpu.VMEM((DSTEP, 512, 256), jnp.bfloat16),
                pltpu.VMEM((4096, 128), jnp.float32),
                pltpu.VMEM((DSTEP, 64, 256), jnp.bfloat16),
                pltpu.VMEM((512, 64), jnp.float32),
            ],
        ),
        out_shape=jax.ShapeDtypeStruct((256, 128), jnp.float32),
        compiler_params=pltpu.CompilerParams(
            dimension_semantics=("arbitrary",), vmem_limit_bytes=58 * 1024 * 1024
        ),
        cost_estimate=pl.CostEstimate(
            flops=2 * 4096 * 512 * 1024 + 2 * 64 * 64 * 8 * 8192,
            bytes_accessed=6 * 1024 * 1024,
            transcendentals=0,
        ),
    )(where, own, other, *rights, left)


def both_kernel(own_ref, crossed_ref, pairing_ref, out_ref, turned):
    for yl in range(4):
        rows = [crossed_ref[pl.ds(yl * 2 + r, 32, stride=8), :] for r in range(2)]
        for r in range(2):
            half = slice(r * 64, (r + 1) * 64)
            turned[pl.ds(r, 32, stride=2), :] = jnp.concatenate(
                [rows[0][:, half], rows[1][:, half]], axis=1
            )
        partnered = jnp.dot(
            turned[...],
            pairing_ref[...],
            precision=lax.Precision.HIGHEST,
            preferred_element_type=jnp.float32,
        )
        for z in range(8):
            total = own_ref[z * 32 + yl * 8 : z * 32 + yl * 8 + 8, :] + partnered[z * 8 : z * 8 + 8]
            out_ref[(yl * 8 + z) * 2] = total[:4]
            out_ref[(yl * 8 + z) * 2 + 1] = total[4:]


def both_orders(own, crossed, pairing):
    return pl.pallas_call(
        both_kernel,
        out_shape=jax.ShapeDtypeStruct((64, 4, 128), jnp.float32),
        scratch_shapes=[pltpu.VMEM((64, 128), jnp.float32)],
    )(own, crossed, pairing)


def finish_kernel(parts_ref, shift_ref, out_ref):
    update = jnp.sum(parts_ref[...], axis=0) / shift_ref[...]
    for r in range(2):
        for i in range(4):
            out_ref[r : r + 1, i * 64 : (i + 1) * 64] = update[i : i + 1, r * 64 : (r + 1) * 64]


def finished(parts, shift):
    return pl.pallas_call(
        finish_kernel, out_shape=jax.ShapeDtypeStruct((2, 256), jnp.float32)
    )(parts, shift)


def per_device(factors, amplitudes, pair_order, occ_bin, vir_bin, levels):
    swapped = pair_order % NOCC * NOCC + pair_order // NOCC
    matches = (pair_order[:, None] == swapped[None, :]).astype(jnp.float32)
    pairing = jnp.kron(jnp.eye(2, dtype=jnp.float32), matches)
    virtual_energy = lookup(vir_bin, levels)
    occupied_energy = -lookup(occ_bin, levels)
    pair_energy = lookup(pair_order // NOCC, occupied_energy) + lookup(
        pair_order % NOCC, occupied_energy
    )
    left_energy = lax.dynamic_slice_in_dim(virtual_energy, lax.axis_index(DEV) * 4, 4)
    right_energy = lax.dynamic_slice_in_dim(virtual_energy, lax.axis_index(BA) * 2, 2)
    denominator = (
        right_energy[None, :, None]
        + left_energy[:, None, None]
        - pair_energy[None, None, :]
        + level_shift
    ).reshape(4, 128)

    eighths = factors.reshape(64, 8, 128).transpose(1, 0, 2)
    eighths = jnp.broadcast_to(eighths[None], (2, 8, 64, 128)).reshape(16, 64, 128)
    rows = lax.all_to_all(eighths, ("yh", "yl", "c"), 0, 0, tiled=True)
    amps = amplitudes.transpose(1, 0, 2)
    rows, sent = lax.optimization_barrier((rows, amps))
    amps_other = lax.ppermute(sent, "c", [(0, 1), (1, 0)])
    own = lax.dynamic_slice_in_dim(rows, lax.axis_index("yh") * 8, 8)
    own = jnp.broadcast_to(own.reshape(1, 512, 128), (8, 512, 128))
    left = lax.all_to_all(own, "z", 0, 0, tiled=True).reshape(4096, 128)
    rights = [rows] + [
        lax.ppermute(rows, "x", [(i, (i + s) % 4) for i in range(4)]) for s in (1, 3, 2)
    ]
    where = jnp.stack([lax.axis_index("x"), lax.axis_index("c")]).astype(jnp.int32)
    ladder = ladder_parts(where, amps, amps_other, rights, left)
    crossed = lax.all_to_all(ladder.reshape(8, 32, 128), "z", 0, 0, tiled=True)
    parts = both_orders(ladder, crossed.reshape(256, 128), pairing)
    parts = lax.all_to_all(parts, GROUP, 0, 0, tiled=True)
    return finished(parts, denominator)


def solution(mesh):
    finer = Mesh(mesh.devices.reshape(SIZES), AXES)
    return jax.shard_map(
        per_device,
        mesh=finer,
        in_specs=(P(BA, DEV, None), P(None, DEV, None), P(), P(), P(), P()),
        out_specs=P(BA, DEV),
        check_vma=False,
    )
```

time: 108 us -> 117 us (1.083)
  the two profiles are of different devices: /device:TPU:56 before, /device:TPU:1 now
where the time goes in v3:
time: 117 us; the launch traced here: 116 us
  starting transfers between devices  41.5 us (35%)
  waiting for transfers between devices  41.3 us (35%)
  Pallas kernels  19.8 us (17%)
  local copies, waits for them, and re-layouts  10.9 us (9%)
  other arithmetic  2.46 us (2%)
    pallas_call x1, Pallas kernels, ladder_parts(): pl.pallas_call(ladder_kernel, grid_spec=pltpu.PrefetchScalarGridSpec(num_...  16.1 us
    all_to_all x1, waiting for transfers between devices, per_device(): left = lax.all_to_all(own, 'z', 0, 0, tiled=True).reshape(4096, 128)  12 us
    all_to_all x1, starting transfers between devices, per_device(): rows = lax.all_to_all(eighths, ('yh', 'yl', 'c'), 0, 0, tiled=True)  10.2 us
    ppermute x3, starting transfers between devices, per_device(): lax.ppermute(rows, 'x', [(i, (i + s) % 4) for i in range(4)])  9.93 us
    all_to_all x1, waiting for transfers between devices, per_device(): parts = lax.all_to_all(parts, GROUP, 0, 0, tiled=True)  9.52 us
    all_to_all x1, waiting for transfers between devices, per_device(): rows = lax.all_to_all(eighths, ('yh', 'yl', 'c'), 0, 0, tiled=True)  9.06 us
    all_to_all x1, starting transfers between devices, per_device(): left = lax.all_to_all(own, 'z', 0, 0, tiled=True).reshape(4096, 128)  8.31 us
    all_to_all x1, starting transfers between devices, per_device(): parts = lax.all_to_all(parts, GROUP, 0, 0, tiled=True)  7.82 us
  transfers between devices with their start and end apart: 8, of which 6 were waited for; matrix products, arithmetic and copies ran while one was open for 7% of the time, Pallas kernels for 0%

profile of v3, /device:TPU:1, one launch (start us, length us, event | category | flops | bytes accessed | tf_op | source)
XLA Modules:
  0.0 116.1 jit_solution(16853986840576648027)
XLA Ops:
  0.0 0.9 copy.11
  1.0 0.7 broadcast_in_dim.50
  1.7 10.2 %all-to-all-start = ((bf16[16,64,128]{2,1,0:T(8,128)(2,1)}), bf16[16,64,128]{2,1,0:T(8,128)(2,1)S(1)}, u32[]{:S(2)}, u32[]{:S(2)}) async-start(bf16[16,64,128]{2,1,0:T(8,128)(2,1)} %bitcast.4), calls=%async_computation | async-start | bytes 524288 | tf_op jit(solution)/shard_map/all_to_all | solution.py:181
  11.9 2.8 %copy.13 = bf16[64,32,512]{2,0,1:T(8,128)(2,1)S(1)} copy(bf16[64,32,512]{2,1,0:T(8,128)(2,1)} %param.7) | data formatting | bytes 4194304 | tf_op args[1]
  14.7 0.0 copy-start
  14.7 0.0 copy-start.8
  14.7 0.0 copy-start.9
  14.7 0.0 copy-start.5
  14.7 9.1 %all-to-all-done.r0_ref = bf16[16,64,128]{2,1,0:T(8,128)(2,1)S(1)} async-done(((bf16[16,64,128]{2,1,0:T(8,128)(2,1)}), bf16[16,64,128]{2,1,0:T(8,128)(2,1)S(1)}, u32[]{:S(2)}, u32[]{:S(2)}) %all-to-all-start) | async-done | bytes 262176 | tf_op jit(solution)/shard_map/all_to_all | solution.py:181
  23.8 0.0 copy-start.2
  23.8 1.9 %collective-permute-start = (bf16[32,64,512]{2,1,0:T(8,128)(2,1)S(1)}, bf16[32,64,512]{2,1,0:T(8,128)(2,1)}, u32[]{:S(2)}, u32[]{:S(2)}) collective-permute-start(bf16[32,64,512]{2,1,0:T(8,128)(2,1)S(1)} %bitcast.15), channel_id=1, source_target_pairs={{0,1},{1,0},{2,3},{3,2},{4,5},{5,4},{6,7},{7,6},{8,9},{9,8},{10,11... | collective-permute-start | bytes 6291464 | tf_op jit(solution)/shard_map/ppermute | solution.py:184
  25.7 1.1 broadcast_in_dim.76
  26.8 8.3 %all-to-all-start.1 = ((bf16[8,512,128]{2,1,0:T(8,128)(2,1)}), bf16[8,512,128]{2,1,0:T(8,128)(2,1)S(1)}, u32[]{:S(2)}, u32[]{:S(2)}) async-start(bf16[8,512,128]{2,1,0:T(8,128)(2,1)} %broadcast_in_dim.76), calls=%async_computation.1 | async-start | bytes 2097152 | tf_op jit(solution)/shard_map/all_to_all | solution.py:187
  35.1 0.0 copy-done.8
  35.1 0.0 copy-done.9
  35.1 0.7 select_reduce_fusion
  35.8 0.0 copy-done.5
  35.8 0.1 compare_convert_fusion
  35.9 3.1 %collective-permute-start.1 = (bf16[16,64,128]{2,1,0:T(8,128)(2,1)S(1)}, bf16[16,64,128]{2,1,0:T(8,128)(2,1)S(1)}, u32[]{:S(2)}, u32[]{:S(2)}) collective-permute-start(bf16[16,64,128]{2,1,0:T(8,128)(2,1)S(1)} %all-to-all-done.r0_ref), channel_id=1, source_target_pairs={{0,2},{2,4},{4,6},{6,0},{1,3},{3,5},{5,7},{7,1},{8,10},{10,12},{12... | collective-permute-start | bytes 786440 | tf_op jit(solution)/shard_map/ppermute | solution.py:189
  39.0 3.4 %collective-permute-start.2 = (bf16[16,64,128]{2,1,0:T(8,128)(2,1)S(1)}, bf16[16,64,128]{2,1,0:T(8,128)(2,1)S(1)}, u32[]{:S(2)}, u32[]{:S(2)}) collective-permute-start(bf16[16,64,128]{2,1,0:T(8,128)(2,1)S(1)} %all-to-all-done.r0_ref), channel_id=1, source_target_pairs={{0,6},{2,0},{4,2},{6,4},{1,7},{3,1},{5,3},{7,5},{8,14},{10,8},{12,... | collective-permute-start | bytes 786440 | tf_op jit(solution)/shard_map/ppermute | solution.py:189
  42.4 3.4 %collective-permute-start.3 = (bf16[16,64,128]{2,1,0:T(8,128)(2,1)S(1)}, bf16[16,64,128]{2,1,0:T(8,128)(2,1)}, u32[]{:S(2)}, u32[]{:S(2)}) collective-permute-start(bf16[16,64,128]{2,1,0:T(8,128)(2,1)S(1)} %all-to-all-done.r0_ref), channel_id=1, source_target_pairs={{0,4},{2,6},{4,0},{6,2},{1,5},{3,7},{5,1},{7,3},{8,12},{10,14},{12... | collective-permute-start | bytes 786440 | tf_op jit(solution)/shard_map/ppermute | solution.py:189
  45.9 0.7 pad_add_fusion.where_ref
  46.5 0.1 broadcast_multiply_fusion
  46.6 0.0 collective-permute-done.1.rp_ref
  46.6 0.0 copy-start.6
  46.7 1.0 collective-permute-done.2.rm_ref
  47.7 0.0 copy-done.6
  47.7 0.0 copy-start.7
  47.7 0.7 copy-done.7
  48.4 4.0 %collective-permute-done.3.rt_ref = bf16[16,64,128]{2,1,0:T(8,128)(2,1)} collective-permute-done((bf16[16,64,128]{2,1,0:T(8,128)(2,1)S(1)}, bf16[16,64,128]{2,1,0:T(8,128)(2,1)}, u32[]{:S(2)}, u32[]{:S(2)}) %collective-permute-start.3) | collective-permute-done | bytes 262176 | tf_op jit(solution)/shard_map/ppermute | solution.py:189
  52.4 12.0 %all-to-all-done.1 = bf16[8,512,128]{2,1,0:T(8,128)(2,1)S(1)} async-done(((bf16[8,512,128]{2,1,0:T(8,128)(2,1)}), bf16[8,512,128]{2,1,0:T(8,128)(2,1)S(1)}, u32[]{:S(2)}, u32[]{:S(2)}) %all-to-all-start.1) | async-done | bytes 1048608 | tf_op jit(solution)/shard_map/all_to_all | solution.py:187
  64.3 0.0 copy-start.1
  64.4 0.0 collective-permute-done.other_ref
  64.4 0.0 copy-done
  64.4 0.0 copy-done.2
  64.4 0.9 copy-done.1
  65.3 0.0 copy-start.10
  65.3 16.1 %shard_map.64.own_ref = f32[256,128]{1,0:T(8,128)} custom-call(s32[2]{0:T(128)} %pad_add_fusion.where_ref, bf16[32,64,512]{2,1,0:T(8,128)(2,1)} %bitcast.16, bf16[32,64,512]{2,1,0:T(8,128)(2,1)} %collective-permute-done.other_ref, bf16[16,64,128]{2,1,0:T(8,128)(2,1)} %copy-done.2, bf16[16,64,128]{2,1,0:T(8,128)(2,1)} %copy-done.6, ...), custom_call_target="tpu_custom_call" | custom-call | flops 4831838208 | bytes 6291456 | tf_op jit(solution)/shard_map/pallas_call | solution.py:92
  81.4 3.4 %all-to-all-start.2 = ((f32[8,32,128]{2,1,0:T(8,128)}), f32[8,32,128]{2,1,0:T(8,128)S(1)}, u32[]{:S(2)}, u32[]{:S(2)}) async-start(f32[8,32,128]{2,1,0:T(8,128)} %bitcast.18), calls=%async_computation.2 | async-start | bytes 262144 | tf_op jit(solution)/shard_map/all_to_all | solution.py:193
  84.8 0.0 copy-done.10
  84.8 0.2 select_reduce_fusion.3
  85.0 0.7 mul.49.pairing_ref
  85.8 0.7 dynamic_slice.11
  86.4 0.7 dynamic_slice.10
  87.1 0.1 broadcast_add_fusion
  87.2 5.7 %all-to-all-done.2 = f32[8,32,128]{2,1,0:T(8,128)S(1)} async-done(((f32[8,32,128]{2,1,0:T(8,128)}), f32[8,32,128]{2,1,0:T(8,128)S(1)}, u32[]{:S(2)}, u32[]{:S(2)}) %all-to-all-start.2) | async-done | bytes 131104 | tf_op jit(solution)/shard_map/all_to_all | solution.py:193
  92.9 0.0 copy-start.3
  92.9 0.6 copy-done.3
  93.5 2.0 %shard_map.65 = f32[64,4,128]{2,1,0:T(4,128)} custom-call(f32[256,128]{1,0:T(8,128)} %shard_map.64.own_ref, f32[256,128]{1,0:T(8,128)} %bitcast.19, f32[128,128]{1,0:T(8,128)} %mul.49.pairing_ref), custom_call_target="tpu_custom_call" | custom-call | tf_op jit(solution)/shard_map/pallas_call | solution.py:141
  95.5 7.8 %all-to-all-start.3 = ((f32[64,4,128]{2,1,0:T(4,128)}), f32[64,4,128]{2,1,0:T(4,128)S(1)}, u32[]{:S(2)}, u32[]{:S(2)}) async-start(f32[64,4,128]{2,1,0:T(4,128)} %shard_map.65), calls=%async_computation.3 | async-start | bytes 262144 | tf_op jit(solution)/shard_map/all_to_all | solution.py:195
  103.4 0.1 select_reduce_fusion.1
  103.5 0.1 sub.29
  103.5 0.1 sub.30
  103.6 0.1 sub.32
  103.7 0.6 subtract_add_fusion.shift_ref
  104.3 9.5 %all-to-all-done.3.parts_ref = f32[64,4,128]{2,1,0:T(4,128)S(1)} async-done(((f32[64,4,128]{2,1,0:T(4,128)}), f32[64,4,128]{2,1,0:T(4,128)S(1)}, u32[]{:S(2)}, u32[]{:S(2)}) %all-to-all-start.3) | async-done | bytes 131104 | tf_op jit(solution)/shard_map/all_to_all | solution.py:195
  113.8 0.0 copy-start.4
  113.8 0.6 copy-done.4
  114.4 1.6 %shard_map.66 = f32[2,256]{1,0:T(2,128)} custom-call(f32[64,4,128]{2,1,0:T(4,128)} %copy-done.4, f32[4,128]{1,0:T(4,128)} %subtract_add_fusion.shift_ref), custom_call_target="tpu_custom_call" | custom-call | tf_op jit(solution)/shard_map/pallas_call | solution.py:156
  (7 shorter events, 0.1 us)
Async XLA Ops:
  1.7 22.1 %all-to-all-start = ((bf16[16,64,128]{2,1,0:T(8,128)(2,1)}), bf16[16,64,128]{2,1,0:T(8,128)(2,1)S(1)}, u32[]{:S(2)}, u32[]{:S(2)}) async-start(bf16[16,64,128]{2,1,0:T(8,128)(2,1)} %bitcast.4), calls=%async_computation | async-start | bytes 524288 | tf_op jit(solution)/shard_map/all_to_all | solution.py:181
  14.7 49.7 %copy-start = (bf16[64,32,512]{2,0,1:T(8,128)(2,1)}, bf16[64,32,512]{2,0,1:T(8,128)(2,1)S(1)}, u32[]{:S(2)}) copy-start(bf16[64,32,512]{2,0,1:T(8,128)(2,1)S(1)} %copy.13) | copy-start | bytes 6291460
  14.7 20.5 %copy-start.8 = (s32[64]{0:T(128)S(1)}, s32[64]{0:T(128)}, u32[]{:S(2)}) copy-start(s32[64]{0:T(128)} %param.10) | copy-start | bytes 772
  14.7 20.5 %copy-start.9 = (f32[128]{0:T(128)S(1)}, f32[128]{0:T(128)}, u32[]{:S(2)}) copy-start(f32[128]{0:T(128)} %param.11) | copy-start | bytes 1540
  14.7 21.1 %copy-start.5 = (s32[64]{0:T(128)S(1)}, s32[64]{0:T(128)}, u32[]{:S(2)}) copy-start(s32[64]{0:T(128)} %param.8) | copy-start | bytes 772
  23.8 40.6 %copy-start.2 = (bf16[16,64,128]{2,1,0:T(8,128)(2,1)}, bf16[16,64,128]{2,1,0:T(8,128)(2,1)S(1)}, u32[]{:S(2)}) copy-start(bf16[16,64,128]{2,1,0:T(8,128)(2,1)S(1)} %all-to-all-done.r0_ref) | copy-start | bytes 786436
  23.8 40.6 %collective-permute-start = (bf16[32,64,512]{2,1,0:T(8,128)(2,1)S(1)}, bf16[32,64,512]{2,1,0:T(8,128)(2,1)}, u32[]{:S(2)}, u32[]{:S(2)}) collective-permute-start(bf16[32,64,512]{2,1,0:T(8,128)(2,1)S(1)} %bitcast.15), channel_id=1, source_target_pairs={{0,1},{1,0},{2,3},{3,2},{4,5},{5,4},{6,7},{7,6},{8,9},{9,8},{10,11... | collective-permute-start | bytes 6291464 | tf_op jit(solution)/shard_map/ppermute | solution.py:184
  26.8 37.5 %all-to-all-start.1 = ((bf16[8,512,128]{2,1,0:T(8,128)(2,1)}), bf16[8,512,128]{2,1,0:T(8,128)(2,1)S(1)}, u32[]{:S(2)}, u32[]{:S(2)}) async-start(bf16[8,512,128]{2,1,0:T(8,128)(2,1)} %broadcast_in_dim.76), calls=%async_computation.1 | async-start | bytes 2097152 | tf_op jit(solution)/shard_map/all_to_all | solution.py:187
  35.9 10.7 %collective-permute-start.1 = (bf16[16,64,128]{2,1,0:T(8,128)(2,1)S(1)}, bf16[16,64,128]{2,1,0:T(8,128)(2,1)S(1)}, u32[]{:S(2)}, u32[]{:S(2)}) collective-permute-start(bf16[16,64,128]{2,1,0:T(8,128)(2,1)S(1)} %all-to-all-done.r0_ref), channel_id=1, source_target_pairs={{0,2},{2,4},{4,6},{6,0},{1,3},{3,5},{5,7},{7,1},{8,10},{10,12},{12... | collective-permute-start | bytes 786440 | tf_op jit(solution)/shard_map/ppermute | solution.py:189
  39.0 8.6 %collective-permute-start.2 = (bf16[16,64,128]{2,1,0:T(8,128)(2,1)S(1)}, bf16[16,64,128]{2,1,0:T(8,128)(2,1)S(1)}, u32[]{:S(2)}, u32[]{:S(2)}) collective-permute-start(bf16[16,64,128]{2,1,0:T(8,128)(2,1)S(1)} %all-to-all-done.r0_ref), channel_id=1, source_target_pairs={{0,6},{2,0},{4,2},{6,4},{1,7},{3,1},{5,3},{7,5},{8,14},{10,8},{12,... | collective-permute-start | bytes 786440 | tf_op jit(solution)/shard_map/ppermute | solution.py:189
  42.4 10.0 %collective-permute-start.3 = (bf16[16,64,128]{2,1,0:T(8,128)(2,1)S(1)}, bf16[16,64,128]{2,1,0:T(8,128)(2,1)}, u32[]{:S(2)}, u32[]{:S(2)}) collective-permute-start(bf16[16,64,128]{2,1,0:T(8,128)(2,1)S(1)} %all-to-all-done.r0_ref), channel_id=1, source_target_pairs={{0,4},{2,6},{4,0},{6,2},{1,5},{3,7},{5,1},{7,3},{8,12},{10,14},{12... | collective-permute-start | bytes 786440 | tf_op jit(solution)/shard_map/ppermute | solution.py:189
  46.6 1.0 copy-start.6
  47.7 0.7 copy-start.7
  64.3 1.0 copy-start.1
  65.3 19.5 %copy-start.10 = (s32[8]{0:T(128)S(1)}, s32[8]{0:T(128)}, u32[]{:S(2)}) copy-start(s32[8]{0:T(128)} %param.9) | copy-start | bytes 100
  81.4 11.4 %all-to-all-start.2 = ((f32[8,32,128]{2,1,0:T(8,128)}), f32[8,32,128]{2,1,0:T(8,128)S(1)}, u32[]{:S(2)}, u32[]{:S(2)}) async-start(f32[8,32,128]{2,1,0:T(8,128)} %bitcast.18), calls=%async_computation.2 | async-start | bytes 262144 | tf_op jit(solution)/shard_map/all_to_all | solution.py:193
  92.9 0.6 copy-start.3
  95.5 18.3 %all-to-all-start.3 = ((f32[64,4,128]{2,1,0:T(4,128)}), f32[64,4,128]{2,1,0:T(4,128)S(1)}, u32[]{:S(2)}, u32[]{:S(2)}) async-start(f32[64,4,128]{2,1,0:T(4,128)} %shard_map.65), calls=%async_computation.3 | async-start | bytes 262144 | tf_op jit(solution)/shard_map/all_to_all | solution.py:195
  113.8 0.7 copy-start.4

commit v4 on v3

--- a/solution.py
+++ b/solution.py
@@ -16,6 +16,8 @@
 GROUP = ("yl", "yh", "x", "c")
 level_shift = 0.3
 DSTEP = 8
+VMEM_A = 24
+VMEM_B = 54
 
 
 def lookup(indices, table):
@@ -25,16 +27,11 @@
     )
 
 
-def ladder_kernel(
-    where_ref, own_ref, other_ref, r0_ref, rp_ref, rm_ref, rt_ref, left_ref, out_ref, bmat, xs, wide, lefts, acc
-):
+def product_kernel(where_ref, own_ref, other_ref, r0_ref, rp_ref, rm_ref, rt_ref, out_ref, bmat):
     x, c = where_ref[0], where_ref[1]
-    step = pl.program_id(0)
-
-    @pl.when(step == 0)
+
+    @pl.when(pl.program_id(0) == 0)
     def _():
-        acc[...] = jnp.zeros_like(acc)
-        wide[...] = left_ref[...].astype(jnp.float32)
         for ref, shift in ((r0_ref, 0), (rp_ref, 3), (rm_ref, 1), (rt_ref, 2)):
             source = (x + shift) & 3
             for yh in range(2):
@@ -47,74 +44,95 @@
                                 (yh * 4 + yl) * 2 + cc, r * 32 : r * 32 + 32, :
                             ]
 
-    for dd in range(DSTEP):
-        for cc in range(2):
-            for r in range(2):
-                start = cc * 64 + r * 32 + step * DSTEP + dd
-                lefts[dd, r * 32 : (r + 1) * 32, cc * 128 : (cc + 1) * 128] = wide[
-                    pl.ds(start, 32, stride=128), :
-                ].astype(jnp.bfloat16)
-
     for amps_ref, cc in ((own_ref, c), (other_ref, 1 - c)):
         amps = amps_ref[...].reshape(DSTEP * 64, 512)
-        lanes = pl.ds(pl.multiple_of(cc * 128, 128), 128)
         for bb in range(4):
             prod = jnp.dot(
                 amps, bmat[:, bb * 256 : (bb + 1) * 256], preferred_element_type=jnp.float32
             ).astype(jnp.bfloat16)
             for dd in range(DSTEP):
+                lanes = pl.ds(pl.multiple_of(dd * 256 + cc * 128, 128), 128)
                 for r in range(2):
                     b = bb * 2 + r
-                    xs[dd, b * 64 : (b + 1) * 64, lanes] = prod[
+                    out_ref[0, b * 64 : (b + 1) * 64, lanes] = prod[
                         dd * 64 : (dd + 1) * 64, r * 128 : (r + 1) * 128
                     ]
-    total = acc[...]
+
+
+def products(where, own, other, rights):
+    block = pl.BlockSpec((DSTEP, 64, 512), lambda i, w: (i, 0, 0))
+    whole = pl.BlockSpec((16, 64, 128), lambda i, w: (0, 0, 0))
+    return pl.pallas_call(
+        product_kernel,
+        grid_spec=pltpu.PrefetchScalarGridSpec(
+            num_scalar_prefetch=1,
+            grid=(32 // DSTEP,),
+            in_specs=[block, block, whole, whole, whole, whole],
+            out_specs=pl.BlockSpec((1, 512, DSTEP * 256), lambda i, w: (i, 0, 0)),
+            scratch_shapes=[pltpu.VMEM((512, 1024), jnp.bfloat16)],
+        ),
+        out_shape=pltpu.HBM((32 // DSTEP, 512, DSTEP * 256), jnp.bfloat16),
+        compiler_params=pltpu.CompilerParams(
+            dimension_semantics=("arbitrary",), vmem_limit_bytes=VMEM_A * 1024 * 1024
+        ),
+        cost_estimate=pl.CostEstimate(
+            flops=2 * 4096 * 512 * 1024, bytes_accessed=14 * 1024 * 1024, transcendentals=0
+        ),
+    )(where, own, other, *rights)
+
+
+def ladder_kernel(prod_ref, left_ref, out_ref, wide, lefts, acc):
+    step = pl.program_id(0)
+
+    @pl.when(step == 0)
+    def _():
+        acc[...] = jnp.zeros_like(acc)
+        wide[...] = left_ref[...].astype(jnp.float32)
+
     for dd in range(DSTEP):
-        total += lax.dot_general(
-            xs[dd], lefts[dd], (((1,), (1,)), ((), ())), preferred_element_type=jnp.float32
-        )
-    acc[...] = total
+        for cc in range(2):
+            lane = dd * 256 + cc * 128
+            for r in range(2):
+                start = cc * 64 + r * 32 + step * DSTEP + dd
+                lefts[r * 32 : (r + 1) * 32, lane : lane + 128] = wide[
+                    pl.ds(start, 32, stride=128), :
+                ].astype(jnp.bfloat16)
+    acc[...] += lax.dot_general(
+        lefts[...], prod_ref[0], (((1,), (1,)), ((), ())), preferred_element_type=jnp.float32
+    )
 
     @pl.when(step == pl.num_programs(0) - 1)
     def _():
         for yl in range(4):
-            w = acc[yl * 128 : (yl + 1) * 128, :].T
             for r in range(2):
                 for z in range(8):
-                    out_ref[pl.ds(z * 32 + yl * 8 + r, 4, stride=2), :] = w[
-                        r * 32 + z * 4 : r * 32 + z * 4 + 4, :
+                    out_ref[pl.ds(z * 32 + yl * 8 + r, 4, stride=2), :] = acc[
+                        r * 32 + z * 4 : r * 32 + z * 4 + 4, yl * 128 : (yl + 1) * 128
                     ]
 
 
-def ladder_parts(where, own, other, rights, left):
-    block = pl.BlockSpec((DSTEP, 64, 512), lambda i, w: (i, 0, 0))
-    whole = pl.BlockSpec((16, 64, 128), lambda i, w: (0, 0, 0))
+def ladder_parts(prods, left):
     return pl.pallas_call(
         ladder_kernel,
-        grid_spec=pltpu.PrefetchScalarGridSpec(
-            num_scalar_prefetch=1,
-            grid=(32 // DSTEP,),
-            in_specs=[block, block, whole, whole, whole, whole]
-            + [pl.BlockSpec((4096, 128), lambda i, w: (0, 0))],
-            out_specs=pl.BlockSpec((256, 128), lambda i, w: (0, 0)),
-            scratch_shapes=[
-                pltpu.VMEM((512, 1024), jnp.bfloat16),
-                pltpu.VMEM((DSTEP, 512, 256), jnp.bfloat16),
-                pltpu.VMEM((4096, 128), jnp.float32),
-                pltpu.VMEM((DSTEP, 64, 256), jnp.bfloat16),
-                pltpu.VMEM((512, 64), jnp.float32),
-            ],
-        ),
+        grid=(32 // DSTEP,),
+        in_specs=[
+            pl.BlockSpec((1, 512, DSTEP * 256), lambda i: (i, 0, 0)),
+            pl.BlockSpec((4096, 128), lambda i: (0, 0)),
+        ],
+        out_specs=pl.BlockSpec((256, 128), lambda i: (0, 0)),
         out_shape=jax.ShapeDtypeStruct((256, 128), jnp.float32),
+        scratch_shapes=[
+            pltpu.VMEM((4096, 128), jnp.float32),
+            pltpu.VMEM((64, DSTEP * 256), jnp.bfloat16),
+            pltpu.VMEM((64, 512), jnp.float32),
+        ],
         compiler_params=pltpu.CompilerParams(
-            dimension_semantics=("arbitrary",), vmem_limit_bytes=58 * 1024 * 1024
+            dimension_semantics=("arbitrary",), vmem_limit_bytes=VMEM_B * 1024 * 1024
         ),
         cost_estimate=pl.CostEstimate(
-            flops=2 * 4096 * 512 * 1024 + 2 * 64 * 64 * 8 * 8192,
-            bytes_accessed=6 * 1024 * 1024,
-            transcendentals=0,
-        ),
-    )(where, own, other, *rights, left)
+            flops=2 * 64 * 64 * 8 * 8192, bytes_accessed=9 * 1024 * 1024, transcendentals=0
+        ),
+    )(prods, left)
 
 
 def both_kernel(own_ref, crossed_ref, pairing_ref, out_ref, turned):
@@ -142,6 +160,7 @@
         both_kernel,
         out_shape=jax.ShapeDtypeStruct((64, 4, 128), jnp.float32),
         scratch_shapes=[pltpu.VMEM((64, 128), jnp.float32)],
+        compiler_params=pltpu.CompilerParams(vmem_limit_bytes=8 * 1024 * 1024),
     )(own, crossed, pairing)
 
 
@@ -154,7 +173,9 @@
 
 def finished(parts, shift):
     return pl.pallas_call(
-        finish_kernel, out_shape=jax.ShapeDtypeStruct((2, 256), jnp.float32)
+        finish_kernel,
+        out_shape=jax.ShapeDtypeStruct((2, 256), jnp.float32),
+        compiler_params=pltpu.CompilerParams(vmem_limit_bytes=8 * 1024 * 1024),
     )(parts, shift)
 
 
@@ -189,7 +210,7 @@
         lax.ppermute(rows, "x", [(i, (i + s) % 4) for i in range(4)]) for s in (1, 3, 2)
     ]
     where = jnp.stack([lax.axis_index("x"), lax.axis_index("c")]).astype(jnp.int32)
-    ladder = ladder_parts(where, amps, amps_other, rights, left)
+    ladder = ladder_parts(products(where, amps, amps_other, rights), left)
     crossed = lax.all_to_all(ladder.reshape(8, 32, 128), "z", 0, 0, tiled=True)
     parts = both_orders(ladder, crossed.reshape(256, 128), pairing)
     parts = lax.all_to_all(parts, GROUP, 0, 0, tiled=True)

time: 117 us -> 108 us (0.923)
  waiting for transfers between devices: 41.3 us -> 36.2 us
  local copies, waits for them, and re-layouts: 10.9 us -> 8.08 us
  starting transfers between devices: 41.5 us -> 43.7 us
  Pallas kernels: 19.8 us -> 18 us
  other arithmetic: 2.46 us -> 0.79 us
    all_to_all x1, waiting for transfers between devices: 12 us -> 3.48 us  [per_device(): left = lax.all_to_all(own, 'z', 0, 0, tiled=True).reshape(4096, 128)]
    all_to_all x1, starting transfers between devices: 7.82 us -> 10 us  [per_device(): parts = lax.all_to_all(parts, GROUP, 0, 0, tiled=True)]
    all_to_all x1, waiting for transfers between devices: 5.72 us -> 7.38 us  [per_device(): crossed = lax.all_to_all(ladder.reshape(8, 32, 128), 'z', 0, 0, tiled=True)]
    ppermute x3, waiting for transfers between devices: 5 us -> 6.22 us  [per_device(): lax.ppermute(rows, 'x', [(i, (i + s) % 4) for i in range(4)])]
    unnamed x24 -> x14, local copies, waits for them, and re-layouts: 6.67 us -> 5.66 us
    pallas_call x1 -> x2, Pallas kernels: 16.1 us -> 16.2 us  [the longest x1 9.09 us: products(): pl.pallas_call(product_kernel, grid_spec=pltpu.PrefetchScalarGridSpec(num...]
  transfers between devices with their start and end apart: 8 -> 8, of which waited for: 6 -> 6; matrix products, arithmetic and copies ran while one was open for 7% -> 5% of each run, Pallas kernels for 0% -> 8%
where the time goes in v4:
time: 108 us; the launch traced here: 107 us
  starting transfers between devices  43.7 us (40%)
  waiting for transfers between devices  36.2 us (34%)
  Pallas kernels  18 us (17%)
  local copies, waits for them, and re-layouts  8.08 us (7%)
    all_to_all x1, starting transfers between devices, per_device(): rows = lax.all_to_all(eighths, ('yh', 'yl', 'c'), 0, 0, tiled=True)  10.2 us
    all_to_all x1, waiting for transfers between devices, per_device(): parts = lax.all_to_all(parts, GROUP, 0, 0, tiled=True)  10.1 us
    all_to_all x1, starting transfers between devices, per_device(): parts = lax.all_to_all(parts, GROUP, 0, 0, tiled=True)  10 us
    ppermute x3, starting transfers between devices, per_device(): lax.ppermute(rows, 'x', [(i, (i + s) % 4) for i in range(4)])  9.93 us
    pallas_call x1, Pallas kernels, products(): pl.pallas_call(product_kernel, grid_spec=pltpu.PrefetchScalarGridSpec(num...  9.09 us
    all_to_all x1, waiting for transfers between devices, per_device(): rows = lax.all_to_all(eighths, ('yh', 'yl', 'c'), 0, 0, tiled=True)  9.07 us
    all_to_all x1, starting transfers between devices, per_device(): left = lax.all_to_all(own, 'z', 0, 0, tiled=True).reshape(4096, 128)  8.31 us
    all_to_all x1, waiting for transfers between devices, per_device(): crossed = lax.all_to_all(ladder.reshape(8, 32, 128), 'z', 0, 0, tiled=True)  7.38 us
  transfers between devices with their start and end apart: 8, of which 6 were waited for; matrix products, arithmetic and copies ran while one was open for 5% of the time, Pallas kernels for 8%

profile of v4, /device:TPU:1, one launch (start us, length us, event | category | flops | bytes accessed | tf_op | source)
XLA Modules:
  0.0 107.0 jit_solution(14784650859434070783)
XLA Ops:
  0.0 0.9 copy.11
  1.0 0.7 broadcast_in_dim.50
  1.7 10.2 %all-to-all-start = ((bf16[16,64,128]{2,1,0:T(8,128)(2,1)}), bf16[16,64,128]{2,1,0:T(8,128)(2,1)S(1)}, u32[]{:S(2)}, u32[]{:S(2)}) async-start(bf16[16,64,128]{2,1,0:T(8,128)(2,1)} %bitcast.4), calls=%async_computation | async-start | bytes 524288 | tf_op jit(solution)/shard_map/all_to_all | solution.py:202
  11.9 2.8 %copy.13 = bf16[64,32,512]{2,0,1:T(8,128)(2,1)S(1)} copy(bf16[64,32,512]{2,1,0:T(8,128)(2,1)} %param.7) | data formatting | bytes 4194304 | tf_op args[1]
  14.7 0.0 copy-start.3
  14.7 0.0 copy-start.4
  14.7 0.0 copy-start.2
  14.7 9.1 %all-to-all-done.r0_ref = bf16[16,64,128]{2,1,0:T(8,128)(2,1)S(1)} async-done(((bf16[16,64,128]{2,1,0:T(8,128)(2,1)}), bf16[16,64,128]{2,1,0:T(8,128)(2,1)S(1)}, u32[]{:S(2)}, u32[]{:S(2)}) %all-to-all-start) | async-done | bytes 262176 | tf_op jit(solution)/shard_map/all_to_all | solution.py:202
  23.8 1.9 %collective-permute-start = (bf16[32,64,512]{2,1,0:T(8,128)(2,1)S(1)}, bf16[32,64,512]{2,1,0:T(8,128)(2,1)}, u32[]{:S(2)}, u32[]{:S(2)}) collective-permute-start(bf16[32,64,512]{2,1,0:T(8,128)(2,1)S(1)} %bitcast.15), channel_id=1, source_target_pairs={{0,1},{1,0},{2,3},{3,2},{4,5},{5,4},{6,7},{7,6},{8,9},{9,8},{10,11... | collective-permute-start | bytes 6291464 | tf_op jit(solution)/shard_map/ppermute | solution.py:205
  25.7 1.1 %broadcast_in_dim.76 = bf16[8,512,128]{2,1,0:T(8,128)(2,1)} broadcast(bf16[512,128]{1,0:T(8,128)(2,1)S(1)} %bitcast.20), dimensions={1,2} | broadcast | bytes 1179648 | tf_op jit(solution)/shard_map/broadcast_in_dim | solution.py:207
  26.8 8.3 %all-to-all-start.1 = ((bf16[8,512,128]{2,1,0:T(8,128)(2,1)}), bf16[8,512,128]{2,1,0:T(8,128)(2,1)S(1)}, u32[]{:S(2)}, u32[]{:S(2)}) async-start(bf16[8,512,128]{2,1,0:T(8,128)(2,1)} %broadcast_in_dim.76), calls=%async_computation.1 | async-start | bytes 2097152 | tf_op jit(solution)/shard_map/all_to_all | solution.py:208
  35.1 0.0 copy-done.3
  35.1 0.0 copy-done.4
  35.2 0.2 select_reduce_fusion
  35.3 0.0 copy-done.2
  35.4 0.1 compare_convert_fusion
  35.4 3.1 %collective-permute-start.1 = (bf16[16,64,128]{2,1,0:T(8,128)(2,1)S(1)}, bf16[16,64,128]{2,1,0:T(8,128)(2,1)S(1)}, u32[]{:S(2)}, u32[]{:S(2)}) collective-permute-start(bf16[16,64,128]{2,1,0:T(8,128)(2,1)S(1)} %all-to-all-done.r0_ref), channel_id=1, source_target_pairs={{0,2},{2,4},{4,6},{6,0},{1,3},{3,5},{5,7},{7,1},{8,10},{10,12},{12... | collective-permute-start | bytes 786440 | tf_op jit(solution)/shard_map/ppermute | solution.py:210
  38.6 3.4 %collective-permute-start.2 = (bf16[16,64,128]{2,1,0:T(8,128)(2,1)S(1)}, bf16[16,64,128]{2,1,0:T(8,128)(2,1)S(1)}, u32[]{:S(2)}, u32[]{:S(2)}) collective-permute-start(bf16[16,64,128]{2,1,0:T(8,128)(2,1)S(1)} %all-to-all-done.r0_ref), channel_id=1, source_target_pairs={{0,6},{2,0},{4,2},{6,4},{1,7},{3,1},{5,3},{7,5},{8,14},{10,8},{12,... | collective-permute-start | bytes 786440 | tf_op jit(solution)/shard_map/ppermute | solution.py:210
  41.9 3.4 %collective-permute-start.3 = (bf16[16,64,128]{2,1,0:T(8,128)(2,1)S(1)}, bf16[16,64,128]{2,1,0:T(8,128)(2,1)S(1)}, u32[]{:S(2)}, u32[]{:S(2)}) collective-permute-start(bf16[16,64,128]{2,1,0:T(8,128)(2,1)S(1)} %all-to-all-done.r0_ref), channel_id=1, source_target_pairs={{0,4},{2,6},{4,0},{6,2},{1,5},{3,7},{5,1},{7,3},{8,12},{10,14},{12... | collective-permute-start | bytes 786440 | tf_op jit(solution)/shard_map/ppermute | solution.py:210
  45.4 0.1 pad_add_fusion.where_ref
  45.5 0.1 broadcast_multiply_fusion
  45.6 0.0 collective-permute-done.1.rp_ref
  45.6 1.6 %collective-permute-done.2.rm_ref = bf16[16,64,128]{2,1,0:T(8,128)(2,1)S(1)} collective-permute-done((bf16[16,64,128]{2,1,0:T(8,128)(2,1)S(1)}, bf16[16,64,128]{2,1,0:T(8,128)(2,1)S(1)}, u32[]{:S(2)}, u32[]{:S(2)}) %collective-permute-start.2) | collective-permute-done | bytes 262176 | tf_op jit(solution)/shard_map/ppermute | solution.py:210
  47.2 4.6 %collective-permute-done.3.rt_ref = bf16[16,64,128]{2,1,0:T(8,128)(2,1)S(1)} collective-permute-done((bf16[16,64,128]{2,1,0:T(8,128)(2,1)S(1)}, bf16[16,64,128]{2,1,0:T(8,128)(2,1)S(1)}, u32[]{:S(2)}, u32[]{:S(2)}) %collective-permute-start.3) | collective-permute-done | bytes 262176 | tf_op jit(solution)/shard_map/ppermute | solution.py:210
  51.8 0.0 collective-permute-done.other_ref
  51.8 9.1 %shard_map.64.prod_ref = bf16[4,512,2048]{2,1,0:T(8,128)(2,1)} custom-call(s32[2]{0:T(128)S(1)} %pad_add_fusion.where_ref, bf16[32,64,512]{2,1,0:T(8,128)(2,1)S(1)} %bitcast.16, bf16[32,64,512]{2,1,0:T(8,128)(2,1)} %collective-permute-done.other_ref, bf16[16,64,128]{2,1,0:T(8,128)(2,1)S(1)} %all-to-all-done.r0_ref, ...), custom_call_target="tpu_custom_call" | custom-call | flops 4294967296 | bytes 14680064 | tf_op jit(solution)/shard_map/pallas_call | solution.py:65
  60.9 3.5 %all-to-all-done.1 = bf16[8,512,128]{2,1,0:T(8,128)(2,1)S(1)} async-done(((bf16[8,512,128]{2,1,0:T(8,128)(2,1)}), bf16[8,512,128]{2,1,0:T(8,128)(2,1)S(1)}, u32[]{:S(2)}, u32[]{:S(2)}) %all-to-all-start.1) | async-done | bytes 1048608 | tf_op jit(solution)/shard_map/all_to_all | solution.py:208
  64.4 0.0 copy-start.1
  64.4 1.1 copy-done.1
  65.4 0.0 copy-start.5
  65.4 7.1 %shard_map.65.own_ref = f32[256,128]{1,0:T(8,128)} custom-call(bf16[4,512,2048]{2,1,0:T(8,128)(2,1)} %shard_map.64.prod_ref, bf16[4096,128]{1,0:T(8,128)(2,1)} %bitcast.19), custom_call_target="tpu_custom_call" | custom-call | flops 536870912 | bytes 9437184 | tf_op jit(solution)/shard_map/pallas_call | solution.py:115
  72.5 3.4 %all-to-all-start.2 = ((f32[8,32,128]{2,1,0:T(8,128)}), f32[8,32,128]{2,1,0:T(8,128)S(1)}, u32[]{:S(2)}, u32[]{:S(2)}) async-start(f32[8,32,128]{2,1,0:T(8,128)} %bitcast.17), calls=%async_computation.2 | async-start | bytes 262144 | tf_op jit(solution)/shard_map/all_to_all | solution.py:214
  75.9 0.0 copy-done.5
  75.9 0.2 select_reduce_fusion.3
  76.1 0.1 mul.49.pairing_ref
  76.2 0.1 dynamic_slice.11
  76.3 0.1 dynamic_slice.10
  76.4 0.1 broadcast_add_fusion
  76.5 7.4 %all-to-all-done.2 = f32[8,32,128]{2,1,0:T(8,128)S(1)} async-done(((f32[8,32,128]{2,1,0:T(8,128)}), f32[8,32,128]{2,1,0:T(8,128)S(1)}, u32[]{:S(2)}, u32[]{:S(2)}) %all-to-all-start.2) | async-done | bytes 131104 | tf_op jit(solution)/shard_map/all_to_all | solution.py:214
  83.8 0.0 copy-start
  83.8 0.9 copy-done
  84.7 1.1 shard_map.66
  85.8 10.0 %all-to-all-start.3 = ((f32[64,4,128]{2,1,0:T(4,128)}), f32[64,4,128]{2,1,0:T(4,128)S(1)}, u32[]{:S(2)}, u32[]{:S(2)}) async-start(f32[64,4,128]{2,1,0:T(4,128)} %shard_map.66), calls=%async_computation.3 | async-start | bytes 262144 | tf_op jit(solution)/shard_map/all_to_all | solution.py:216
  95.8 0.1 select_reduce_fusion.1
  95.9 0.1 sub.29
  96.0 0.1 sub.30
  96.1 0.1 sub.32
  96.2 10.1 %all-to-all-done.3.parts_ref = f32[64,4,128]{2,1,0:T(4,128)S(1)} async-done(((f32[64,4,128]{2,1,0:T(4,128)}), f32[64,4,128]{2,1,0:T(4,128)S(1)}, u32[]{:S(2)}, u32[]{:S(2)}) %all-to-all-start.3) | async-done | bytes 131104 | tf_op jit(solution)/shard_map/all_to_all | solution.py:216
  106.2 0.7 shard_map.67
  (8 shorter events, 0.1 us)
Async XLA Ops:
  1.7 22.1 %all-to-all-start = ((bf16[16,64,128]{2,1,0:T(8,128)(2,1)}), bf16[16,64,128]{2,1,0:T(8,128)(2,1)S(1)}, u32[]{:S(2)}, u32[]{:S(2)}) async-start(bf16[16,64,128]{2,1,0:T(8,128)(2,1)} %bitcast.4), calls=%async_computation | async-start | bytes 524288 | tf_op jit(solution)/shard_map/all_to_all | solution.py:202
  14.7 20.5 %copy-start.3 = (s32[64]{0:T(128)S(1)}, s32[64]{0:T(128)}, u32[]{:S(2)}) copy-start(s32[64]{0:T(128)} %param.10) | copy-start | bytes 772
  14.7 20.5 %copy-start.4 = (f32[128]{0:T(128)S(1)}, f32[128]{0:T(128)}, u32[]{:S(2)}) copy-start(f32[128]{0:T(128)} %param.11) | copy-start | bytes 1540
  14.7 20.7 %copy-start.2 = (s32[64]{0:T(128)S(1)}, s32[64]{0:T(128)}, u32[]{:S(2)}) copy-start(s32[64]{0:T(128)} %param.8) | copy-start | bytes 772
  23.8 28.0 %collective-permute-start = (bf16[32,64,512]{2,1,0:T(8,128)(2,1)S(1)}, bf16[32,64,512]{2,1,0:T(8,128)(2,1)}, u32[]{:S(2)}, u32[]{:S(2)}) collective-permute-start(bf16[32,64,512]{2,1,0:T(8,128)(2,1)S(1)} %bitcast.15), channel_id=1, source_target_pairs={{0,1},{1,0},{2,3},{3,2},{4,5},{5,4},{6,7},{7,6},{8,9},{9,8},{10,11... | collective-permute-start | bytes 6291464 | tf_op jit(solution)/shard_map/ppermute | solution.py:205
  26.8 37.5 %all-to-all-start.1 = ((bf16[8,512,128]{2,1,0:T(8,128)(2,1)}), bf16[8,512,128]{2,1,0:T(8,128)(2,1)S(1)}, u32[]{:S(2)}, u32[]{:S(2)}) async-start(bf16[8,512,128]{2,1,0:T(8,128)(2,1)} %broadcast_in_dim.76), calls=%async_computation.1 | async-start | bytes 2097152 | tf_op jit(solution)/shard_map/all_to_all | solution.py:208
  35.4 10.2 %collective-permute-start.1 = (bf16[16,64,128]{2,1,0:T(8,128)(2,1)S(1)}, bf16[16,64,128]{2,1,0:T(8,128)(2,1)S(1)}, u32[]{:S(2)}, u32[]{:S(2)}) collective-permute-start(bf16[16,64,128]{2,1,0:T(8,128)(2,1)S(1)} %all-to-all-done.r0_ref), channel_id=1, source_target_pairs={{0,2},{2,4},{4,6},{6,0},{1,3},{3,5},{5,7},{7,1},{8,10},{10,12},{12... | collective-permute-start | bytes 786440 | tf_op jit(solution)/shard_map/ppermute | solution.py:210
  38.6 8.6 %collective-permute-start.2 = (bf16[16,64,128]{2,1,0:T(8,128)(2,1)S(1)}, bf16[16,64,128]{2,1,0:T(8,128)(2,1)S(1)}, u32[]{:S(2)}, u32[]{:S(2)}) collective-permute-start(bf16[16,64,128]{2,1,0:T(8,128)(2,1)S(1)} %all-to-all-done.r0_ref), channel_id=1, source_target_pairs={{0,6},{2,0},{4,2},{6,4},{1,7},{3,1},{5,3},{7,5},{8,14},{10,8},{12,... | collective-permute-start | bytes 786440 | tf_op jit(solution)/shard_map/ppermute | solution.py:210
  41.9 9.9 %collective-permute-start.3 = (bf16[16,64,128]{2,1,0:T(8,128)(2,1)S(1)}, bf16[16,64,128]{2,1,0:T(8,128)(2,1)S(1)}, u32[]{:S(2)}, u32[]{:S(2)}) collective-permute-start(bf16[16,64,128]{2,1,0:T(8,128)(2,1)S(1)} %all-to-all-done.r0_ref), channel_id=1, source_target_pairs={{0,4},{2,6},{4,0},{6,2},{1,5},{3,7},{5,1},{7,3},{8,12},{10,14},{12... | collective-permute-start | bytes 786440 | tf_op jit(solution)/shard_map/ppermute | solution.py:210
  64.4 1.1 copy-start.1
  65.4 10.5 %copy-start.5 = (s32[8]{0:T(128)S(1)}, s32[8]{0:T(128)}, u32[]{:S(2)}) copy-start(s32[8]{0:T(128)} %param.9) | copy-start | bytes 100
  72.5 11.3 %all-to-all-start.2 = ((f32[8,32,128]{2,1,0:T(8,128)}), f32[8,32,128]{2,1,0:T(8,128)S(1)}, u32[]{:S(2)}, u32[]{:S(2)}) async-start(f32[8,32,128]{2,1,0:T(8,128)} %bitcast.17), calls=%async_computation.2 | async-start | bytes 262144 | tf_op jit(solution)/shard_map/all_to_all | solution.py:214
  83.8 0.9 copy-start
  85.8 20.5 %all-to-all-start.3 = ((f32[64,4,128]{2,1,0:T(4,128)}), f32[64,4,128]{2,1,0:T(4,128)S(1)}, u32[]{:S(2)}, u32[]{:S(2)}) async-start(f32[64,4,128]{2,1,0:T(4,128)} %shard_map.66), calls=%async_computation.3 | async-start | bytes 262144 | tf_op jit(solution)/shard_map/all_to_all | solution.py:216

commit v5 on v4

v5 whole, which is shorter than its diff:
```python
import functools

import jax
import jax.numpy as jnp
from jax import lax
from jax.experimental import pallas as pl
from jax.experimental.pallas import tpu as pltpu
from jax.sharding import Mesh
from jax.sharding import PartitionSpec as P

NOCC = 8
AXES = ("z", "yl", "yh", "x", "c")
SIZES = (8, 4, 2, 4, 2)
BA = ("z", "yl")
DEV = ("yh", "x", "c")
GROUP = ("yl", "yh", "x", "c")
level_shift = 0.3
DSTEP = 8
STEPS = 4
VMEM_A = 24
VMEM_B = 49


def lookup(indices, table):
    choices_range = jnp.arange(table.shape[0], dtype=jnp.int32)
    return jnp.sum(
        jnp.where(indices[:, None] == choices_range[None, :], table[None, :], 0.0), axis=1
    )


def product_kernel(
    where_ref, own_ref, other_ref, r0_ref, rp_ref, rm_ref, rt_ref, out_ref, amps, bmat, prods, amps_sem, b_sem, out_sem
):
    x, c = where_ref[0], where_ref[1]
    rights = [
        pltpu.make_async_copy(ref, bmat.at[(x + shift) & 3], b_sem.at[n])
        for n, (ref, shift) in enumerate(((r0_ref, 0), (rp_ref, 3), (rm_ref, 1), (rt_ref, 2)))
    ]

    def load(step, half):
        ref, place = ((own_ref, c), (other_ref, 1 - c))[half]
        return pltpu.make_async_copy(ref.at[step], amps.at[place, step], amps_sem.at[half, step])

    def store(step):
        return pltpu.make_async_copy(prods.at[step], out_ref.at[step], out_sem.at[step])

    for copy in rights:
        copy.start()
    for step in range(STEPS):
        load(step, 0).start()
        load(step, 1).start()
    for copy in rights:
        copy.wait()

    def one_step(step, _):
        load(step, 0).wait()
        load(step, 1).wait()
        for yl in range(4):
            right = jnp.concatenate(
                [
                    jnp.concatenate(
                        [bmat[x, (yh * 4 + yl) * 2 + cc, r * 32 : r * 32 + 32, :] for r in range(2)],
                        axis=1,
                    )
                    for yh in range(2)
                    for x in range(4)
                    for cc in range(2)
                ],
                axis=0,
            )
            for cc in range(2):
                prod = jnp.dot(
                    amps[cc, step].reshape(DSTEP * 64, 512), right, preferred_element_type=jnp.float32
                ).astype(jnp.bfloat16)
                for dd in range(DSTEP):
                    lane = dd * 256 + cc * 128
                    for r in range(2):
                        b = yl * 2 + r
                        prods[step, b * 64 : (b + 1) * 64, lane : lane + 128] = prod[
                            dd * 64 : (dd + 1) * 64, r * 128 : (r + 1) * 128
                        ]
        store(step).start()
        return 0

    lax.fori_loop(0, STEPS, one_step, 0)
    for step in range(STEPS):
        store(step).wait()


def products(where, own, other, rights):
    anywhere = pl.BlockSpec(memory_space=pl.ANY)
    shape = (STEPS, 512, DSTEP * 256)
    return pl.pallas_call(
        product_kernel,
        in_specs=[pl.BlockSpec(memory_space=pltpu.SMEM)] + [anywhere] * 6,
        out_specs=pl.BlockSpec(memory_space=pltpu.HBM),
        out_shape=pltpu.HBM(shape, jnp.bfloat16),
        scratch_shapes=[
            pltpu.VMEM((2, STEPS, DSTEP, 64, 512), jnp.bfloat16),
            pltpu.VMEM((4, 16, 64, 128), jnp.bfloat16),
            pltpu.VMEM(shape, jnp.bfloat16),
            pltpu.SemaphoreType.DMA((2, STEPS)),
            pltpu.SemaphoreType.DMA((4,)),
            pltpu.SemaphoreType.DMA((STEPS,)),
        ],
        compiler_params=pltpu.CompilerParams(vmem_limit_bytes=VMEM_A * 1024 * 1024),
        cost_estimate=pl.CostEstimate(
            flops=2 * 4096 * 512 * 1024, bytes_accessed=14 * 1024 * 1024, transcendentals=0
        ),
    )(where, own, other, *rights)


def ladder_kernel(prod_ref, left_ref, out_ref, prods, wide, lefts, sem):
    copies = [
        pltpu.make_async_copy(prod_ref.at[step], prods.at[step], sem.at[step])
        for step in range(STEPS)
    ]
    for copy in copies:
        copy.start()
    wide[...] = left_ref[...].astype(jnp.float32)
    for step in range(STEPS):
        for dd in range(DSTEP):
            for cc in range(2):
                lane = dd * 256 + cc * 128
                for r in range(2):
                    start = cc * 64 + r * 32 + step * DSTEP + dd
                    lefts[step, r * 32 : (r + 1) * 32, lane : lane + 128] = wide[
                        pl.ds(start, 32, stride=128), :
                    ].astype(jnp.bfloat16)
    total = jnp.zeros((64, 512), jnp.float32)
    for step in range(STEPS):
        copies[step].wait()
        total += lax.dot_general(
            lefts[step], prods[step], (((1,), (1,)), ((), ())), preferred_element_type=jnp.float32
        )
    for yl in range(4):
        for r in range(2):
            for z in range(8):
                out_ref[pl.ds(z * 32 + yl * 8 + r, 4, stride=2), :] = total[
                    r * 32 + z * 4 : r * 32 + z * 4 + 4, yl * 128 : (yl + 1) * 128
                ]


def ladder_parts(prods, left):
    return pl.pallas_call(
        ladder_kernel,
        in_specs=[
            pl.BlockSpec(memory_space=pltpu.HBM),
            pl.BlockSpec(memory_space=pltpu.VMEM),
        ],
        out_specs=pl.BlockSpec(memory_space=pltpu.VMEM),
        out_shape=jax.ShapeDtypeStruct((256, 128), jnp.float32),
        scratch_shapes=[
            pltpu.VMEM((STEPS, 512, DSTEP * 256), jnp.bfloat16),
            pltpu.VMEM((4096, 128), jnp.float32),
            pltpu.VMEM((STEPS, 64, DSTEP * 256), jnp.bfloat16),
            pltpu.SemaphoreType.DMA((STEPS,)),
        ],
        compiler_params=pltpu.CompilerParams(vmem_limit_bytes=VMEM_B * 1024 * 1024),
        cost_estimate=pl.CostEstimate(
            flops=2 * 64 * 64 * 8 * 8192, bytes_accessed=9 * 1024 * 1024, transcendentals=0
        ),
    )(prods, left)


def both_kernel(own_ref, crossed_ref, pairing_ref, out_ref, turned):
    for yl in range(4):
        rows = [crossed_ref[pl.ds(yl * 2 + r, 32, stride=8), :] for r in range(2)]
        for r in range(2):
            half = slice(r * 64, (r + 1) * 64)
            turned[pl.ds(r, 32, stride=2), :] = jnp.concatenate(
                [rows[0][:, half], rows[1][:, half]], axis=1
            )
        partnered = jnp.dot(
            turned[...],
            pairing_ref[...],
            precision=lax.Precision.HIGHEST,
            preferred_element_type=jnp.float32,
        )
        for z in range(8):
            total = own_ref[z * 32 + yl * 8 : z * 32 + yl * 8 + 8, :] + partnered[z * 8 : z * 8 + 8]
            out_ref[(yl * 8 + z) * 2] = total[:4]
            out_ref[(yl * 8 + z) * 2 + 1] = total[4:]


def both_orders(own, crossed, pairing):
    return pl.pallas_call(
        both_kernel,
        out_shape=jax.ShapeDtypeStruct((64, 4, 128), jnp.float32),
        scratch_shapes=[pltpu.VMEM((64, 128), jnp.float32)],
        compiler_params=pltpu.CompilerParams(vmem_limit_bytes=8 * 1024 * 1024),
    )(own, crossed, pairing)


def finish_kernel(parts_ref, shift_ref, out_ref):
    update = jnp.sum(parts_ref[...], axis=0) / shift_ref[...]
    for r in range(2):
        for i in range(4):
            out_ref[r : r + 1, i * 64 : (i + 1) * 64] = update[i : i + 1, r * 64 : (r + 1) * 64]


def finished(parts, shift):
    return pl.pallas_call(
        finish_kernel,
        out_shape=jax.ShapeDtypeStruct((2, 256), jnp.float32),
        compiler_params=pltpu.CompilerParams(vmem_limit_bytes=8 * 1024 * 1024),
    )(parts, shift)


def per_device(factors, amplitudes, pair_order, occ_bin, vir_bin, levels):
    swapped = pair_order % NOCC * NOCC + pair_order // NOCC
    matches = (pair_order[:, None] == swapped[None, :]).astype(jnp.float32)
    pairing = jnp.kron(jnp.eye(2, dtype=jnp.float32), matches)
    virtual_energy = lookup(vir_bin, levels)
    occupied_energy = -lookup(occ_bin, levels)
    pair_energy = lookup(pair_order // NOCC, occupied_energy) + lookup(
        pair_order % NOCC, occupied_energy
    )
    left_energy = lax.dynamic_slice_in_dim(virtual_energy, lax.axis_index(DEV) * 4, 4)
    right_energy = lax.dynamic_slice_in_dim(virtual_energy, lax.axis_index(BA) * 2, 2)
    denominator = (
        right_energy[None, :, None]
        + left_energy[:, None, None]
        - pair_energy[None, None, :]
        + level_shift
    ).reshape(4, 128)

    eighths = factors.reshape(64, 8, 128).transpose(1, 0, 2)
    eighths = jnp.broadcast_to(eighths[None], (2, 8, 64, 128)).reshape(16, 64, 128)
    rows = lax.all_to_all(eighths, ("yh", "yl", "c"), 0, 0, tiled=True)
    other = lax.ppermute(amplitudes, "c", [(0, 1), (1, 0)])
    amps, amps_other = (
        t.transpose(1, 0, 2).reshape(STEPS, DSTEP, 64, 512) for t in (amplitudes, other)
    )
    own = lax.dynamic_slice_in_dim(rows, lax.axis_index("yh") * 8, 8)
    own = jnp.broadcast_to(own.reshape(1, 512, 128), (8, 512, 128))
    left = lax.all_to_all(own, "z", 0, 0, tiled=True).reshape(4096, 128)
    rights = [rows] + [
        lax.ppermute(rows, "x", [(i, (i + s) % 4) for i in range(4)]) for s in (1, 3, 2)
    ]
    where = jnp.stack([lax.axis_index("x"), lax.axis_index("c")]).astype(jnp.int32)
    ladder = ladder_parts(products(where, amps, amps_other, rights), left)
    crossed = lax.all_to_all(ladder.reshape(8, 32, 128), "z", 0, 0, tiled=True)
    parts = both_orders(ladder, crossed.reshape(256, 128), pairing)
    parts = lax.all_to_all(parts, GROUP, 0, 0, tiled=True)
    return finished(parts, denominator)


def solution(mesh):
    finer = Mesh(mesh.devices.reshape(SIZES), AXES)
    return jax.shard_map(
        per_device,
        mesh=finer,
        in_specs=(P(BA, DEV, None), P(None, DEV, None), P(), P(), P(), P()),
        out_specs=P(BA, DEV),
        check_vma=False,
    )
```

time: 108 us -> 103 us (0.954)
  Pallas kernels: 18 us -> 15.7 us
  starting transfers between devices: 43.7 us -> 42.2 us
    ppermute x1, starting transfers between devices: 1.91 us -> 8.78 us  [per_device(): other = lax.ppermute(amplitudes, 'c', [(0, 1), (1, 0)])]
    all_to_all x1, starting transfers between devices: 10.2 us -> 3.57 us  [per_device(): rows = lax.all_to_all(eighths, ('yh', 'yl', 'c'), 0, 0, tiled=True)]
    unnamed x14 -> x11, local copies, waits for them, and re-layouts: 5.66 us -> 0.94 us
    transpose x0 -> x2, local copies, waits for them, and re-layouts: none -> 3.92 us  [per_device(): t.transpose(1, 0, 2).reshape(STEPS, DSTEP, 64, 512)]
    pallas_call x2, Pallas kernels: 16.2 us -> 13 us  [the longest x1 7.45 us: products(): pl.pallas_call(product_kernel, in_specs=[pl.BlockSpec(memory_space=pltpu....]
    ppermute x3, waiting for transfers between devices: 6.22 us -> 3.26 us  [per_device(): lax.ppermute(rows, 'x', [(i, (i + s) % 4) for i in range(4)])]
    all_to_all x1, waiting for transfers between devices: 9.07 us -> 11.7 us  [per_device(): rows = lax.all_to_all(eighths, ('yh', 'yl', 'c'), 0, 0, tiled=True)]
    all_to_all x1, starting transfers between devices: 10 us -> 8.14 us  [per_device(): parts = lax.all_to_all(parts, GROUP, 0, 0, tiled=True)]
  transfers between devices with their start and end apart: 8 -> 8, of which waited for: 6 -> 5; matrix products, arithmetic and copies ran while one was open for 5% -> 8% of each run, Pallas kernels for 8% -> 7%
where the time goes in v5:
time: 103 us
  starting transfers between devices  42.2 us (41%)
  waiting for transfers between devices  36.5 us (35%)
  Pallas kernels  15.7 us (15%)
  local copies, waits for them, and re-layouts  7.34 us (7%)
    all_to_all x1, waiting for transfers between devices, per_device(): rows = lax.all_to_all(eighths, ('yh', 'yl', 'c'), 0, 0, tiled=True)  11.7 us
    all_to_all x1, waiting for transfers between devices, per_device(): parts = lax.all_to_all(parts, GROUP, 0, 0, tiled=True)  10.1 us
    ppermute x3, starting transfers between devices, per_device(): lax.ppermute(rows, 'x', [(i, (i + s) % 4) for i in range(4)])  9.93 us
    ppermute x1, starting transfers between devices, per_device(): other = lax.ppermute(amplitudes, 'c', [(0, 1), (1, 0)])  8.78 us
    all_to_all x1, starting transfers between devices, per_device(): left = lax.all_to_all(own, 'z', 0, 0, tiled=True).reshape(4096, 128)  8.41 us
    all_to_all x1, starting transfers between devices, per_device(): parts = lax.all_to_all(parts, GROUP, 0, 0, tiled=True)  8.14 us
    pallas_call x1, Pallas kernels, products(): pl.pallas_call(product_kernel, in_specs=[pl.BlockSpec(memory_space=pltpu....  7.45 us
    all_to_all x1, waiting for transfers between devices, per_device(): crossed = lax.all_to_all(ladder.reshape(8, 32, 128), 'z', 0, 0, tiled=True)  7.15 us
  transfers between devices with their start and end apart: 8, of which 5 were waited for; matrix products, arithmetic and copies ran while one was open for 8% of the time, Pallas kernels for 7%

profile of v5, /device:TPU:1, one launch (start us, length us, event | category | flops | bytes accessed | tf_op | source)
XLA Modules:
  0.0 102.7 jit_solution(4455750785102515884)
XLA Ops:
  0.0 8.8 %collective-permute-start = (bf16[64,32,512]{2,1,0:T(8,128)(2,1)}, bf16[64,32,512]{2,1,0:T(8,128)(2,1)}, u32[]{:S(2)}, u32[]{:S(2)}) collective-permute-start(bf16[64,32,512]{2,1,0:T(8,128)(2,1)} %param.7), channel_id=1, source_target_pairs={{0,1},{1,0},{2,3},{3,2},{4,5},{5,4},{6,7},{7,6},{8,9},{9,8},{10,11... | collective-permute-start | bytes 6291464 | tf_op jit(solution)/shard_map/ppermute | solution.py:231
  8.8 0.9 copy.13
  9.7 0.7 broadcast_in_dim.50
  10.5 0.0 copy-start.2
  10.5 0.0 copy-start.3
  10.5 0.0 copy-start.1
  10.5 0.0 copy-start
  10.5 3.6 %all-to-all-start = ((bf16[16,64,128]{2,1,0:T(8,128)(2,1)}), bf16[16,64,128]{2,1,0:T(8,128)(2,1)S(1)}, u32[]{:S(2)}, u32[]{:S(2)}) async-start(bf16[16,64,128]{2,1,0:T(8,128)(2,1)} %bitcast.7), calls=%async_computation | async-start | bytes 524288 | tf_op jit(solution)/shard_map/all_to_all | solution.py:230
  14.1 11.7 %all-to-all-done.r0_ref = bf16[16,64,128]{2,1,0:T(8,128)(2,1)S(1)} async-done(((bf16[16,64,128]{2,1,0:T(8,128)(2,1)}), bf16[16,64,128]{2,1,0:T(8,128)(2,1)S(1)}, u32[]{:S(2)}, u32[]{:S(2)}) %all-to-all-start) | async-done | bytes 262176 | tf_op jit(solution)/shard_map/all_to_all | solution.py:230
  25.8 1.2 %broadcast_in_dim.76 = bf16[8,512,128]{2,1,0:T(8,128)(2,1)} broadcast(bf16[512,128]{1,0:T(8,128)(2,1)S(1)} %bitcast.21), dimensions={1,2} | broadcast | bytes 1179648 | tf_op jit(solution)/shard_map/broadcast_in_dim | solution.py:236
  27.0 8.4 %all-to-all-start.1 = ((bf16[8,512,128]{2,1,0:T(8,128)(2,1)}), bf16[8,512,128]{2,1,0:T(8,128)(2,1)S(1)}, u32[]{:S(2)}, u32[]{:S(2)}) async-start(bf16[8,512,128]{2,1,0:T(8,128)(2,1)} %broadcast_in_dim.76), calls=%async_computation.1 | async-start | bytes 2097152 | tf_op jit(solution)/shard_map/all_to_all | solution.py:237
  35.4 0.0 copy-done.2
  35.5 0.0 copy-done.3
  35.5 0.2 select_reduce_fusion
  35.6 0.0 copy-done.1
  35.7 0.1 compare_convert_fusion
  35.7 3.1 %collective-permute-start.1 = (bf16[16,64,128]{2,1,0:T(8,128)(2,1)S(1)}, bf16[16,64,128]{2,1,0:T(8,128)(2,1)S(1)}, u32[]{:S(2)}, u32[]{:S(2)}) collective-permute-start(bf16[16,64,128]{2,1,0:T(8,128)(2,1)S(1)} %all-to-all-done.r0_ref), channel_id=1, source_target_pairs={{0,2},{2,4},{4,6},{6,0},{1,3},{3,5},{5,7},{7,1},{8,10},{10,12},{12... | collective-permute-start | bytes 786440 | tf_op jit(solution)/shard_map/ppermute | solution.py:239
  38.9 3.4 %collective-permute-start.2 = (bf16[16,64,128]{2,1,0:T(8,128)(2,1)S(1)}, bf16[16,64,128]{2,1,0:T(8,128)(2,1)S(1)}, u32[]{:S(2)}, u32[]{:S(2)}) collective-permute-start(bf16[16,64,128]{2,1,0:T(8,128)(2,1)S(1)} %all-to-all-done.r0_ref), channel_id=1, source_target_pairs={{0,6},{2,0},{4,2},{6,4},{1,7},{3,1},{5,3},{7,5},{8,14},{10,8},{12,... | collective-permute-start | bytes 786440 | tf_op jit(solution)/shard_map/ppermute | solution.py:239
  42.2 3.4 %collective-permute-start.3 = (bf16[16,64,128]{2,1,0:T(8,128)(2,1)S(1)}, bf16[16,64,128]{2,1,0:T(8,128)(2,1)S(1)}, u32[]{:S(2)}, u32[]{:S(2)}) collective-permute-start(bf16[16,64,128]{2,1,0:T(8,128)(2,1)S(1)} %all-to-all-done.r0_ref), channel_id=1, source_target_pairs={{0,4},{2,6},{4,0},{6,2},{1,5},{3,7},{5,1},{7,3},{8,12},{10,14},{12... | collective-permute-start | bytes 786440 | tf_op jit(solution)/shard_map/ppermute | solution.py:239
  45.7 0.1 pad_add_fusion.where_ref
  45.8 0.0 copy-done
  45.8 1.2 %copy.10 = bf16[32,64,512]{2,1,0:T(8,128)(2,1)S(1)} copy(bf16[32,64,512]{2,0,1:T(8,128)(2,1)S(1)} %bitcast.20) | data formatting | bytes 4194304 | tf_op jit(solution)/shard_map/transpose | solution.py:233
  46.9 0.1 broadcast_multiply_fusion
  47.0 0.0 collective-permute-done
  47.1 2.8 %copy.11 = bf16[32,64,512]{2,1,0:T(8,128)(2,1)S(1)} copy(bf16[32,64,512]{2,0,1:T(8,128)(2,1)} %bitcast.4) | data formatting | bytes 4194304 | tf_op jit(solution)/shard_map/transpose | solution.py:233
  49.8 0.0 collective-permute-done.1.rp_ref
  49.8 0.0 collective-permute-done.2.rm_ref
  49.8 3.3 %collective-permute-done.3.rt_ref = bf16[16,64,128]{2,1,0:T(8,128)(2,1)S(1)} collective-permute-done((bf16[16,64,128]{2,1,0:T(8,128)(2,1)S(1)}, bf16[16,64,128]{2,1,0:T(8,128)(2,1)S(1)}, u32[]{:S(2)}, u32[]{:S(2)}) %collective-permute-start.3) | collective-permute-done | bytes 262176 | tf_op jit(solution)/shard_map/ppermute | solution.py:239
  53.1 7.5 %shard_map.64.prod_ref = bf16[4,512,2048]{2,1,0:T(8,128)(2,1)} custom-call(s32[2]{0:T(128)S(1)} %pad_add_fusion.where_ref, bf16[4,8,64,512]{3,2,1,0:T(8,128)(2,1)S(1)} %bitcast.17, bf16[4,8,64,512]{3,2,1,0:T(8,128)(2,1)S(1)} %bitcast.18, bf16[16,64,128]{2,1,0:T(8,128)(2,1)S(1)} %all-to-all-done.r0_ref, ...), custom_call_target="tpu_custom_call" | custom-call | flops 4294967296 | bytes 14680064 | tf_op jit(solution)/shard_map/pallas_call | solution.py:93
  60.6 4.2 %all-to-all-done.1 = bf16[8,512,128]{2,1,0:T(8,128)(2,1)S(1)} async-done(((bf16[8,512,128]{2,1,0:T(8,128)(2,1)}), bf16[8,512,128]{2,1,0:T(8,128)(2,1)S(1)}, u32[]{:S(2)}, u32[]{:S(2)}) %all-to-all-start.1) | async-done | bytes 1048608 | tf_op jit(solution)/shard_map/all_to_all | solution.py:237
  64.8 0.0 copy-start.4
  64.8 5.6 %shard_map.65.own_ref = f32[256,128]{1,0:T(8,128)} custom-call(bf16[4,512,2048]{2,1,0:T(8,128)(2,1)} %shard_map.64.prod_ref, bf16[4096,128]{1,0:T(8,128)(2,1)S(1)} %bitcast.16), custom_call_target="tpu_custom_call" | custom-call | flops 536870912 | bytes 9437184 | tf_op jit(solution)/shard_map/pallas_call | solution.py:145
  70.4 3.4 %all-to-all-start.2 = ((f32[8,32,128]{2,1,0:T(8,128)}), f32[8,32,128]{2,1,0:T(8,128)S(1)}, u32[]{:S(2)}, u32[]{:S(2)}) async-start(f32[8,32,128]{2,1,0:T(8,128)} %bitcast.10), calls=%async_computation.2 | async-start | bytes 262144 | tf_op jit(solution)/shard_map/all_to_all | solution.py:243
  73.8 0.0 copy-done.4
  73.8 0.2 select_reduce_fusion.3
  74.0 0.1 mul.49.pairing_ref
  74.1 0.1 dynamic_slice.11
  74.2 0.1 dynamic_slice.10
  74.3 0.1 broadcast_add_fusion
  74.3 7.2 %all-to-all-done.2 = f32[8,32,128]{2,1,0:T(8,128)S(1)} async-done(((f32[8,32,128]{2,1,0:T(8,128)}), f32[8,32,128]{2,1,0:T(8,128)S(1)}, u32[]{:S(2)}, u32[]{:S(2)}) %all-to-all-start.2) | async-done | bytes 131104 | tf_op jit(solution)/shard_map/all_to_all | solution.py:243
  81.5 2.0 %shard_map.66 = f32[64,4,128]{2,1,0:T(4,128)} custom-call(f32[256,128]{1,0:T(8,128)} %shard_map.65.own_ref, f32[256,128]{1,0:T(8,128)S(1)} %bitcast.19, f32[128,128]{1,0:T(8,128)S(1)} %mul.49.pairing_ref), custom_call_target="tpu_custom_call" | custom-call | tf_op jit(solution)/shard_map/pallas_call | solution.py:187
  83.4 8.1 %all-to-all-start.3 = ((f32[64,4,128]{2,1,0:T(4,128)}), f32[64,4,128]{2,1,0:T(4,128)S(1)}, u32[]{:S(2)}, u32[]{:S(2)}) async-start(f32[64,4,128]{2,1,0:T(4,128)} %shard_map.66), calls=%async_computation.3 | async-start | bytes 262144 | tf_op jit(solution)/shard_map/all_to_all | solution.py:245
  91.6 0.1 select_reduce_fusion.1
  91.7 0.1 sub.29
  91.7 0.1 sub.30
  91.8 0.1 sub.32
  91.9 10.1 %all-to-all-done.3.parts_ref = f32[64,4,128]{2,1,0:T(4,128)S(1)} async-done(((f32[64,4,128]{2,1,0:T(4,128)}), f32[64,4,128]{2,1,0:T(4,128)S(1)}, u32[]{:S(2)}, u32[]{:S(2)}) %all-to-all-start.3) | async-done | bytes 131104 | tf_op jit(solution)/shard_map/all_to_all | solution.py:245
  102.0 0.7 shard_map.67
  (8 shorter events, 0.1 us)
Async XLA Ops:
  0.0 47.0 %collective-permute-start = (bf16[64,32,512]{2,1,0:T(8,128)(2,1)}, bf16[64,32,512]{2,1,0:T(8,128)(2,1)}, u32[]{:S(2)}, u32[]{:S(2)}) collective-permute-start(bf16[64,32,512]{2,1,0:T(8,128)(2,1)} %param.7), channel_id=1, source_target_pairs={{0,1},{1,0},{2,3},{3,2},{4,5},{5,4},{6,7},{7,6},{8,9},{9,8},{10,11... | collective-permute-start | bytes 6291464 | tf_op jit(solution)/shard_map/ppermute | solution.py:231
  10.5 25.0 %copy-start.2 = (s32[64]{0:T(128)S(1)}, s32[64]{0:T(128)}, u32[]{:S(2)}) copy-start(s32[64]{0:T(128)} %param.10) | copy-start | bytes 772
  10.5 25.0 %copy-start.3 = (f32[128]{0:T(128)S(1)}, f32[128]{0:T(128)}, u32[]{:S(2)}) copy-start(f32[128]{0:T(128)} %param.11) | copy-start | bytes 1540
  10.5 25.1 %copy-start.1 = (s32[64]{0:T(128)S(1)}, s32[64]{0:T(128)}, u32[]{:S(2)}) copy-start(s32[64]{0:T(128)} %param.8) | copy-start | bytes 772
  10.5 35.3 %copy-start = (bf16[64,32,512]{2,1,0:T(8,128)(2,1)S(1)}, bf16[64,32,512]{2,1,0:T(8,128)(2,1)}, u32[]{:S(2)}) copy-start(bf16[64,32,512]{2,1,0:T(8,128)(2,1)} %param.7) | copy-start | bytes 6291460
  10.5 15.3 %all-to-all-start = ((bf16[16,64,128]{2,1,0:T(8,128)(2,1)}), bf16[16,64,128]{2,1,0:T(8,128)(2,1)S(1)}, u32[]{:S(2)}, u32[]{:S(2)}) async-start(bf16[16,64,128]{2,1,0:T(8,128)(2,1)} %bitcast.7), calls=%async_computation | async-start | bytes 524288 | tf_op jit(solution)/shard_map/all_to_all | solution.py:230
  27.0 37.8 %all-to-all-start.1 = ((bf16[8,512,128]{2,1,0:T(8,128)(2,1)}), bf16[8,512,128]{2,1,0:T(8,128)(2,1)S(1)}, u32[]{:S(2)}, u32[]{:S(2)}) async-start(bf16[8,512,128]{2,1,0:T(8,128)(2,1)} %broadcast_in_dim.76), calls=%async_computation.1 | async-start | bytes 2097152 | tf_op jit(solution)/shard_map/all_to_all | solution.py:237
  35.7 14.1 %collective-permute-start.1 = (bf16[16,64,128]{2,1,0:T(8,128)(2,1)S(1)}, bf16[16,64,128]{2,1,0:T(8,128)(2,1)S(1)}, u32[]{:S(2)}, u32[]{:S(2)}) collective-permute-start(bf16[16,64,128]{2,1,0:T(8,128)(2,1)S(1)} %all-to-all-done.r0_ref), channel_id=1, source_target_pairs={{0,2},{2,4},{4,6},{6,0},{1,3},{3,5},{5,7},{7,1},{8,10},{10,12},{12... | collective-permute-start | bytes 786440 | tf_op jit(solution)/shard_map/ppermute | solution.py:239
  38.9 11.0 %collective-permute-start.2 = (bf16[16,64,128]{2,1,0:T(8,128)(2,1)S(1)}, bf16[16,64,128]{2,1,0:T(8,128)(2,1)S(1)}, u32[]{:S(2)}, u32[]{:S(2)}) collective-permute-start(bf16[16,64,128]{2,1,0:T(8,128)(2,1)S(1)} %all-to-all-done.r0_ref), channel_id=1, source_target_pairs={{0,6},{2,0},{4,2},{6,4},{1,7},{3,1},{5,3},{7,5},{8,14},{10,8},{12,... | collective-permute-start | bytes 786440 | tf_op jit(solution)/shard_map/ppermute | solution.py:239
  42.2 10.9 %collective-permute-start.3 = (bf16[16,64,128]{2,1,0:T(8,128)(2,1)S(1)}, bf16[16,64,128]{2,1,0:T(8,128)(2,1)S(1)}, u32[]{:S(2)}, u32[]{:S(2)}) collective-permute-start(bf16[16,64,128]{2,1,0:T(8,128)(2,1)S(1)} %all-to-all-done.r0_ref), channel_id=1, source_target_pairs={{0,4},{2,6},{4,0},{6,2},{1,5},{3,7},{5,1},{7,3},{8,12},{10,14},{12... | collective-permute-start | bytes 786440 | tf_op jit(solution)/shard_map/ppermute | solution.py:239
  64.8 9.0 %copy-start.4 = (s32[8]{0:T(128)S(1)}, s32[8]{0:T(128)}, u32[]{:S(2)}) copy-start(s32[8]{0:T(128)} %param.9) | copy-start | bytes 100
  70.4 11.1 %all-to-all-start.2 = ((f32[8,32,128]{2,1,0:T(8,128)}), f32[8,32,128]{2,1,0:T(8,128)S(1)}, u32[]{:S(2)}, u32[]{:S(2)}) async-start(f32[8,32,128]{2,1,0:T(8,128)} %bitcast.10), calls=%async_computation.2 | async-start | bytes 262144 | tf_op jit(solution)/shard_map/all_to_all | solution.py:243
  83.4 18.6 %all-to-all-start.3 = ((f32[64,4,128]{2,1,0:T(4,128)}), f32[64,4,128]{2,1,0:T(4,128)S(1)}, u32[]{:S(2)}, u32[]{:S(2)}) async-start(f32[64,4,128]{2,1,0:T(4,128)} %shard_map.66), calls=%async_computation.3 | async-start | bytes 262144 | tf_op jit(solution)/shard_map/all_to_all | solution.py:245

commit v6 on v5

--- a/solution.py
+++ b/solution.py
@@ -13,7 +13,7 @@
 SIZES = (8, 4, 2, 4, 2)
 BA = ("z", "yl")
 DEV = ("yh", "x", "c")
-GROUP = ("yl", "yh", "x", "c")
+GROUP = ("yh", "x", "yl", "c")
 level_shift = 0.3
 DSTEP = 8
 STEPS = 4
@@ -29,12 +29,12 @@
 
 
 def product_kernel(
-    where_ref, own_ref, other_ref, r0_ref, rp_ref, rm_ref, rt_ref, out_ref, amps, bmat, prods, amps_sem, b_sem, out_sem
+    where_ref, own_ref, other_ref, r0_ref, rt_ref, rp_ref, rm_ref, out_ref, amps, bmat, prods, amps_sem, b_sem, out_sem
 ):
     x, c = where_ref[0], where_ref[1]
     rights = [
         pltpu.make_async_copy(ref, bmat.at[(x + shift) & 3], b_sem.at[n])
-        for n, (ref, shift) in enumerate(((r0_ref, 0), (rp_ref, 3), (rm_ref, 1), (rt_ref, 2)))
+        for n, (ref, shift) in enumerate(((r0_ref, 0), (rt_ref, 2), (rp_ref, 3), (rm_ref, 1)))
     ]
 
     def load(step, half):
@@ -110,7 +110,7 @@
     )(where, own, other, *rights)
 
 
-def ladder_kernel(prod_ref, left_ref, out_ref, prods, wide, lefts, sem):
+def ladder_kernel(prod_ref, left_ref, pairing_ref, own_ref, sent_ref, prods, wide, lefts, sem):
     copies = [
         pltpu.make_async_copy(prod_ref.at[step], prods.at[step], sem.at[step])
         for step in range(STEPS)
@@ -118,6 +118,7 @@
     for copy in copies:
         copy.start()
     wide[...] = left_ref[...].astype(jnp.float32)
+    total = jnp.zeros((64, 512), jnp.float32)
     for step in range(STEPS):
         for dd in range(DSTEP):
             for cc in range(2):
@@ -127,29 +128,36 @@
                     lefts[step, r * 32 : (r + 1) * 32, lane : lane + 128] = wide[
                         pl.ds(start, 32, stride=128), :
                     ].astype(jnp.bfloat16)
-    total = jnp.zeros((64, 512), jnp.float32)
-    for step in range(STEPS):
         copies[step].wait()
         total += lax.dot_general(
             lefts[step], prods[step], (((1,), (1,)), ((), ())), preferred_element_type=jnp.float32
         )
     for yl in range(4):
+        rows = total[:, yl * 128 : (yl + 1) * 128]
         for r in range(2):
             for z in range(8):
-                out_ref[pl.ds(z * 32 + yl * 8 + r, 4, stride=2), :] = total[
-                    r * 32 + z * 4 : r * 32 + z * 4 + 4, yl * 128 : (yl + 1) * 128
+                own_ref[pl.ds(z * 32 + yl * 8 + r, 4, stride=2), :] = rows[
+                    r * 32 + z * 4 : r * 32 + z * 4 + 4, :
                 ]
-
-
-def ladder_parts(prods, left):
+        rows = jnp.dot(
+            rows,
+            pairing_ref[...],
+            precision=lax.Precision.HIGHEST,
+            preferred_element_type=jnp.float32,
+        )
+        for r in range(2):
+            sent_ref[pl.ds(yl * 2 + r, 32, stride=8), :] = jnp.concatenate(
+                [rows[:32, r * 64 : (r + 1) * 64], rows[32:, r * 64 : (r + 1) * 64]], axis=1
+            )
+
+
+def ladder_parts(prods, left, pairing):
+    inside = pl.BlockSpec(memory_space=pltpu.VMEM)
     return pl.pallas_call(
         ladder_kernel,
-        in_specs=[
-            pl.BlockSpec(memory_space=pltpu.HBM),
-            pl.BlockSpec(memory_space=pltpu.VMEM),
-        ],
-        out_specs=pl.BlockSpec(memory_space=pltpu.VMEM),
-        out_shape=jax.ShapeDtypeStruct((256, 128), jnp.float32),
+        in_specs=[pl.BlockSpec(memory_space=pltpu.HBM), inside, inside],
+        out_specs=[inside] * 2,
+        out_shape=[jax.ShapeDtypeStruct((256, 128), jnp.float32)] * 2,
         scratch_shapes=[
             pltpu.VMEM((STEPS, 512, DSTEP * 256), jnp.bfloat16),
             pltpu.VMEM((4096, 128), jnp.float32),
@@ -160,36 +168,7 @@
         cost_estimate=pl.CostEstimate(
             flops=2 * 64 * 64 * 8 * 8192, bytes_accessed=9 * 1024 * 1024, transcendentals=0
         ),
-    )(prods, left)
-
-
-def both_kernel(own_ref, crossed_ref, pairing_ref, out_ref, turned):
-    for yl in range(4):
-        rows = [crossed_ref[pl.ds(yl * 2 + r, 32, stride=8), :] for r in range(2)]
-        for r in range(2):
-            half = slice(r * 64, (r + 1) * 64)
-            turned[pl.ds(r, 32, stride=2), :] = jnp.concatenate(
-                [rows[0][:, half], rows[1][:, half]], axis=1
-            )
-        partnered = jnp.dot(
-            turned[...],
-            pairing_ref[...],
-            precision=lax.Precision.HIGHEST,
-            preferred_element_type=jnp.float32,
-        )
-        for z in range(8):
-            total = own_ref[z * 32 + yl * 8 : z * 32 + yl * 8 + 8, :] + partnered[z * 8 : z * 8 + 8]
-            out_ref[(yl * 8 + z) * 2] = total[:4]
-            out_ref[(yl * 8 + z) * 2 + 1] = total[4:]
-
-
-def both_orders(own, crossed, pairing):
-    return pl.pallas_call(
-        both_kernel,
-        out_shape=jax.ShapeDtypeStruct((64, 4, 128), jnp.float32),
-        scratch_shapes=[pltpu.VMEM((64, 128), jnp.float32)],
-        compiler_params=pltpu.CompilerParams(vmem_limit_bytes=8 * 1024 * 1024),
-    )(own, crossed, pairing)
+    )(prods, left, pairing)
 
 
 def finish_kernel(parts_ref, shift_ref, out_ref):
@@ -227,8 +206,9 @@
 
     eighths = factors.reshape(64, 8, 128).transpose(1, 0, 2)
     eighths = jnp.broadcast_to(eighths[None], (2, 8, 64, 128)).reshape(16, 64, 128)
+    eighths, sent = lax.optimization_barrier((eighths, amplitudes))
     rows = lax.all_to_all(eighths, ("yh", "yl", "c"), 0, 0, tiled=True)
-    other = lax.ppermute(amplitudes, "c", [(0, 1), (1, 0)])
+    other = lax.ppermute(sent, "c", [(0, 1), (1, 0)])
     amps, amps_other = (
         t.transpose(1, 0, 2).reshape(STEPS, DSTEP, 64, 512) for t in (amplitudes, other)
     )
@@ -236,12 +216,12 @@
     own = jnp.broadcast_to(own.reshape(1, 512, 128), (8, 512, 128))
     left = lax.all_to_all(own, "z", 0, 0, tiled=True).reshape(4096, 128)
     rights = [rows] + [
-        lax.ppermute(rows, "x", [(i, (i + s) % 4) for i in range(4)]) for s in (1, 3, 2)
+        lax.ppermute(rows, "x", [(i, (i + s) % 4) for i in range(4)]) for s in (2, 1, 3)
     ]
     where = jnp.stack([lax.axis_index("x"), lax.axis_index("c")]).astype(jnp.int32)
-    ladder = ladder_parts(products(where, amps, amps_other, rights), left)
-    crossed = lax.all_to_all(ladder.reshape(8, 32, 128), "z", 0, 0, tiled=True)
-    parts = both_orders(ladder, crossed.reshape(256, 128), pairing)
+    own, sent = ladder_parts(products(where, amps, amps_other, rights), left, pairing)
+    crossed = lax.all_to_all(sent.reshape(8, 32, 128), "z", 0, 0, tiled=True)
+    parts = (own.reshape(8, 32, 128) + crossed).reshape(64, 4, 128)
     parts = lax.all_to_all(parts, GROUP, 0, 0, tiled=True)
     return finished(parts, denominator)
 

time: 103 us -> 104 us (level)
  waiting for transfers between devices: 36.5 us -> 32.7 us
  local copies, waits for them, and re-layouts: 7.34 us -> 9.86 us
  other arithmetic: 0.8 us -> 2.11 us
    ppermute x3, waiting for transfers between devices: 3.26 us -> 0.01 us  [per_device(): lax.ppermute(rows, 'x', [(i, (i + s) % 4) for i in range(4)])]
    all_to_all x1, waiting for transfers between devices: 4.23 us -> 2.23 us  [per_device(): left = lax.all_to_all(own, 'z', 0, 0, tiled=True).reshape(4096, 128)]
    pallas_call x1 -> x0, Pallas kernels: 1.96 us -> none  [both_orders(): pl.pallas_call(both_kernel, out_shape=jax.ShapeDtypeStruct((64, 4, 128),...]
    all_to_all x1, starting transfers between devices: 8.14 us -> 6.48 us  [per_device(): parts = lax.all_to_all(parts, GROUP, 0, 0, tiled=True)]
    transpose x2, local copies, waits for them, and re-layouts: 3.92 us -> 5.54 us  [per_device(): t.transpose(1, 0, 2).reshape(STEPS, DSTEP, 64, 512)]
    pallas_call x1, Pallas kernels: 5.59 us -> 6.88 us  [ladder_parts(): pl.pallas_call(ladder_kernel, in_specs=[pl.BlockSpec(memory_space=pltpu.H...]
    ppermute x3, starting transfers between devices: 9.93 us -> 11.1 us  [per_device(): lax.ppermute(rows, 'x', [(i, (i + s) % 4) for i in range(4)])]
    all_to_all x1, starting transfers between devices: 3.38 us -> 4.43 us  [per_device(): crossed = lax.all_to_all(sent.reshape(8, 32, 128), 'z', 0, 0, tiled=True)]
  transfers between devices with their start and end apart: 8 -> 8, of which waited for: 5 -> 4; matrix products, arithmetic and copies ran while one was open for 8% -> 9% of each run, Pallas kernels for 7% -> 8%
where the time goes in v6:
time: 104 us; the launch traced here: 103 us
  starting transfers between devices  42.8 us (41%)
  waiting for transfers between devices  32.7 us (31%)
  Pallas kernels  15.8 us (15%)
  local copies, waits for them, and re-layouts  9.86 us (9%)
  other arithmetic  2.11 us (2%)
    all_to_all x1, waiting for transfers between devices, per_device(): rows = lax.all_to_all(eighths, ('yh', 'yl', 'c'), 0, 0, tiled=True)  11.7 us
    ppermute x3, starting transfers between devices, per_device(): lax.ppermute(rows, 'x', [(i, (i + s) % 4) for i in range(4)])  11.1 us
    all_to_all x1, waiting for transfers between devices, per_device(): parts = lax.all_to_all(parts, GROUP, 0, 0, tiled=True)  11.1 us
    ppermute x1, starting transfers between devices, per_device(): other = lax.ppermute(sent, 'c', [(0, 1), (1, 0)])  8.91 us
    all_to_all x1, starting transfers between devices, per_device(): left = lax.all_to_all(own, 'z', 0, 0, tiled=True).reshape(4096, 128)  8.41 us
    pallas_call x1, Pallas kernels, products(): pl.pallas_call(product_kernel, in_specs=[pl.BlockSpec(memory_space=pltpu....  8.21 us
    all_to_all x1, waiting for transfers between devices, per_device(): crossed = lax.all_to_all(sent.reshape(8, 32, 128), 'z', 0, 0, tiled=True)  7.61 us
    pallas_call x1, Pallas kernels, ladder_parts(): pl.pallas_call(ladder_kernel, in_specs=[pl.BlockSpec(memory_space=pltpu.H...  6.88 us
  transfers between devices with their start and end apart: 8, of which 4 were waited for; matrix products, arithmetic and copies ran while one was open for 9% of the time, Pallas kernels for 8%

profile of v6, /device:TPU:1, one launch (start us, length us, event | category | flops | bytes accessed | tf_op | source)
XLA Modules:
  0.0 103.4 jit_solution(2675765921790822618)
XLA Ops:
  0.0 0.9 copy.13
  1.0 0.7 broadcast_in_dim.50
  1.7 0.0 copy-start
  1.7 8.9 %collective-permute-start = (bf16[64,32,512]{2,1,0:T(8,128)(2,1)}, bf16[64,32,512]{2,1,0:T(8,128)(2,1)}, u32[]{:S(2)}, u32[]{:S(2)}) collective-permute-start(bf16[64,32,512]{2,1,0:T(8,128)(2,1)} %param.7), channel_id=1, source_target_pairs={{0,1},{1,0},{2,3},{3,2},{4,5},{5,4},{6,7},{7,6},{8,9},{9,8},{10,11... | collective-permute-start | bytes 6291464 | tf_op jit(solution)/shard_map/ppermute | solution.py:211
  10.6 3.4 %all-to-all-start = ((bf16[16,64,128]{2,1,0:T(8,128)(2,1)}), bf16[16,64,128]{2,1,0:T(8,128)(2,1)S(1)}, u32[]{:S(2)}, u32[]{:S(2)}) async-start(bf16[16,64,128]{2,1,0:T(8,128)(2,1)} %bitcast.5), calls=%async_computation | async-start | bytes 524288 | tf_op jit(solution)/shard_map/all_to_all | solution.py:210
  14.1 11.7 %all-to-all-done.r0_ref = bf16[16,64,128]{2,1,0:T(8,128)(2,1)S(1)} async-done(((bf16[16,64,128]{2,1,0:T(8,128)(2,1)}), bf16[16,64,128]{2,1,0:T(8,128)(2,1)S(1)}, u32[]{:S(2)}, u32[]{:S(2)}) %all-to-all-start) | async-done | bytes 262176 | tf_op jit(solution)/shard_map/all_to_all | solution.py:210
  25.8 1.2 %broadcast_in_dim.76 = bf16[8,512,128]{2,1,0:T(8,128)(2,1)} broadcast(bf16[512,128]{1,0:T(8,128)(2,1)S(1)} %bitcast.22), dimensions={1,2} | broadcast | bytes 1179648 | tf_op jit(solution)/shard_map/broadcast_in_dim | solution.py:216
  27.0 8.4 %all-to-all-start.1 = ((bf16[8,512,128]{2,1,0:T(8,128)(2,1)}), bf16[8,512,128]{2,1,0:T(8,128)(2,1)S(1)}, u32[]{:S(2)}, u32[]{:S(2)}) async-start(bf16[8,512,128]{2,1,0:T(8,128)(2,1)} %broadcast_in_dim.76), calls=%async_computation.1 | async-start | bytes 2097152 | tf_op jit(solution)/shard_map/all_to_all | solution.py:217
  35.4 0.0 copy-done
  35.5 0.1 compare_convert_fusion
  35.5 4.6 %collective-permute-start.1 = (bf16[16,64,128]{2,1,0:T(8,128)(2,1)S(1)}, bf16[16,64,128]{2,1,0:T(8,128)(2,1)}, u32[]{:S(2)}, u32[]{:S(2)}) collective-permute-start(bf16[16,64,128]{2,1,0:T(8,128)(2,1)S(1)} %all-to-all-done.r0_ref), channel_id=1, source_target_pairs={{0,4},{2,6},{4,0},{6,2},{1,5},{3,7},{5,1},{7,3},{8,12},{10,14},{12... | collective-permute-start | bytes 786440 | tf_op jit(solution)/shard_map/ppermute | solution.py:219
  40.2 2.2 %collective-permute-start.2 = (bf16[16,64,128]{2,1,0:T(8,128)(2,1)S(1)}, bf16[16,64,128]{2,1,0:T(8,128)(2,1)}, u32[]{:S(2)}, u32[]{:S(2)}) collective-permute-start(bf16[16,64,128]{2,1,0:T(8,128)(2,1)S(1)} %all-to-all-done.r0_ref), channel_id=1, source_target_pairs={{0,2},{2,4},{4,6},{6,0},{1,3},{3,5},{5,7},{7,1},{8,10},{10,12},{12... | collective-permute-start | bytes 786440 | tf_op jit(solution)/shard_map/ppermute | solution.py:219
  42.4 4.3 %collective-permute-start.3 = (bf16[16,64,128]{2,1,0:T(8,128)(2,1)S(1)}, bf16[16,64,128]{2,1,0:T(8,128)(2,1)}, u32[]{:S(2)}, u32[]{:S(2)}) collective-permute-start(bf16[16,64,128]{2,1,0:T(8,128)(2,1)S(1)} %all-to-all-done.r0_ref), channel_id=1, source_target_pairs={{0,6},{2,0},{4,2},{6,4},{1,7},{3,1},{5,3},{7,5},{8,14},{10,8},{12,... | collective-permute-start | bytes 786440 | tf_op jit(solution)/shard_map/ppermute | solution.py:219
  46.7 0.7 broadcast_multiply_fusion
  47.5 0.0 copy-start.1
  47.5 0.0 copy-start.2
  47.5 2.8 %copy.10 = bf16[32,64,512]{2,1,0:T(8,128)(2,1)S(1)} copy(bf16[32,64,512]{2,0,1:T(8,128)(2,1)} %bitcast.21) | data formatting | bytes 4194304 | tf_op jit(solution)/shard_map/transpose | solution.py:213
  50.2 1.0 mul.49.pairing_ref
  51.3 0.1 pad_add_fusion.where_ref
  51.3 0.0 copy-done.1
  51.3 0.0 copy-done.2
  51.4 0.2 select_reduce_fusion
  51.5 0.0 collective-permute-done
  51.5 2.8 %copy.12 = bf16[32,64,512]{2,1,0:T(8,128)(2,1)S(1)} copy(bf16[32,64,512]{2,0,1:T(8,128)(2,1)} %bitcast.6) | data formatting | bytes 4194304 | tf_op jit(solution)/shard_map/transpose | solution.py:213
  54.3 0.0 collective-permute-done.1.rt_ref
  54.3 0.0 collective-permute-done.2.rp_ref
  54.3 0.0 collective-permute-done.3.rm_ref
  54.3 8.2 %shard_map.64.prod_ref = bf16[4,512,2048]{2,1,0:T(8,128)(2,1)} custom-call(s32[2]{0:T(128)S(1)} %pad_add_fusion.where_ref, bf16[4,8,64,512]{3,2,1,0:T(8,128)(2,1)S(1)} %bitcast.18, bf16[4,8,64,512]{3,2,1,0:T(8,128)(2,1)S(1)} %bitcast.19, bf16[16,64,128]{2,1,0:T(8,128)(2,1)S(1)} %all-to-all-done.r0_ref, bf16[16,64,128]{2,1,0:T(8,128)(2,1)} %collective-permute-done.1.rt_ref, ...), custom_call_target="tpu_custom_call" | custom-call | flops 4294967296 | bytes 14680064 | tf_op jit(solution)/shard_map/pallas_call | solution.py:93
  62.5 2.2 %all-to-all-done.1 = bf16[8,512,128]{2,1,0:T(8,128)(2,1)S(1)} async-done(((bf16[8,512,128]{2,1,0:T(8,128)(2,1)}), bf16[8,512,128]{2,1,0:T(8,128)(2,1)S(1)}, u32[]{:S(2)}, u32[]{:S(2)}) %all-to-all-start.1) | async-done | bytes 1048608 | tf_op jit(solution)/shard_map/all_to_all | solution.py:217
  64.8 0.0 copy-start.3
  64.8 6.9 %shard_map.65 = (f32[256,128]{1,0:T(8,128)S(1)}, f32[256,128]{1,0:T(8,128)}) custom-call(bf16[4,512,2048]{2,1,0:T(8,128)(2,1)} %shard_map.64.prod_ref, bf16[4096,128]{1,0:T(8,128)(2,1)S(1)} %bitcast.17, f32[128,128]{1,0:T(8,128)S(1)} %mul.49.pairing_ref), custom_call_target="tpu_custom_call" | custom-call | flops 536870912 | bytes 9437184 | tf_op jit(solution)/shard_map/pallas_call | solution.py:156
  71.7 4.4 %all-to-all-start.2 = ((f32[8,32,128]{2,1,0:T(8,128)}), f32[8,32,128]{2,1,0:T(8,128)S(1)}, u32[]{:S(2)}, u32[]{:S(2)}) async-start(f32[8,32,128]{2,1,0:T(8,128)} %bitcast.11), calls=%async_computation.2 | async-start | bytes 262144 | tf_op jit(solution)/shard_map/all_to_all | solution.py:223
  76.1 0.0 copy-done.3
  76.1 0.2 select_reduce_fusion.3
  76.3 0.1 dynamic_slice.11
  76.4 0.1 dynamic_slice.10
  76.5 0.1 broadcast_add_fusion
  76.5 7.6 %all-to-all-done.2 = f32[8,32,128]{2,1,0:T(8,128)S(1)} async-done(((f32[8,32,128]{2,1,0:T(8,128)}), f32[8,32,128]{2,1,0:T(8,128)S(1)}, u32[]{:S(2)}, u32[]{:S(2)}) %all-to-all-start.2) | async-done | bytes 131104 | tf_op jit(solution)/shard_map/all_to_all | solution.py:223
  84.1 0.7 add.68
  84.8 6.5 %all-to-all-start.3 = ((f32[64,4,128]{2,1,0:T(4,128)}), f32[64,4,128]{2,1,0:T(4,128)S(1)}, u32[]{:S(2)}, u32[]{:S(2)}) async-start(f32[64,4,128]{2,1,0:T(4,128)} %bitcast.12), calls=%async_computation.3 | async-start | bytes 262144 | tf_op jit(solution)/shard_map/all_to_all | solution.py:225
  91.3 0.1 select_reduce_fusion.1
  91.4 0.1 sub.29
  91.4 0.1 sub.30
  91.5 0.1 sub.32
  91.6 11.1 %all-to-all-done.3.parts_ref = f32[64,4,128]{2,1,0:T(4,128)S(1)} async-done(((f32[64,4,128]{2,1,0:T(4,128)}), f32[64,4,128]{2,1,0:T(4,128)S(1)}, u32[]{:S(2)}, u32[]{:S(2)}) %all-to-all-start.3) | async-done | bytes 131104 | tf_op jit(solution)/shard_map/all_to_all | solution.py:225
  102.7 0.7 shard_map.66
  (8 shorter events, 0.1 us)
Async XLA Ops:
  1.7 33.7 %copy-start = (s32[64]{0:T(128)S(1)}, s32[64]{0:T(128)}, u32[]{:S(2)}) copy-start(s32[64]{0:T(128)} %param.8) | copy-start | bytes 772
  1.7 49.8 %collective-permute-start = (bf16[64,32,512]{2,1,0:T(8,128)(2,1)}, bf16[64,32,512]{2,1,0:T(8,128)(2,1)}, u32[]{:S(2)}, u32[]{:S(2)}) collective-permute-start(bf16[64,32,512]{2,1,0:T(8,128)(2,1)} %param.7), channel_id=1, source_target_pairs={{0,1},{1,0},{2,3},{3,2},{4,5},{5,4},{6,7},{7,6},{8,9},{9,8},{10,11... | collective-permute-start | bytes 6291464 | tf_op jit(solution)/shard_map/ppermute | solution.py:211
  10.6 15.2 %all-to-all-start = ((bf16[16,64,128]{2,1,0:T(8,128)(2,1)}), bf16[16,64,128]{2,1,0:T(8,128)(2,1)S(1)}, u32[]{:S(2)}, u32[]{:S(2)}) async-start(bf16[16,64,128]{2,1,0:T(8,128)(2,1)} %bitcast.5), calls=%async_computation | async-start | bytes 524288 | tf_op jit(solution)/shard_map/all_to_all | solution.py:210
  27.0 37.8 %all-to-all-start.1 = ((bf16[8,512,128]{2,1,0:T(8,128)(2,1)}), bf16[8,512,128]{2,1,0:T(8,128)(2,1)S(1)}, u32[]{:S(2)}, u32[]{:S(2)}) async-start(bf16[8,512,128]{2,1,0:T(8,128)(2,1)} %broadcast_in_dim.76), calls=%async_computation.1 | async-start | bytes 2097152 | tf_op jit(solution)/shard_map/all_to_all | solution.py:217
  35.5 18.8 %collective-permute-start.1 = (bf16[16,64,128]{2,1,0:T(8,128)(2,1)S(1)}, bf16[16,64,128]{2,1,0:T(8,128)(2,1)}, u32[]{:S(2)}, u32[]{:S(2)}) collective-permute-start(bf16[16,64,128]{2,1,0:T(8,128)(2,1)S(1)} %all-to-all-done.r0_ref), channel_id=1, source_target_pairs={{0,4},{2,6},{4,0},{6,2},{1,5},{3,7},{5,1},{7,3},{8,12},{10,14},{12... | collective-permute-start | bytes 786440 | tf_op jit(solution)/shard_map/ppermute | solution.py:219
  40.2 14.1 %collective-permute-start.2 = (bf16[16,64,128]{2,1,0:T(8,128)(2,1)S(1)}, bf16[16,64,128]{2,1,0:T(8,128)(2,1)}, u32[]{:S(2)}, u32[]{:S(2)}) collective-permute-start(bf16[16,64,128]{2,1,0:T(8,128)(2,1)S(1)} %all-to-all-done.r0_ref), channel_id=1, source_target_pairs={{0,2},{2,4},{4,6},{6,0},{1,3},{3,5},{5,7},{7,1},{8,10},{10,12},{12... | collective-permute-start | bytes 786440 | tf_op jit(solution)/shard_map/ppermute | solution.py:219
  42.4 11.9 %collective-permute-start.3 = (bf16[16,64,128]{2,1,0:T(8,128)(2,1)S(1)}, bf16[16,64,128]{2,1,0:T(8,128)(2,1)}, u32[]{:S(2)}, u32[]{:S(2)}) collective-permute-start(bf16[16,64,128]{2,1,0:T(8,128)(2,1)S(1)} %all-to-all-done.r0_ref), channel_id=1, source_target_pairs={{0,6},{2,0},{4,2},{6,4},{1,7},{3,1},{5,3},{7,5},{8,14},{10,8},{12,... | collective-permute-start | bytes 786440 | tf_op jit(solution)/shard_map/ppermute | solution.py:219
  47.5 3.9 %copy-start.1 = (s32[64]{0:T(128)S(1)}, s32[64]{0:T(128)}, u32[]{:S(2)}) copy-start(s32[64]{0:T(128)} %param.10) | copy-start | bytes 772
  47.5 3.9 %copy-start.2 = (f32[128]{0:T(128)S(1)}, f32[128]{0:T(128)}, u32[]{:S(2)}) copy-start(f32[128]{0:T(128)} %param.11) | copy-start | bytes 1540
  64.8 11.3 %copy-start.3 = (s32[8]{0:T(128)S(1)}, s32[8]{0:T(128)}, u32[]{:S(2)}) copy-start(s32[8]{0:T(128)} %param.9) | copy-start | bytes 100
  71.7 12.5 %all-to-all-start.2 = ((f32[8,32,128]{2,1,0:T(8,128)}), f32[8,32,128]{2,1,0:T(8,128)S(1)}, u32[]{:S(2)}, u32[]{:S(2)}) async-start(f32[8,32,128]{2,1,0:T(8,128)} %bitcast.11), calls=%async_computation.2 | async-start | bytes 262144 | tf_op jit(solution)/shard_map/all_to_all | solution.py:223
  84.8 17.9 %all-to-all-start.3 = ((f32[64,4,128]{2,1,0:T(4,128)}), f32[64,4,128]{2,1,0:T(4,128)S(1)}, u32[]{:S(2)}, u32[]{:S(2)}) async-start(f32[64,4,128]{2,1,0:T(4,128)} %bitcast.12), calls=%async_computation.3 | async-start | bytes 262144 | tf_op jit(solution)/shard_map/all_to_all | solution.py:225

commit v7 on v6

--- a/solution.py
+++ b/solution.py
@@ -17,7 +17,7 @@
 level_shift = 0.3
 DSTEP = 8
 STEPS = 4
-VMEM_A = 24
+VMEM_A = 52
 VMEM_B = 49
 
 
@@ -132,19 +132,21 @@
         total += lax.dot_general(
             lefts[step], prods[step], (((1,), (1,)), ((), ())), preferred_element_type=jnp.float32
         )
-    for yl in range(4):
-        rows = total[:, yl * 128 : (yl + 1) * 128]
+    chunks = [total[:, yl * 128 : (yl + 1) * 128] for yl in range(4)]
+    for yl, rows in enumerate(chunks):
         for r in range(2):
             for z in range(8):
                 own_ref[pl.ds(z * 32 + yl * 8 + r, 4, stride=2), :] = rows[
                     r * 32 + z * 4 : r * 32 + z * 4 + 4, :
                 ]
-        rows = jnp.dot(
-            rows,
-            pairing_ref[...],
-            precision=lax.Precision.HIGHEST,
-            preferred_element_type=jnp.float32,
-        )
+    rest = jnp.concatenate(chunks, axis=0)
+    paired = jnp.zeros((256, 128), jnp.float32)
+    for _ in range(3):
+        part = rest.astype(jnp.bfloat16)
+        paired += jnp.dot(part, pairing_ref[...], preferred_element_type=jnp.float32)
+        rest = rest - part.astype(jnp.float32)
+    for yl in range(4):
+        rows = paired[yl * 64 : (yl + 1) * 64]
         for r in range(2):
             sent_ref[pl.ds(yl * 2 + r, 32, stride=8), :] = jnp.concatenate(
                 [rows[:32, r * 64 : (r + 1) * 64], rows[32:, r * 64 : (r + 1) * 64]], axis=1
@@ -188,8 +190,9 @@
 
 def per_device(factors, amplitudes, pair_order, occ_bin, vir_bin, levels):
     swapped = pair_order % NOCC * NOCC + pair_order // NOCC
-    matches = (pair_order[:, None] == swapped[None, :]).astype(jnp.float32)
-    pairing = jnp.kron(jnp.eye(2, dtype=jnp.float32), matches)
+    lane = jnp.arange(128, dtype=jnp.int32)
+    matches = jnp.tile(pair_order, 2)[:, None] == jnp.tile(swapped, 2)[None, :]
+    pairing = (matches & (lane[:, None] // 64 == lane[None, :] // 64)).astype(jnp.bfloat16)
     virtual_energy = lookup(vir_bin, levels)
     occupied_energy = -lookup(occ_bin, levels)
     pair_energy = lookup(pair_order // NOCC, occupied_energy) + lookup(
@@ -212,6 +215,7 @@
     amps, amps_other = (
         t.transpose(1, 0, 2).reshape(STEPS, DSTEP, 64, 512) for t in (amplitudes, other)
     )
+    rows, amps, amps_other, pairing = lax.optimization_barrier((rows, amps, amps_other, pairing))
     own = lax.dynamic_slice_in_dim(rows, lax.axis_index("yh") * 8, 8)
     own = jnp.broadcast_to(own.reshape(1, 512, 128), (8, 512, 128))
     left = lax.all_to_all(own, "z", 0, 0, tiled=True).reshape(4096, 128)

time: 104 us -> 105 us (level)
    all_to_all x1, waiting for transfers between devices: 11.7 us -> 3.51 us  [per_device(): rows = lax.all_to_all(eighths, ('yh', 'yl', 'c'), 0, 0, tiled=True)]
    ppermute x3, waiting for transfers between devices: 0.01 us -> 5.85 us  [per_device(): lax.ppermute(rows, 'x', [(i, (i + s) % 4) for i in range(4)])]
    all_to_all x1, starting transfers between devices: 6.48 us -> 8.27 us  [per_device(): parts = lax.all_to_all(parts, GROUP, 0, 0, tiled=True)]
    all_to_all x1, waiting for transfers between devices: 2.23 us -> 3.73 us  [per_device(): left = lax.all_to_all(own, 'z', 0, 0, tiled=True).reshape(4096, 128)]
    transpose x2, local copies, waits for them, and re-layouts: 5.54 us -> 6.61 us  [per_device(): t.transpose(1, 0, 2).reshape(STEPS, DSTEP, 64, 512)]
    all_to_all x1, starting transfers between devices: 4.43 us -> 3.38 us  [per_device(): crossed = lax.all_to_all(sent.reshape(8, 32, 128), 'z', 0, 0, tiled=True)]
  transfers between devices with their start and end apart: 8 -> 8, of which waited for: 4 -> 5; matrix products, arithmetic and copies ran while one was open for 9% -> 9% of each run, Pallas kernels for 8% -> 8%
where the time goes in v7:
time: 105 us; the launch traced here: 104 us
  starting transfers between devices  43.4 us (41%)
  waiting for transfers between devices  31.8 us (30%)
  Pallas kernels  15.8 us (15%)
  local copies, waits for them, and re-layouts  10.7 us (10%)
  other arithmetic  2.04 us (2%)
    ppermute x3, starting transfers between devices, per_device(): lax.ppermute(rows, 'x', [(i, (i + s) % 4) for i in range(4)])  11.1 us
    all_to_all x1, waiting for transfers between devices, per_device(): parts = lax.all_to_all(parts, GROUP, 0, 0, tiled=True)  11.1 us
    ppermute x1, starting transfers between devices, per_device(): other = lax.ppermute(sent, 'c', [(0, 1), (1, 0)])  8.78 us
    all_to_all x1, starting transfers between devices, per_device(): left = lax.all_to_all(own, 'z', 0, 0, tiled=True).reshape(4096, 128)  8.41 us
    pallas_call x1, Pallas kernels, products(): pl.pallas_call(product_kernel, in_specs=[pl.BlockSpec(memory_space=pltpu....  8.34 us
    all_to_all x1, starting transfers between devices, per_device(): parts = lax.all_to_all(parts, GROUP, 0, 0, tiled=True)  8.27 us
    all_to_all x1, waiting for transfers between devices, per_device(): crossed = lax.all_to_all(sent.reshape(8, 32, 128), 'z', 0, 0, tiled=True)  7.67 us
    pallas_call x1, Pallas kernels, ladder_parts(): pl.pallas_call(ladder_kernel, in_specs=[pl.BlockSpec(memory_space=pltpu.H...  6.71 us
  transfers between devices with their start and end apart: 8, of which 5 were waited for; matrix products, arithmetic and copies ran while one was open for 9% of the time, Pallas kernels for 8%

profile of v7, /device:TPU:1, one launch (start us, length us, event | category | flops | bytes accessed | tf_op | source)
XLA Modules:
  0.0 103.9 jit_solution(13351403373503302733)
XLA Ops:
  0.0 0.9 copy.13
  1.0 0.8 broadcast_in_dim.46
  1.7 8.8 %collective-permute-start = (bf16[64,32,512]{2,1,0:T(8,128)(2,1)}, bf16[64,32,512]{2,1,0:T(8,128)(2,1)S(1)}, u32[]{:S(2)}, u32[]{:S(2)}) collective-permute-start(bf16[64,32,512]{2,1,0:T(8,128)(2,1)} %param.7), channel_id=1, source_target_pairs={{0,1},{1,0},{2,3},{3,2},{4,5},{5,4},{6,7},{7,6},{8,9},{9,8},{10,11... | collective-permute-start | bytes 6291464 | tf_op jit(solution)/shard_map/ppermute | solution.py:214
  10.5 3.4 %all-to-all-start = ((bf16[16,64,128]{2,1,0:T(8,128)(2,1)}), bf16[16,64,128]{2,1,0:T(8,128)(2,1)S(1)}, u32[]{:S(2)}, u32[]{:S(2)}) async-start(bf16[16,64,128]{2,1,0:T(8,128)(2,1)} %bitcast.3), calls=%async_computation | async-start | bytes 524288 | tf_op jit(solution)/shard_map/all_to_all | solution.py:213
  13.9 0.7 multiply_add_fusion
  14.6 0.1 eq.87
  14.7 0.7 tile.4
  15.4 0.1 eq.43
  15.4 4.1 %copy.11 = bf16[32,64,512]{2,1,0:T(8,128)(2,1)} copy(bf16[32,64,512]{2,0,1:T(8,128)(2,1)} %bitcast.19) | data formatting | bytes 4194304 | tf_op jit(solution)/shard_map/transpose | solution.py:216
  19.6 0.1 and_convert_fusion.pairing_ref
  19.7 0.0 collective-permute-done
  19.7 2.5 %copy.12 = bf16[32,64,512]{2,1,0:T(8,128)(2,1)} copy(bf16[32,64,512]{2,0,1:T(8,128)(2,1)S(1)} %bitcast.22) | data formatting | bytes 4194304 | tf_op jit(solution)/shard_map/transpose | solution.py:216
  22.2 0.0 copy-start
  22.2 0.0 copy-start.1
  22.2 3.5 %all-to-all-done.r0_ref = bf16[16,64,128]{2,1,0:T(8,128)(2,1)S(1)} async-done(((bf16[16,64,128]{2,1,0:T(8,128)(2,1)}), bf16[16,64,128]{2,1,0:T(8,128)(2,1)S(1)}, u32[]{:S(2)}, u32[]{:S(2)}) %all-to-all-start) | async-done | bytes 262176 | tf_op jit(solution)/shard_map/all_to_all | solution.py:213
  25.7 1.2 %broadcast_in_dim.72 = bf16[8,512,128]{2,1,0:T(8,128)(2,1)} broadcast(bf16[512,128]{1,0:T(8,128)(2,1)S(1)} %bitcast.23), dimensions={1,2} | broadcast | bytes 1179648 | tf_op jit(solution)/shard_map/broadcast_in_dim | solution.py:220
  26.9 8.4 %all-to-all-start.1 = ((bf16[8,512,128]{2,1,0:T(8,128)(2,1)}), bf16[8,512,128]{2,1,0:T(8,128)(2,1)S(1)}, u32[]{:S(2)}, u32[]{:S(2)}) async-start(bf16[8,512,128]{2,1,0:T(8,128)(2,1)} %broadcast_in_dim.72), calls=%async_computation.1 | async-start | bytes 2097152 | tf_op jit(solution)/shard_map/all_to_all | solution.py:221
  35.3 4.6 %collective-permute-start.1 = (bf16[16,64,128]{2,1,0:T(8,128)(2,1)S(1)}, bf16[16,64,128]{2,1,0:T(8,128)(2,1)S(1)}, u32[]{:S(2)}, u32[]{:S(2)}) collective-permute-start(bf16[16,64,128]{2,1,0:T(8,128)(2,1)S(1)} %all-to-all-done.r0_ref), channel_id=1, source_target_pairs={{0,4},{2,6},{4,0},{6,2},{1,5},{3,7},{5,1},{7,3},{8,12},{10,14},{12... | collective-permute-start | bytes 786440 | tf_op jit(solution)/shard_map/ppermute | solution.py:223
  39.9 2.2 %collective-permute-start.2 = (bf16[16,64,128]{2,1,0:T(8,128)(2,1)S(1)}, bf16[16,64,128]{2,1,0:T(8,128)(2,1)S(1)}, u32[]{:S(2)}, u32[]{:S(2)}) collective-permute-start(bf16[16,64,128]{2,1,0:T(8,128)(2,1)S(1)} %all-to-all-done.r0_ref), channel_id=1, source_target_pairs={{0,2},{2,4},{4,6},{6,0},{1,3},{3,5},{5,7},{7,1},{8,10},{10,12},{12... | collective-permute-start | bytes 786440 | tf_op jit(solution)/shard_map/ppermute | solution.py:223
  42.2 4.3 %collective-permute-start.3 = (bf16[16,64,128]{2,1,0:T(8,128)(2,1)S(1)}, bf16[16,64,128]{2,1,0:T(8,128)(2,1)S(1)}, u32[]{:S(2)}, u32[]{:S(2)}) collective-permute-start(bf16[16,64,128]{2,1,0:T(8,128)(2,1)S(1)} %all-to-all-done.r0_ref), channel_id=1, source_target_pairs={{0,6},{2,0},{4,2},{6,4},{1,7},{3,1},{5,3},{7,5},{8,14},{10,8},{12,... | collective-permute-start | bytes 786440 | tf_op jit(solution)/shard_map/ppermute | solution.py:223
  46.5 0.1 pad_add_fusion.where_ref
  46.5 0.0 copy-done
  46.5 0.0 copy-done.1
  46.5 0.2 select_reduce_fusion
  46.7 0.0 collective-permute-done.1.rt_ref
  46.7 5.8 %collective-permute-done.2.rp_ref = bf16[16,64,128]{2,1,0:T(8,128)(2,1)S(1)} collective-permute-done((bf16[16,64,128]{2,1,0:T(8,128)(2,1)S(1)}, bf16[16,64,128]{2,1,0:T(8,128)(2,1)S(1)}, u32[]{:S(2)}, u32[]{:S(2)}) %collective-permute-start.2) | collective-permute-done | bytes 262176 | tf_op jit(solution)/shard_map/ppermute | solution.py:223
  52.6 0.0 collective-permute-done.3.rm_ref
  52.6 8.3 %shard_map.64.prod_ref = bf16[4,512,2048]{2,1,0:T(8,128)(2,1)} custom-call(s32[2]{0:T(128)S(1)} %pad_add_fusion.where_ref, bf16[4,8,64,512]{3,2,1,0:T(8,128)(2,1)} %bitcast.20, bf16[4,8,64,512]{3,2,1,0:T(8,128)(2,1)} %bitcast.21, bf16[16,64,128]{2,1,0:T(8,128)(2,1)S(1)} %all-to-all-done.r0_ref, bf16[16,64,128]{2,1,0:T(8,128)(2,1)S(1)} %collective-permute-done.1.rt_ref, ...), custom_call_target="tpu_custom_call" | custom-call | flops 4294967296 | bytes 14680064 | tf_op jit(solution)/shard_map/pallas_call | solution.py:93
  60.9 3.7 %all-to-all-done.1 = bf16[8,512,128]{2,1,0:T(8,128)(2,1)S(1)} async-done(((bf16[8,512,128]{2,1,0:T(8,128)(2,1)}), bf16[8,512,128]{2,1,0:T(8,128)(2,1)S(1)}, u32[]{:S(2)}, u32[]{:S(2)}) %all-to-all-start.1) | async-done | bytes 1048608 | tf_op jit(solution)/shard_map/all_to_all | solution.py:221
  64.6 0.0 copy-start.2
  64.7 6.7 %shard_map.65 = (f32[256,128]{1,0:T(8,128)S(1)}, f32[256,128]{1,0:T(8,128)}) custom-call(bf16[4,512,2048]{2,1,0:T(8,128)(2,1)} %shard_map.64.prod_ref, bf16[4096,128]{1,0:T(8,128)(2,1)S(1)} %bitcast.17, bf16[128,128]{1,0:T(8,128)(2,1)S(1)} %and_convert_fusion.pairing_ref), custom_call_target="tpu_custom_call" | custom-call | flops 536870912 | bytes 9437184 | tf_op jit(solution)/shard_map/pallas_call | solution.py:158
  71.4 3.4 %all-to-all-start.2 = ((f32[8,32,128]{2,1,0:T(8,128)}), f32[8,32,128]{2,1,0:T(8,128)S(1)}, u32[]{:S(2)}, u32[]{:S(2)}) async-start(f32[8,32,128]{2,1,0:T(8,128)} %bitcast.11), calls=%async_computation.2 | async-start | bytes 262144 | tf_op jit(solution)/shard_map/all_to_all | solution.py:227
  74.8 0.0 copy-done.2
  74.8 0.2 select_reduce_fusion.3
  75.0 0.1 dynamic_slice.11
  75.0 0.1 dynamic_slice.10
  75.1 0.1 broadcast_add_fusion
  75.2 7.7 %all-to-all-done.2 = f32[8,32,128]{2,1,0:T(8,128)S(1)} async-done(((f32[8,32,128]{2,1,0:T(8,128)}), f32[8,32,128]{2,1,0:T(8,128)S(1)}, u32[]{:S(2)}, u32[]{:S(2)}) %all-to-all-start.2) | async-done | bytes 131104 | tf_op jit(solution)/shard_map/all_to_all | solution.py:227
  82.8 0.7 add.80
  83.5 8.3 %all-to-all-start.3 = ((f32[64,4,128]{2,1,0:T(4,128)}), f32[64,4,128]{2,1,0:T(4,128)S(1)}, u32[]{:S(2)}, u32[]{:S(2)}) async-start(f32[64,4,128]{2,1,0:T(4,128)} %bitcast.12), calls=%async_computation.3 | async-start | bytes 262144 | tf_op jit(solution)/shard_map/all_to_all | solution.py:229
  91.8 0.1 select_reduce_fusion.1
  91.9 0.1 sub.40
  91.9 0.1 sub.41
  92.0 0.1 sub.43
  92.1 11.1 %all-to-all-done.3.parts_ref = f32[64,4,128]{2,1,0:T(4,128)S(1)} async-done(((f32[64,4,128]{2,1,0:T(4,128)}), f32[64,4,128]{2,1,0:T(4,128)S(1)}, u32[]{:S(2)}, u32[]{:S(2)}) %all-to-all-start.3) | async-done | bytes 131104 | tf_op jit(solution)/shard_map/all_to_all | solution.py:229
  103.2 0.7 shard_map.66
  (8 shorter events, 0.1 us)
Async XLA Ops:
  1.7 18.0 %collective-permute-start = (bf16[64,32,512]{2,1,0:T(8,128)(2,1)}, bf16[64,32,512]{2,1,0:T(8,128)(2,1)S(1)}, u32[]{:S(2)}, u32[]{:S(2)}) collective-permute-start(bf16[64,32,512]{2,1,0:T(8,128)(2,1)} %param.7), channel_id=1, source_target_pairs={{0,1},{1,0},{2,3},{3,2},{4,5},{5,4},{6,7},{7,6},{8,9},{9,8},{10,11... | collective-permute-start | bytes 6291464 | tf_op jit(solution)/shard_map/ppermute | solution.py:214
  10.5 15.2 %all-to-all-start = ((bf16[16,64,128]{2,1,0:T(8,128)(2,1)}), bf16[16,64,128]{2,1,0:T(8,128)(2,1)S(1)}, u32[]{:S(2)}, u32[]{:S(2)}) async-start(bf16[16,64,128]{2,1,0:T(8,128)(2,1)} %bitcast.3), calls=%async_computation | async-start | bytes 524288 | tf_op jit(solution)/shard_map/all_to_all | solution.py:213
  22.2 24.4 %copy-start = (s32[64]{0:T(128)S(1)}, s32[64]{0:T(128)}, u32[]{:S(2)}) copy-start(s32[64]{0:T(128)} %param.10) | copy-start | bytes 772
  22.2 24.4 %copy-start.1 = (f32[128]{0:T(128)S(1)}, f32[128]{0:T(128)}, u32[]{:S(2)}) copy-start(f32[128]{0:T(128)} %param.11) | copy-start | bytes 1540
  26.9 37.8 %all-to-all-start.1 = ((bf16[8,512,128]{2,1,0:T(8,128)(2,1)}), bf16[8,512,128]{2,1,0:T(8,128)(2,1)S(1)}, u32[]{:S(2)}, u32[]{:S(2)}) async-start(bf16[8,512,128]{2,1,0:T(8,128)(2,1)} %broadcast_in_dim.72), calls=%async_computation.1 | async-start | bytes 2097152 | tf_op jit(solution)/shard_map/all_to_all | solution.py:221
  35.3 11.4 %collective-permute-start.1 = (bf16[16,64,128]{2,1,0:T(8,128)(2,1)S(1)}, bf16[16,64,128]{2,1,0:T(8,128)(2,1)S(1)}, u32[]{:S(2)}, u32[]{:S(2)}) collective-permute-start(bf16[16,64,128]{2,1,0:T(8,128)(2,1)S(1)} %all-to-all-done.r0_ref), channel_id=1, source_target_pairs={{0,4},{2,6},{4,0},{6,2},{1,5},{3,7},{5,1},{7,3},{8,12},{10,14},{12... | collective-permute-start | bytes 786440 | tf_op jit(solution)/shard_map/ppermute | solution.py:223
  39.9 12.6 %collective-permute-start.2 = (bf16[16,64,128]{2,1,0:T(8,128)(2,1)S(1)}, bf16[16,64,128]{2,1,0:T(8,128)(2,1)S(1)}, u32[]{:S(2)}, u32[]{:S(2)}) collective-permute-start(bf16[16,64,128]{2,1,0:T(8,128)(2,1)S(1)} %all-to-all-done.r0_ref), channel_id=1, source_target_pairs={{0,2},{2,4},{4,6},{6,0},{1,3},{3,5},{5,7},{7,1},{8,10},{10,12},{12... | collective-permute-start | bytes 786440 | tf_op jit(solution)/shard_map/ppermute | solution.py:223
  42.2 10.4 %collective-permute-start.3 = (bf16[16,64,128]{2,1,0:T(8,128)(2,1)S(1)}, bf16[16,64,128]{2,1,0:T(8,128)(2,1)S(1)}, u32[]{:S(2)}, u32[]{:S(2)}) collective-permute-start(bf16[16,64,128]{2,1,0:T(8,128)(2,1)S(1)} %all-to-all-done.r0_ref), channel_id=1, source_target_pairs={{0,6},{2,0},{4,2},{6,4},{1,7},{3,1},{5,3},{7,5},{8,14},{10,8},{12,... | collective-permute-start | bytes 786440 | tf_op jit(solution)/shard_map/ppermute | solution.py:223
  64.6 10.1 %copy-start.2 = (s32[8]{0:T(128)S(1)}, s32[8]{0:T(128)}, u32[]{:S(2)}) copy-start(s32[8]{0:T(128)} %param.9) | copy-start | bytes 100
  71.4 11.5 %all-to-all-start.2 = ((f32[8,32,128]{2,1,0:T(8,128)}), f32[8,32,128]{2,1,0:T(8,128)S(1)}, u32[]{:S(2)}, u32[]{:S(2)}) async-start(f32[8,32,128]{2,1,0:T(8,128)} %bitcast.11), calls=%async_computation.2 | async-start | bytes 262144 | tf_op jit(solution)/shard_map/all_to_all | solution.py:227
  83.5 19.7 %all-to-all-start.3 = ((f32[64,4,128]{2,1,0:T(4,128)}), f32[64,4,128]{2,1,0:T(4,128)S(1)}, u32[]{:S(2)}, u32[]{:S(2)}) async-start(f32[64,4,128]{2,1,0:T(4,128)} %bitcast.12), calls=%async_computation.3 | async-start | bytes 262144 | tf_op jit(solution)/shard_map/all_to_all | solution.py:229

commit v8 on v7

--- a/solution.py
+++ b/solution.py
@@ -28,6 +28,45 @@
     )
 
 
+def eighths_kernel(factors_ref, out_ref):
+    for part in range(8):
+        for r in range(2):
+            chunk = factors_ref[r, :, part * 128 : (part + 1) * 128]
+            for yh in range(2):
+                out_ref[yh * 8 + part, r * 32 : (r + 1) * 32, :] = chunk
+
+
+def in_eighths(factors):
+    return pl.pallas_call(
+        eighths_kernel,
+        out_shape=jax.ShapeDtypeStruct((16, 64, 128), jnp.bfloat16),
+        compiler_params=pltpu.CompilerParams(vmem_limit_bytes=60 * 1024 * 1024),
+    )(factors)
+
+
+def spread_kernel(where_ref, rows_ref, out_ref, sem):
+    own = rows_ref.at[pl.ds(where_ref[2] * 8, 8)]
+    copies = [pltpu.make_async_copy(own, out_ref.at[z], sem.at[z]) for z in range(8)]
+    for copy in copies:
+        copy.start()
+    for copy in copies:
+        copy.wait()
+
+
+def for_each_plane(where, rows):
+    return pl.pallas_call(
+        spread_kernel,
+        in_specs=[
+            pl.BlockSpec(memory_space=pltpu.SMEM),
+            pl.BlockSpec(memory_space=pl.ANY),
+        ],
+        out_specs=pl.BlockSpec(memory_space=pl.ANY),
+        out_shape=jax.ShapeDtypeStruct((8, 8, 64, 128), jnp.bfloat16),
+        scratch_shapes=[pltpu.SemaphoreType.DMA((8,))],
+        compiler_params=pltpu.CompilerParams(vmem_limit_bytes=8 * 1024 * 1024),
+    )(where, rows)
+
+
 def product_kernel(
     where_ref, own_ref, other_ref, r0_ref, rt_ref, rp_ref, rm_ref, out_ref, amps, bmat, prods, amps_sem, b_sem, out_sem
 ):
@@ -41,12 +80,17 @@
         ref, place = ((own_ref, c), (other_ref, 1 - c))[half]
         return pltpu.make_async_copy(ref.at[step], amps.at[place, step], amps_sem.at[half, step])
 
-    def store(step):
-        return pltpu.make_async_copy(prods.at[step], out_ref.at[step], out_sem.at[step])
-
+    def store(step, yl):
+        rows = pl.ds(yl * 128, 128)
+        return pltpu.make_async_copy(
+            prods.at[step, rows], out_ref.at[step, rows], out_sem.at[step, yl]
+        )
+
+    load(0, 0).start()
+    load(0, 1).start()
     for copy in rights:
         copy.start()
-    for step in range(STEPS):
+    for step in range(1, STEPS):
         load(step, 0).start()
         load(step, 1).start()
     for copy in rights:
@@ -79,12 +123,13 @@
                         prods[step, b * 64 : (b + 1) * 64, lane : lane + 128] = prod[
                             dd * 64 : (dd + 1) * 64, r * 128 : (r + 1) * 128
                         ]
-        store(step).start()
+            store(step, yl).start()
         return 0
 
     lax.fori_loop(0, STEPS, one_step, 0)
     for step in range(STEPS):
-        store(step).wait()
+        for yl in range(4):
+            store(step, yl).wait()
 
 
 def products(where, own, other, rights):
@@ -101,7 +146,7 @@
             pltpu.VMEM(shape, jnp.bfloat16),
             pltpu.SemaphoreType.DMA((2, STEPS)),
             pltpu.SemaphoreType.DMA((4,)),
-            pltpu.SemaphoreType.DMA((STEPS,)),
+            pltpu.SemaphoreType.DMA((STEPS, 4)),
         ],
         compiler_params=pltpu.CompilerParams(vmem_limit_bytes=VMEM_A * 1024 * 1024),
         cost_estimate=pl.CostEstimate(
@@ -207,22 +252,22 @@
         + level_shift
     ).reshape(4, 128)
 
-    eighths = factors.reshape(64, 8, 128).transpose(1, 0, 2)
-    eighths = jnp.broadcast_to(eighths[None], (2, 8, 64, 128)).reshape(16, 64, 128)
+    where = jnp.stack([lax.axis_index(n) for n in ("x", "c", "yh")]).astype(jnp.int32)
+    eighths = in_eighths(factors)
     eighths, sent = lax.optimization_barrier((eighths, amplitudes))
     rows = lax.all_to_all(eighths, ("yh", "yl", "c"), 0, 0, tiled=True)
     other = lax.ppermute(sent, "c", [(0, 1), (1, 0)])
     amps, amps_other = (
         t.transpose(1, 0, 2).reshape(STEPS, DSTEP, 64, 512) for t in (amplitudes, other)
     )
-    rows, amps, amps_other, pairing = lax.optimization_barrier((rows, amps, amps_other, pairing))
-    own = lax.dynamic_slice_in_dim(rows, lax.axis_index("yh") * 8, 8)
-    own = jnp.broadcast_to(own.reshape(1, 512, 128), (8, 512, 128))
+    rows, amps, amps_other, pairing, where = lax.optimization_barrier(
+        (rows, amps, amps_other, pairing, where)
+    )
+    own = for_each_plane(where, rows).reshape(8, 512, 128)
     left = lax.all_to_all(own, "z", 0, 0, tiled=True).reshape(4096, 128)
     rights = [rows] + [
         lax.ppermute(rows, "x", [(i, (i + s) % 4) for i in range(4)]) for s in (2, 1, 3)
     ]
-    where = jnp.stack([lax.axis_index("x"), lax.axis_index("c")]).astype(jnp.int32)
     own, sent = ladder_parts(products(where, amps, amps_other, rights), left, pairing)
     crossed = lax.all_to_all(sent.reshape(8, 32, 128), "z", 0, 0, tiled=True)
     parts = (own.reshape(8, 32, 128) + crossed).reshape(64, 4, 128)

time: 105 us -> 105 us (level)
  local copies, waits for them, and re-layouts: 10.7 us -> 7.84 us
  Pallas kernels: 15.8 us -> 18.6 us
    pallas_call x0 -> x2, Pallas kernels: none -> 3.3 us  [the longest x1 1.66 us: for_each_plane(): pl.pallas_call(spread_kernel, in_specs=[pl.BlockSpec(memory_space=pltpu.S...]
    broadcast_in_dim x2 -> x0, local copies, waits for them, and re-layouts: 1.93 us -> none  [the longest x1 1.18 us: per_device(): own = jnp.broadcast_to(own.reshape(1, 512, 128), (8, 512, 128))]
where the time goes in v8:
time: 105 us; the launch traced here: 104 us
  starting transfers between devices  43.3 us (41%)
  waiting for transfers between devices  32.3 us (31%)
  Pallas kernels  18.6 us (18%)
  local copies, waits for them, and re-layouts  7.84 us (7%)
  other arithmetic  2.04 us (2%)
    ppermute x3, starting transfers between devices, per_device(): lax.ppermute(rows, 'x', [(i, (i + s) % 4) for i in range(4)])  11.1 us
    all_to_all x1, waiting for transfers between devices, per_device(): parts = lax.all_to_all(parts, GROUP, 0, 0, tiled=True)  11.1 us
    ppermute x1, starting transfers between devices, per_device(): other = lax.ppermute(sent, 'c', [(0, 1), (1, 0)])  8.78 us
    all_to_all x1, starting transfers between devices, per_device(): left = lax.all_to_all(own, 'z', 0, 0, tiled=True).reshape(4096, 128)  8.42 us
    all_to_all x1, starting transfers between devices, per_device(): parts = lax.all_to_all(parts, GROUP, 0, 0, tiled=True)  8.2 us
    pallas_call x1, Pallas kernels, products(): pl.pallas_call(product_kernel, in_specs=[pl.BlockSpec(memory_space=pltpu....  7.87 us
    all_to_all x1, waiting for transfers between devices, per_device(): crossed = lax.all_to_all(sent.reshape(8, 32, 128), 'z', 0, 0, tiled=True)  7.66 us
    pallas_call x1, Pallas kernels, ladder_parts(): pl.pallas_call(ladder_kernel, in_specs=[pl.BlockSpec(memory_space=pltpu.H...  6.7 us
  transfers between devices with their start and end apart: 8, of which 5 were waited for; matrix products, arithmetic and copies ran while one was open for 9% of the time, Pallas kernels for 8%

profile of v8, /device:TPU:1, one launch (start us, length us, event | category | flops | bytes accessed | tf_op | source)
XLA Modules:
  0.0 104.3 jit_solution(680046307328945275)
XLA Ops:
  0.0 1.6 %shard_map.64 = bf16[16,64,128]{2,1,0:T(8,128)(2,1)} custom-call(bf16[2,32,1024]{2,1,0:T(8,128)(2,1)} %factors_ref.1), custom_call_target="tpu_custom_call" | custom-call | tf_op jit(solution)/shard_map/pallas_call | solution.py:40
  1.6 8.8 %collective-permute-start = (bf16[64,32,512]{2,1,0:T(8,128)(2,1)}, bf16[64,32,512]{2,1,0:T(8,128)(2,1)S(1)}, u32[]{:S(2)}, u32[]{:S(2)}) collective-permute-start(bf16[64,32,512]{2,1,0:T(8,128)(2,1)} %param.7), channel_id=1, source_target_pairs={{0,1},{1,0},{2,3},{3,2},{4,5},{5,4},{6,7},{7,6},{8,9},{9,8},{10,11... | collective-permute-start | bytes 6291464 | tf_op jit(solution)/shard_map/ppermute | solution.py:259
  10.4 3.4 %all-to-all-start = ((bf16[16,64,128]{2,1,0:T(8,128)(2,1)}), bf16[16,64,128]{2,1,0:T(8,128)(2,1)S(1)}, u32[]{:S(2)}, u32[]{:S(2)}) async-start(bf16[16,64,128]{2,1,0:T(8,128)(2,1)} %shard_map.64), calls=%async_computation | async-start | bytes 524288 | tf_op jit(solution)/shard_map/all_to_all | solution.py:258
  13.9 0.7 multiply_add_fusion
  14.5 0.1 eq.87
  14.6 0.7 tile.4
  15.3 0.1 eq.43
  15.4 4.1 %copy.9 = bf16[32,64,512]{2,1,0:T(8,128)(2,1)} copy(bf16[32,64,512]{2,0,1:T(8,128)(2,1)} %bitcast.14) | data formatting | bytes 4194304 | tf_op jit(solution)/shard_map/transpose | solution.py:261
  19.5 0.1 pad_add_fusion.where_ref
  19.6 0.1 and_convert_fusion.pairing_ref
  19.7 0.0 collective-permute-done
  19.7 2.5 %copy.10 = bf16[32,64,512]{2,1,0:T(8,128)(2,1)} copy(bf16[32,64,512]{2,0,1:T(8,128)(2,1)S(1)} %bitcast.16) | data formatting | bytes 4194304 | tf_op jit(solution)/shard_map/transpose | solution.py:261
  22.2 0.0 copy-start
  22.2 0.0 copy-start.1
  22.2 3.4 %all-to-all-done.r0_ref.rows_ref = bf16[16,64,128]{2,1,0:T(8,128)(2,1)S(1)} async-done(((bf16[16,64,128]{2,1,0:T(8,128)(2,1)}), bf16[16,64,128]{2,1,0:T(8,128)(2,1)S(1)}, u32[]{:S(2)}, u32[]{:S(2)}) %all-to-all-start) | async-done | bytes 262176 | tf_op jit(solution)/shard_map/all_to_all | solution.py:258
  25.6 1.7 %shard_map.66 = bf16[8,8,64,128]{3,2,1,0:T(8,128)(2,1)} custom-call(s32[3]{0:T(128)S(1)} %pad_add_fusion.where_ref, bf16[16,64,128]{2,1,0:T(8,128)(2,1)S(1)} %all-to-all-done.r0_ref.rows_ref), custom_call_target="tpu_custom_call" | custom-call | tf_op jit(solution)/shard_map/pallas_call | solution.py:57
  27.3 8.4 %all-to-all-start.1 = ((bf16[8,512,128]{2,1,0:T(8,128)(2,1)}), bf16[8,512,128]{2,1,0:T(8,128)(2,1)S(1)}, u32[]{:S(2)}, u32[]{:S(2)}) async-start(bf16[8,512,128]{2,1,0:T(8,128)(2,1)} %bitcast.7), calls=%async_computation.1 | async-start | bytes 2097152 | tf_op jit(solution)/shard_map/all_to_all | solution.py:267
  35.7 4.6 %collective-permute-start.1 = (bf16[16,64,128]{2,1,0:T(8,128)(2,1)S(1)}, bf16[16,64,128]{2,1,0:T(8,128)(2,1)S(1)}, u32[]{:S(2)}, u32[]{:S(2)}) collective-permute-start(bf16[16,64,128]{2,1,0:T(8,128)(2,1)S(1)} %all-to-all-done.r0_ref.rows_ref), channel_id=1, source_target_pairs={{0,4},{2,6},{4,0},{6,2},{1,5},{3,7},{5,1},{7,3},{8,12},{10,14},{12... | collective-permute-start | bytes 786440 | tf_op jit(solution)/shard_map/ppermute | solution.py:269
  40.4 2.2 %collective-permute-start.2 = (bf16[16,64,128]{2,1,0:T(8,128)(2,1)S(1)}, bf16[16,64,128]{2,1,0:T(8,128)(2,1)S(1)}, u32[]{:S(2)}, u32[]{:S(2)}) collective-permute-start(bf16[16,64,128]{2,1,0:T(8,128)(2,1)S(1)} %all-to-all-done.r0_ref.rows_ref), channel_id=1, source_target_pairs={{0,2},{2,4},{4,6},{6,0},{1,3},{3,5},{5,7},{7,1},{8,10},{10,12},{12... | collective-permute-start | bytes 786440 | tf_op jit(solution)/shard_map/ppermute | solution.py:269
  42.6 4.3 %collective-permute-start.3 = (bf16[16,64,128]{2,1,0:T(8,128)(2,1)S(1)}, bf16[16,64,128]{2,1,0:T(8,128)(2,1)S(1)}, u32[]{:S(2)}, u32[]{:S(2)}) collective-permute-start(bf16[16,64,128]{2,1,0:T(8,128)(2,1)S(1)} %all-to-all-done.r0_ref.rows_ref), channel_id=1, source_target_pairs={{0,6},{2,0},{4,2},{6,4},{1,7},{3,1},{5,3},{7,5},{8,14},{10,8},{12,... | collective-permute-start | bytes 786440 | tf_op jit(solution)/shard_map/ppermute | solution.py:269
  46.9 0.0 copy-done
  46.9 0.0 copy-done.1
  46.9 0.2 select_reduce_fusion
  47.1 0.0 collective-permute-done.1.rt_ref
  47.1 5.9 %collective-permute-done.2.rp_ref = bf16[16,64,128]{2,1,0:T(8,128)(2,1)S(1)} collective-permute-done((bf16[16,64,128]{2,1,0:T(8,128)(2,1)S(1)}, bf16[16,64,128]{2,1,0:T(8,128)(2,1)S(1)}, u32[]{:S(2)}, u32[]{:S(2)}) %collective-permute-start.2) | collective-permute-done | bytes 262176 | tf_op jit(solution)/shard_map/ppermute | solution.py:269
  53.0 0.0 collective-permute-done.3.rm_ref
  53.0 7.9 %shard_map.65.prod_ref = bf16[4,512,2048]{2,1,0:T(8,128)(2,1)} custom-call(s32[3]{0:T(128)S(1)} %pad_add_fusion.where_ref, bf16[4,8,64,512]{3,2,1,0:T(8,128)(2,1)} %bitcast.15, bf16[4,8,64,512]{3,2,1,0:T(8,128)(2,1)} %bitcast.17, bf16[16,64,128]{2,1,0:T(8,128)(2,1)S(1)} %all-to-all-done.r0_ref.rows_ref, ...), custom_call_target="tpu_custom_call" | custom-call | flops 4294967296 | bytes 14680064 | tf_op jit(solution)/shard_map/pallas_call | solution.py:138
  60.9 4.2 %all-to-all-done.1 = bf16[8,512,128]{2,1,0:T(8,128)(2,1)S(1)} async-done(((bf16[8,512,128]{2,1,0:T(8,128)(2,1)}), bf16[8,512,128]{2,1,0:T(8,128)(2,1)S(1)}, u32[]{:S(2)}, u32[]{:S(2)}) %all-to-all-start.1) | async-done | bytes 1048608 | tf_op jit(solution)/shard_map/all_to_all | solution.py:267
  65.1 0.0 copy-start.2
  65.1 6.7 %shard_map.67 = (f32[256,128]{1,0:T(8,128)S(1)}, f32[256,128]{1,0:T(8,128)}) custom-call(bf16[4,512,2048]{2,1,0:T(8,128)(2,1)} %shard_map.65.prod_ref, bf16[4096,128]{1,0:T(8,128)(2,1)S(1)} %bitcast.12, bf16[128,128]{1,0:T(8,128)(2,1)S(1)} %and_convert_fusion.pairing_ref), custom_call_target="tpu_custom_call" | custom-call | flops 536870912 | bytes 9437184 | tf_op jit(solution)/shard_map/pallas_call | solution.py:203
  71.8 3.4 %all-to-all-start.2 = ((f32[8,32,128]{2,1,0:T(8,128)}), f32[8,32,128]{2,1,0:T(8,128)S(1)}, u32[]{:S(2)}, u32[]{:S(2)}) async-start(f32[8,32,128]{2,1,0:T(8,128)} %bitcast.10), calls=%async_computation.2 | async-start | bytes 262144 | tf_op jit(solution)/shard_map/all_to_all | solution.py:272
  75.2 0.0 copy-done.2
  75.2 0.2 select_reduce_fusion.3
  75.4 0.1 dynamic_slice.7
  75.4 0.1 dynamic_slice.6
  75.5 0.1 broadcast_add_fusion
  75.6 7.7 %all-to-all-done.2 = f32[8,32,128]{2,1,0:T(8,128)S(1)} async-done(((f32[8,32,128]{2,1,0:T(8,128)}), f32[8,32,128]{2,1,0:T(8,128)S(1)}, u32[]{:S(2)}, u32[]{:S(2)}) %all-to-all-start.2) | async-done | bytes 131104 | tf_op jit(solution)/shard_map/all_to_all | solution.py:272
  83.3 0.7 add.76
  83.9 8.2 %all-to-all-start.3 = ((f32[64,4,128]{2,1,0:T(4,128)}), f32[64,4,128]{2,1,0:T(4,128)S(1)}, u32[]{:S(2)}, u32[]{:S(2)}) async-start(f32[64,4,128]{2,1,0:T(4,128)} %bitcast.11), calls=%async_computation.3 | async-start | bytes 262144 | tf_op jit(solution)/shard_map/all_to_all | solution.py:274
  92.1 0.1 select_reduce_fusion.1
  92.2 0.1 sub.40
  92.3 0.1 sub.41
  92.4 0.1 sub.43
  92.5 11.1 %all-to-all-done.3.parts_ref = f32[64,4,128]{2,1,0:T(4,128)S(1)} async-done(((f32[64,4,128]{2,1,0:T(4,128)}), f32[64,4,128]{2,1,0:T(4,128)S(1)}, u32[]{:S(2)}, u32[]{:S(2)}) %all-to-all-start.3) | async-done | bytes 131104 | tf_op jit(solution)/shard_map/all_to_all | solution.py:274
  103.6 0.7 shard_map.68
  (6 shorter events, 0.0 us)
Async XLA Ops:
  1.6 18.0 %collective-permute-start = (bf16[64,32,512]{2,1,0:T(8,128)(2,1)}, bf16[64,32,512]{2,1,0:T(8,128)(2,1)S(1)}, u32[]{:S(2)}, u32[]{:S(2)}) collective-permute-start(bf16[64,32,512]{2,1,0:T(8,128)(2,1)} %param.7), channel_id=1, source_target_pairs={{0,1},{1,0},{2,3},{3,2},{4,5},{5,4},{6,7},{7,6},{8,9},{9,8},{10,11... | collective-permute-start | bytes 6291464 | tf_op jit(solution)/shard_map/ppermute | solution.py:259
  10.4 15.2 %all-to-all-start = ((bf16[16,64,128]{2,1,0:T(8,128)(2,1)}), bf16[16,64,128]{2,1,0:T(8,128)(2,1)S(1)}, u32[]{:S(2)}, u32[]{:S(2)}) async-start(bf16[16,64,128]{2,1,0:T(8,128)(2,1)} %shard_map.64), calls=%async_computation | async-start | bytes 524288 | tf_op jit(solution)/shard_map/all_to_all | solution.py:258
  22.2 24.7 %copy-start = (s32[64]{0:T(128)S(1)}, s32[64]{0:T(128)}, u32[]{:S(2)}) copy-start(s32[64]{0:T(128)} %param.10) | copy-start | bytes 772
  22.2 24.7 %copy-start.1 = (f32[128]{0:T(128)S(1)}, f32[128]{0:T(128)}, u32[]{:S(2)}) copy-start(f32[128]{0:T(128)} %param.11) | copy-start | bytes 1540
  27.3 37.8 %all-to-all-start.1 = ((bf16[8,512,128]{2,1,0:T(8,128)(2,1)}), bf16[8,512,128]{2,1,0:T(8,128)(2,1)S(1)}, u32[]{:S(2)}, u32[]{:S(2)}) async-start(bf16[8,512,128]{2,1,0:T(8,128)(2,1)} %bitcast.7), calls=%async_computation.1 | async-start | bytes 2097152 | tf_op jit(solution)/shard_map/all_to_all | solution.py:267
  35.7 11.4 %collective-permute-start.1 = (bf16[16,64,128]{2,1,0:T(8,128)(2,1)S(1)}, bf16[16,64,128]{2,1,0:T(8,128)(2,1)S(1)}, u32[]{:S(2)}, u32[]{:S(2)}) collective-permute-start(bf16[16,64,128]{2,1,0:T(8,128)(2,1)S(1)} %all-to-all-done.r0_ref.rows_ref), channel_id=1, source_target_pairs={{0,4},{2,6},{4,0},{6,2},{1,5},{3,7},{5,1},{7,3},{8,12},{10,14},{12... | collective-permute-start | bytes 786440 | tf_op jit(solution)/shard_map/ppermute | solution.py:269
  40.4 12.6 %collective-permute-start.2 = (bf16[16,64,128]{2,1,0:T(8,128)(2,1)S(1)}, bf16[16,64,128]{2,1,0:T(8,128)(2,1)S(1)}, u32[]{:S(2)}, u32[]{:S(2)}) collective-permute-start(bf16[16,64,128]{2,1,0:T(8,128)(2,1)S(1)} %all-to-all-done.r0_ref.rows_ref), channel_id=1, source_target_pairs={{0,2},{2,4},{4,6},{6,0},{1,3},{3,5},{5,7},{7,1},{8,10},{10,12},{12... | collective-permute-start | bytes 786440 | tf_op jit(solution)/shard_map/ppermute | solution.py:269
  42.6 10.4 %collective-permute-start.3 = (bf16[16,64,128]{2,1,0:T(8,128)(2,1)S(1)}, bf16[16,64,128]{2,1,0:T(8,128)(2,1)S(1)}, u32[]{:S(2)}, u32[]{:S(2)}) collective-permute-start(bf16[16,64,128]{2,1,0:T(8,128)(2,1)S(1)} %all-to-all-done.r0_ref.rows_ref), channel_id=1, source_target_pairs={{0,6},{2,0},{4,2},{6,4},{1,7},{3,1},{5,3},{7,5},{8,14},{10,8},{12,... | collective-permute-start | bytes 786440 | tf_op jit(solution)/shard_map/ppermute | solution.py:269
  65.1 10.1 %copy-start.2 = (s32[8]{0:T(128)S(1)}, s32[8]{0:T(128)}, u32[]{:S(2)}) copy-start(s32[8]{0:T(128)} %param.9) | copy-start | bytes 100
  71.8 11.5 %all-to-all-start.2 = ((f32[8,32,128]{2,1,0:T(8,128)}), f32[8,32,128]{2,1,0:T(8,128)S(1)}, u32[]{:S(2)}, u32[]{:S(2)}) async-start(f32[8,32,128]{2,1,0:T(8,128)} %bitcast.10), calls=%async_computation.2 | async-start | bytes 262144 | tf_op jit(solution)/shard_map/all_to_all | solution.py:272
  83.9 19.6 %all-to-all-start.3 = ((f32[64,4,128]{2,1,0:T(4,128)}), f32[64,4,128]{2,1,0:T(4,128)S(1)}, u32[]{:S(2)}, u32[]{:S(2)}) async-start(f32[64,4,128]{2,1,0:T(4,128)} %bitcast.11), calls=%async_computation.3 | async-start | bytes 262144 | tf_op jit(solution)/shard_map/all_to_all | solution.py:274

commit v9 on v5

--- a/solution.py
+++ b/solution.py
@@ -28,6 +28,46 @@
     )
 
 
+def spread_kernel(where_ref, rows_ref, out_ref, wide, tiles, packed, sem):
+    first = where_ref[2] * 8
+    for n in range(8):
+        wide[n * 64 : (n + 1) * 64, :] = rows_ref[first + n].astype(jnp.float32)
+    for dd in range(32):
+        for c in range(2):
+            tile = dd * 2 + c
+            for r in range(2):
+                tiles[pl.ds(tile * 8 + r, 4, stride=2), :] = wide[
+                    pl.ds(c * 64 + r * 32 + dd, 4, stride=128), :
+                ]
+            packed[:, tile * 128 : (tile + 1) * 128] = tiles[tile * 8 : (tile + 1) * 8, :].astype(
+                jnp.bfloat16
+            )
+    copies = [pltpu.make_async_copy(packed, out_ref.at[z], sem.at[z]) for z in range(8)]
+    for copy in copies:
+        copy.start()
+    for copy in copies:
+        copy.wait()
+
+
+def for_each_plane(where, rows):
+    return pl.pallas_call(
+        spread_kernel,
+        in_specs=[
+            pl.BlockSpec(memory_space=pltpu.SMEM),
+            pl.BlockSpec(memory_space=pltpu.VMEM),
+        ],
+        out_specs=pl.BlockSpec(memory_space=pl.ANY),
+        out_shape=jax.ShapeDtypeStruct((8, 8, 8192), jnp.bfloat16),
+        scratch_shapes=[
+            pltpu.VMEM((512, 128), jnp.float32),
+            pltpu.VMEM((512, 128), jnp.float32),
+            pltpu.VMEM((8, 8192), jnp.bfloat16),
+            pltpu.SemaphoreType.DMA((8,)),
+        ],
+        compiler_params=pltpu.CompilerParams(vmem_limit_bytes=8 * 1024 * 1024),
+    )(where, rows)
+
+
 def product_kernel(
     where_ref, own_ref, other_ref, r0_ref, rp_ref, rm_ref, rt_ref, out_ref, amps, bmat, prods, amps_sem, b_sem, out_sem
 ):
@@ -41,12 +81,17 @@
         ref, place = ((own_ref, c), (other_ref, 1 - c))[half]
         return pltpu.make_async_copy(ref.at[step], amps.at[place, step], amps_sem.at[half, step])
 
-    def store(step):
-        return pltpu.make_async_copy(prods.at[step], out_ref.at[step], out_sem.at[step])
-
+    def store(step, yl):
+        rows = pl.ds(yl * 128, 128)
+        return pltpu.make_async_copy(
+            prods.at[step, rows], out_ref.at[step, rows], out_sem.at[step, yl]
+        )
+
+    load(0, 0).start()
+    load(0, 1).start()
     for copy in rights:
         copy.start()
-    for step in range(STEPS):
+    for step in range(1, STEPS):
         load(step, 0).start()
         load(step, 1).start()
     for copy in rights:
@@ -79,12 +124,13 @@
                         prods[step, b * 64 : (b + 1) * 64, lane : lane + 128] = prod[
                             dd * 64 : (dd + 1) * 64, r * 128 : (r + 1) * 128
                         ]
-        store(step).start()
+            store(step, yl).start()
         return 0
 
     lax.fori_loop(0, STEPS, one_step, 0)
     for step in range(STEPS):
-        store(step).wait()
+        for yl in range(4):
+            store(step, yl).wait()
 
 
 def products(where, own, other, rights):
@@ -101,7 +147,7 @@
             pltpu.VMEM(shape, jnp.bfloat16),
             pltpu.SemaphoreType.DMA((2, STEPS)),
             pltpu.SemaphoreType.DMA((4,)),
-            pltpu.SemaphoreType.DMA((STEPS,)),
+            pltpu.SemaphoreType.DMA((STEPS, 4)),
         ],
         compiler_params=pltpu.CompilerParams(vmem_limit_bytes=VMEM_A * 1024 * 1024),
         cost_estimate=pl.CostEstimate(
@@ -110,35 +156,28 @@
     )(where, own, other, *rights)
 
 
-def ladder_kernel(prod_ref, left_ref, out_ref, prods, wide, lefts, sem):
+def ladder_kernel(prod_ref, left_ref, out_ref, prods, sem):
     copies = [
         pltpu.make_async_copy(prod_ref.at[step], prods.at[step], sem.at[step])
         for step in range(STEPS)
     ]
     for copy in copies:
         copy.start()
-    wide[...] = left_ref[...].astype(jnp.float32)
-    for step in range(STEPS):
-        for dd in range(DSTEP):
-            for cc in range(2):
-                lane = dd * 256 + cc * 128
-                for r in range(2):
-                    start = cc * 64 + r * 32 + step * DSTEP + dd
-                    lefts[step, r * 32 : (r + 1) * 32, lane : lane + 128] = wide[
-                        pl.ds(start, 32, stride=128), :
-                    ].astype(jnp.bfloat16)
     total = jnp.zeros((64, 512), jnp.float32)
+    width = DSTEP * 256
     for step in range(STEPS):
         copies[step].wait()
         total += lax.dot_general(
-            lefts[step], prods[step], (((1,), (1,)), ((), ())), preferred_element_type=jnp.float32
+            left_ref[:, step * width : (step + 1) * width],
+            prods[step],
+            (((1,), (1,)), ((), ())),
+            preferred_element_type=jnp.float32,
         )
     for yl in range(4):
-        for r in range(2):
-            for z in range(8):
-                out_ref[pl.ds(z * 32 + yl * 8 + r, 4, stride=2), :] = total[
-                    r * 32 + z * 4 : r * 32 + z * 4 + 4, yl * 128 : (yl + 1) * 128
-                ]
+        for z in range(8):
+            out_ref[z * 32 + yl * 8 : z * 32 + yl * 8 + 8, :] = total[
+                z * 8 : z * 8 + 8, yl * 128 : (yl + 1) * 128
+            ]
 
 
 def ladder_parts(prods, left):
@@ -152,8 +191,6 @@
         out_shape=jax.ShapeDtypeStruct((256, 128), jnp.float32),
         scratch_shapes=[
             pltpu.VMEM((STEPS, 512, DSTEP * 256), jnp.bfloat16),
-            pltpu.VMEM((4096, 128), jnp.float32),
-            pltpu.VMEM((STEPS, 64, DSTEP * 256), jnp.bfloat16),
             pltpu.SemaphoreType.DMA((STEPS,)),
         ],
         compiler_params=pltpu.CompilerParams(vmem_limit_bytes=VMEM_B * 1024 * 1024),
@@ -225,6 +262,7 @@
         + level_shift
     ).reshape(4, 128)
 
+    where = jnp.stack([lax.axis_index(n) for n in ("x", "c", "yh")]).astype(jnp.int32)
     eighths = factors.reshape(64, 8, 128).transpose(1, 0, 2)
     eighths = jnp.broadcast_to(eighths[None], (2, 8, 64, 128)).reshape(16, 64, 128)
     rows = lax.all_to_all(eighths, ("yh", "yl", "c"), 0, 0, tiled=True)
@@ -232,13 +270,10 @@
     amps, amps_other = (
         t.transpose(1, 0, 2).reshape(STEPS, DSTEP, 64, 512) for t in (amplitudes, other)
     )
-    own = lax.dynamic_slice_in_dim(rows, lax.axis_index("yh") * 8, 8)
-    own = jnp.broadcast_to(own.reshape(1, 512, 128), (8, 512, 128))
-    left = lax.all_to_all(own, "z", 0, 0, tiled=True).reshape(4096, 128)
+    left = lax.all_to_all(for_each_plane(where, rows), "z", 0, 0, tiled=True).reshape(64, 8192)
     rights = [rows] + [
         lax.ppermute(rows, "x", [(i, (i + s) % 4) for i in range(4)]) for s in (1, 3, 2)
     ]
-    where = jnp.stack([lax.axis_index("x"), lax.axis_index("c")]).astype(jnp.int32)
     ladder = ladder_parts(products(where, amps, amps_other, rights), left)
     crossed = lax.all_to_all(ladder.reshape(8, 32, 128), "z", 0, 0, tiled=True)
     parts = both_orders(ladder, crossed.reshape(256, 128), pairing)

time: 103 us -> 104 us (level)
  Pallas kernels: 15.7 us -> 17.2 us
  local copies, waits for them, and re-layouts: 7.34 us -> 6.16 us
    pallas_call x0 -> x1, Pallas kernels: none -> 1.93 us  [for_each_plane(): pl.pallas_call(spread_kernel, in_specs=[pl.BlockSpec(memory_space=pltpu.S...]
    broadcast_in_dim x1 -> x0, local copies, waits for them, and re-layouts: 1.18 us -> none  [per_device(): own = jnp.broadcast_to(own.reshape(1, 512, 128), (8, 512, 128))]
  transfers between devices with their start and end apart: 8 -> 8, of which waited for: 5 -> 5; matrix products, arithmetic and copies ran while one was open for 8% -> 7% of each run, Pallas kernels for 7% -> 9%
where the time goes in v9:
time: 104 us; the launch traced here: 103 us
  starting transfers between devices  41.4 us (40%)
  waiting for transfers between devices  37.3 us (36%)
  Pallas kernels  17.2 us (17%)
  local copies, waits for them, and re-layouts  6.16 us (6%)
    all_to_all x1, waiting for transfers between devices, per_device(): rows = lax.all_to_all(eighths, ('yh', 'yl', 'c'), 0, 0, tiled=True)  11.7 us
    all_to_all x1, waiting for transfers between devices, per_device(): parts = lax.all_to_all(parts, GROUP, 0, 0, tiled=True)  10.1 us
    ppermute x3, starting transfers between devices, per_device(): lax.ppermute(rows, 'x', [(i, (i + s) % 4) for i in range(4)])  9.93 us
    ppermute x1, starting transfers between devices, per_device(): other = lax.ppermute(amplitudes, 'c', [(0, 1), (1, 0)])  8.78 us
    all_to_all x1, starting transfers between devices, per_device(): lax.all_to_all(for_each_plane(where, rows), 'z', 0, 0, tiled=True)  8.42 us
    all_to_all x1, waiting for transfers between devices, per_device(): crossed = lax.all_to_all(ladder.reshape(8, 32, 128), 'z', 0, 0, tiled=True)  7.53 us
    all_to_all x1, starting transfers between devices, per_device(): parts = lax.all_to_all(parts, GROUP, 0, 0, tiled=True)  7.33 us
    pallas_call x1, Pallas kernels, products(): pl.pallas_call(product_kernel, in_specs=[pl.BlockSpec(memory_space=pltpu....  7.04 us
  transfers between devices with their start and end apart: 8, of which 5 were waited for; matrix products, arithmetic and copies ran while one was open for 7% of the time, Pallas kernels for 9%

profile of v9, /device:TPU:1, one launch (start us, length us, event | category | flops | bytes accessed | tf_op | source)
XLA Modules:
  0.0 103.1 jit_solution(2909817976751708510)
XLA Ops:
  0.0 8.8 %collective-permute-start = (bf16[64,32,512]{2,1,0:T(8,128)(2,1)}, bf16[64,32,512]{2,1,0:T(8,128)(2,1)}, u32[]{:S(2)}, u32[]{:S(2)}) collective-permute-start(bf16[64,32,512]{2,1,0:T(8,128)(2,1)} %param.7), channel_id=1, source_target_pairs={{0,1},{1,0},{2,3},{3,2},{4,5},{5,4},{6,7},{7,6},{8,9},{9,8},{10,11... | collective-permute-start | bytes 6291464 | tf_op jit(solution)/shard_map/ppermute | solution.py:269
  8.8 0.9 copy.13
  9.7 0.0 copy-start.2
  9.8 0.0 copy-start.3
  9.8 0.0 copy-start.1
  9.8 0.7 broadcast_in_dim.46
  10.5 0.0 copy-start
  10.5 3.6 %all-to-all-start = ((bf16[16,64,128]{2,1,0:T(8,128)(2,1)}), bf16[16,64,128]{2,1,0:T(8,128)(2,1)S(1)}, u32[]{:S(2)}, u32[]{:S(2)}) async-start(bf16[16,64,128]{2,1,0:T(8,128)(2,1)} %bitcast.8), calls=%async_computation | async-start | bytes 524288 | tf_op jit(solution)/shard_map/all_to_all | solution.py:268
  14.1 0.1 pad_add_fusion.where_ref
  14.2 11.7 %all-to-all-done.r0_ref.rows_ref = bf16[16,64,128]{2,1,0:T(8,128)(2,1)S(1)} async-done(((bf16[16,64,128]{2,1,0:T(8,128)(2,1)}), bf16[16,64,128]{2,1,0:T(8,128)(2,1)S(1)}, u32[]{:S(2)}, u32[]{:S(2)}) %all-to-all-start) | async-done | bytes 262176 | tf_op jit(solution)/shard_map/all_to_all | solution.py:268
  25.8 1.9 %shard_map.65 = bf16[8,8,8192]{2,1,0:T(8,128)(2,1)} custom-call(s32[3]{0:T(128)S(1)} %pad_add_fusion.where_ref, bf16[16,64,128]{2,1,0:T(8,128)(2,1)S(1)} %all-to-all-done.r0_ref.rows_ref), custom_call_target="tpu_custom_call" | custom-call | tf_op jit(solution)/shard_map/pallas_call | solution.py:53
  27.8 8.4 %all-to-all-start.1 = ((bf16[8,8,8192]{2,1,0:T(8,128)(2,1)}), bf16[8,8,8192]{2,1,0:T(8,128)(2,1)S(1)}, u32[]{:S(2)}, u32[]{:S(2)}) async-start(bf16[8,8,8192]{2,1,0:T(8,128)(2,1)} %shard_map.65), calls=%async_computation.1 | async-start | bytes 2097152 | tf_op jit(solution)/shard_map/all_to_all | solution.py:273
  36.2 0.0 copy-done.2
  36.2 0.0 copy-done.3
  36.2 0.2 select_reduce_fusion
  36.4 0.0 copy-done.1
  36.4 0.1 compare_convert_fusion
  36.5 3.1 %collective-permute-start.1 = (bf16[16,64,128]{2,1,0:T(8,128)(2,1)S(1)}, bf16[16,64,128]{2,1,0:T(8,128)(2,1)S(1)}, u32[]{:S(2)}, u32[]{:S(2)}) collective-permute-start(bf16[16,64,128]{2,1,0:T(8,128)(2,1)S(1)} %all-to-all-done.r0_ref.rows_ref), channel_id=1, source_target_pairs={{0,2},{2,4},{4,6},{6,0},{1,3},{3,5},{5,7},{7,1},{8,10},{10,12},{12... | collective-permute-start | bytes 786440 | tf_op jit(solution)/shard_map/ppermute | solution.py:275
  39.6 3.4 %collective-permute-start.2 = (bf16[16,64,128]{2,1,0:T(8,128)(2,1)S(1)}, bf16[16,64,128]{2,1,0:T(8,128)(2,1)S(1)}, u32[]{:S(2)}, u32[]{:S(2)}) collective-permute-start(bf16[16,64,128]{2,1,0:T(8,128)(2,1)S(1)} %all-to-all-done.r0_ref.rows_ref), channel_id=1, source_target_pairs={{0,6},{2,0},{4,2},{6,4},{1,7},{3,1},{5,3},{7,5},{8,14},{10,8},{12,... | collective-permute-start | bytes 786440 | tf_op jit(solution)/shard_map/ppermute | solution.py:275
  43.0 3.4 %collective-permute-start.3 = (bf16[16,64,128]{2,1,0:T(8,128)(2,1)S(1)}, bf16[16,64,128]{2,1,0:T(8,128)(2,1)S(1)}, u32[]{:S(2)}, u32[]{:S(2)}) collective-permute-start(bf16[16,64,128]{2,1,0:T(8,128)(2,1)S(1)} %all-to-all-done.r0_ref.rows_ref), channel_id=1, source_target_pairs={{0,4},{2,6},{4,0},{6,2},{1,5},{3,7},{5,1},{7,3},{8,12},{10,14},{12... | collective-permute-start | bytes 786440 | tf_op jit(solution)/shard_map/ppermute | solution.py:275
  46.5 0.0 copy-done
  46.5 1.2 %copy.10 = bf16[32,64,512]{2,1,0:T(8,128)(2,1)S(1)} copy(bf16[32,64,512]{2,0,1:T(8,128)(2,1)S(1)} %bitcast.20) | data formatting | bytes 4194304 | tf_op jit(solution)/shard_map/transpose | solution.py:271
  47.6 0.1 broadcast_multiply_fusion
  47.8 0.0 collective-permute-done
  47.8 2.8 %copy.11 = bf16[32,64,512]{2,1,0:T(8,128)(2,1)S(1)} copy(bf16[32,64,512]{2,0,1:T(8,128)(2,1)} %bitcast.5) | data formatting | bytes 4194304 | tf_op jit(solution)/shard_map/transpose | solution.py:271
  50.5 0.0 collective-permute-done.1.rp_ref
  50.5 0.0 collective-permute-done.2.rm_ref
  50.5 3.3 %collective-permute-done.3.rt_ref = bf16[16,64,128]{2,1,0:T(8,128)(2,1)S(1)} collective-permute-done((bf16[16,64,128]{2,1,0:T(8,128)(2,1)S(1)}, bf16[16,64,128]{2,1,0:T(8,128)(2,1)S(1)}, u32[]{:S(2)}, u32[]{:S(2)}) %collective-permute-start.3) | collective-permute-done | bytes 262176 | tf_op jit(solution)/shard_map/ppermute | solution.py:275
  53.9 7.0 %shard_map.64.prod_ref = bf16[4,512,2048]{2,1,0:T(8,128)(2,1)} custom-call(s32[3]{0:T(128)S(1)} %pad_add_fusion.where_ref, bf16[4,8,64,512]{3,2,1,0:T(8,128)(2,1)S(1)} %bitcast.17, bf16[4,8,64,512]{3,2,1,0:T(8,128)(2,1)S(1)} %bitcast.18, bf16[16,64,128]{2,1,0:T(8,128)(2,1)S(1)} %all-to-all-done.r0_ref.rows_ref, ...), custom_call_target="tpu_custom_call" | custom-call | flops 4294967296 | bytes 14680064 | tf_op jit(solution)/shard_map/pallas_call | solution.py:139
  60.9 4.7 %all-to-all-done.1 = bf16[8,8,8192]{2,1,0:T(8,128)(2,1)S(1)} async-done(((bf16[8,8,8192]{2,1,0:T(8,128)(2,1)}), bf16[8,8,8192]{2,1,0:T(8,128)(2,1)S(1)}, u32[]{:S(2)}, u32[]{:S(2)}) %all-to-all-start.1) | async-done | bytes 1048608 | tf_op jit(solution)/shard_map/all_to_all | solution.py:273
  65.6 0.0 copy-start.4
  65.6 5.6 %shard_map.66.own_ref = f32[256,128]{1,0:T(8,128)} custom-call(bf16[4,512,2048]{2,1,0:T(8,128)(2,1)} %shard_map.64.prod_ref, bf16[64,8192]{1,0:T(8,128)(2,1)S(1)} %bitcast.16), custom_call_target="tpu_custom_call" | custom-call | flops 536870912 | bytes 9437184 | tf_op jit(solution)/shard_map/pallas_call | solution.py:184
  71.2 3.4 %all-to-all-start.2 = ((f32[8,32,128]{2,1,0:T(8,128)}), f32[8,32,128]{2,1,0:T(8,128)S(1)}, u32[]{:S(2)}, u32[]{:S(2)}) async-start(f32[8,32,128]{2,1,0:T(8,128)} %bitcast.10), calls=%async_computation.2 | async-start | bytes 262144 | tf_op jit(solution)/shard_map/all_to_all | solution.py:278
  74.5 0.0 copy-done.4
  74.5 0.2 select_reduce_fusion.3
  74.7 0.1 mul.47.pairing_ref
  74.9 0.1 dynamic_slice.7
  74.9 0.1 dynamic_slice.6
  75.0 0.1 broadcast_add_fusion
  75.1 7.5 %all-to-all-done.2 = f32[8,32,128]{2,1,0:T(8,128)S(1)} async-done(((f32[8,32,128]{2,1,0:T(8,128)}), f32[8,32,128]{2,1,0:T(8,128)S(1)}, u32[]{:S(2)}, u32[]{:S(2)}) %all-to-all-start.2) | async-done | bytes 131104 | tf_op jit(solution)/shard_map/all_to_all | solution.py:278
  82.6 2.0 %shard_map.67 = f32[64,4,128]{2,1,0:T(4,128)} custom-call(f32[256,128]{1,0:T(8,128)} %shard_map.66.own_ref, f32[256,128]{1,0:T(8,128)S(1)} %bitcast.19, f32[128,128]{1,0:T(8,128)S(1)} %mul.47.pairing_ref), custom_call_target="tpu_custom_call" | custom-call | tf_op jit(solution)/shard_map/pallas_call | solution.py:224
  84.6 7.3 %all-to-all-start.3 = ((f32[64,4,128]{2,1,0:T(4,128)}), f32[64,4,128]{2,1,0:T(4,128)S(1)}, u32[]{:S(2)}, u32[]{:S(2)}) async-start(f32[64,4,128]{2,1,0:T(4,128)} %shard_map.67), calls=%async_computation.3 | async-start | bytes 262144 | tf_op jit(solution)/shard_map/all_to_all | solution.py:280
  91.9 0.1 select_reduce_fusion.1
  92.0 0.1 sub.29
  92.1 0.1 sub.30
  92.2 0.1 sub.32
  92.3 10.1 %all-to-all-done.3.parts_ref = f32[64,4,128]{2,1,0:T(4,128)S(1)} async-done(((f32[64,4,128]{2,1,0:T(4,128)}), f32[64,4,128]{2,1,0:T(4,128)S(1)}, u32[]{:S(2)}, u32[]{:S(2)}) %all-to-all-start.3) | async-done | bytes 131104 | tf_op jit(solution)/shard_map/all_to_all | solution.py:280
  102.3 0.7 shard_map.68
  (7 shorter events, 0.1 us)
Async XLA Ops:
  0.0 47.8 %collective-permute-start = (bf16[64,32,512]{2,1,0:T(8,128)(2,1)}, bf16[64,32,512]{2,1,0:T(8,128)(2,1)}, u32[]{:S(2)}, u32[]{:S(2)}) collective-permute-start(bf16[64,32,512]{2,1,0:T(8,128)(2,1)} %param.7), channel_id=1, source_target_pairs={{0,1},{1,0},{2,3},{3,2},{4,5},{5,4},{6,7},{7,6},{8,9},{9,8},{10,11... | collective-permute-start | bytes 6291464 | tf_op jit(solution)/shard_map/ppermute | solution.py:269
  9.7 26.5 %copy-start.2 = (s32[64]{0:T(128)S(1)}, s32[64]{0:T(128)}, u32[]{:S(2)}) copy-start(s32[64]{0:T(128)} %param.10) | copy-start | bytes 772
  9.8 26.5 %copy-start.3 = (f32[128]{0:T(128)S(1)}, f32[128]{0:T(128)}, u32[]{:S(2)}) copy-start(f32[128]{0:T(128)} %param.11) | copy-start | bytes 1540
  9.8 26.6 %copy-start.1 = (s32[64]{0:T(128)S(1)}, s32[64]{0:T(128)}, u32[]{:S(2)}) copy-start(s32[64]{0:T(128)} %param.8) | copy-start | bytes 772
  10.5 35.9 %copy-start = (bf16[64,32,512]{2,1,0:T(8,128)(2,1)S(1)}, bf16[64,32,512]{2,1,0:T(8,128)(2,1)}, u32[]{:S(2)}) copy-start(bf16[64,32,512]{2,1,0:T(8,128)(2,1)} %param.7) | copy-start | bytes 6291460
  10.5 15.3 %all-to-all-start = ((bf16[16,64,128]{2,1,0:T(8,128)(2,1)}), bf16[16,64,128]{2,1,0:T(8,128)(2,1)S(1)}, u32[]{:S(2)}, u32[]{:S(2)}) async-start(bf16[16,64,128]{2,1,0:T(8,128)(2,1)} %bitcast.8), calls=%async_computation | async-start | bytes 524288 | tf_op jit(solution)/shard_map/all_to_all | solution.py:268
  27.8 37.8 %all-to-all-start.1 = ((bf16[8,8,8192]{2,1,0:T(8,128)(2,1)}), bf16[8,8,8192]{2,1,0:T(8,128)(2,1)S(1)}, u32[]{:S(2)}, u32[]{:S(2)}) async-start(bf16[8,8,8192]{2,1,0:T(8,128)(2,1)} %shard_map.65), calls=%async_computation.1 | async-start | bytes 2097152 | tf_op jit(solution)/shard_map/all_to_all | solution.py:273
  36.5 14.0 %collective-permute-start.1 = (bf16[16,64,128]{2,1,0:T(8,128)(2,1)S(1)}, bf16[16,64,128]{2,1,0:T(8,128)(2,1)S(1)}, u32[]{:S(2)}, u32[]{:S(2)}) collective-permute-start(bf16[16,64,128]{2,1,0:T(8,128)(2,1)S(1)} %all-to-all-done.r0_ref.rows_ref), channel_id=1, source_target_pairs={{0,2},{2,4},{4,6},{6,0},{1,3},{3,5},{5,7},{7,1},{8,10},{10,12},{12... | collective-permute-start | bytes 786440 | tf_op jit(solution)/shard_map/ppermute | solution.py:275
  39.6 10.9 %collective-permute-start.2 = (bf16[16,64,128]{2,1,0:T(8,128)(2,1)S(1)}, bf16[16,64,128]{2,1,0:T(8,128)(2,1)S(1)}, u32[]{:S(2)}, u32[]{:S(2)}) collective-permute-start(bf16[16,64,128]{2,1,0:T(8,128)(2,1)S(1)} %all-to-all-done.r0_ref.rows_ref), channel_id=1, source_target_pairs={{0,6},{2,0},{4,2},{6,4},{1,7},{3,1},{5,3},{7,5},{8,14},{10,8},{12,... | collective-permute-start | bytes 786440 | tf_op jit(solution)/shard_map/ppermute | solution.py:275
  43.0 10.9 %collective-permute-start.3 = (bf16[16,64,128]{2,1,0:T(8,128)(2,1)S(1)}, bf16[16,64,128]{2,1,0:T(8,128)(2,1)S(1)}, u32[]{:S(2)}, u32[]{:S(2)}) collective-permute-start(bf16[16,64,128]{2,1,0:T(8,128)(2,1)S(1)} %all-to-all-done.r0_ref.rows_ref), channel_id=1, source_target_pairs={{0,4},{2,6},{4,0},{6,2},{1,5},{3,7},{5,1},{7,3},{8,12},{10,14},{12... | collective-permute-start | bytes 786440 | tf_op jit(solution)/shard_map/ppermute | solution.py:275
  65.6 9.0 %copy-start.4 = (s32[8]{0:T(128)S(1)}, s32[8]{0:T(128)}, u32[]{:S(2)}) copy-start(s32[8]{0:T(128)} %param.9) | copy-start | bytes 100
  71.2 11.5 %all-to-all-start.2 = ((f32[8,32,128]{2,1,0:T(8,128)}), f32[8,32,128]{2,1,0:T(8,128)S(1)}, u32[]{:S(2)}, u32[]{:S(2)}) async-start(f32[8,32,128]{2,1,0:T(8,128)} %bitcast.10), calls=%async_computation.2 | async-start | bytes 262144 | tf_op jit(solution)/shard_map/all_to_all | solution.py:278
  84.6 17.8 %all-to-all-start.3 = ((f32[64,4,128]{2,1,0:T(4,128)}), f32[64,4,128]{2,1,0:T(4,128)S(1)}, u32[]{:S(2)}, u32[]{:S(2)}) async-start(f32[64,4,128]{2,1,0:T(4,128)} %shard_map.67), calls=%async_computation.3 | async-start | bytes 262144 | tf_op jit(solution)/shard_map/all_to_all | solution.py:280

commit v10 on v9

--- a/solution.py
+++ b/solution.py
@@ -69,7 +69,7 @@
 
 
 def product_kernel(
-    where_ref, own_ref, other_ref, r0_ref, rp_ref, rm_ref, rt_ref, out_ref, amps, bmat, prods, amps_sem, b_sem, out_sem
+    where_ref, own_ref, other_ref, r0_ref, rp_ref, rm_ref, rt_ref, near_ref, out_ref, amps, bmat, prods, amps_sem, b_sem, out_sem
 ):
     x, c = where_ref[0], where_ref[1]
     rights = [
@@ -87,17 +87,17 @@
             prods.at[step, rows], out_ref.at[step, rows], out_sem.at[step, yl]
         )
 
-    load(0, 0).start()
-    load(0, 1).start()
+    load(1, 0).start()
+    load(1, 1).start()
     for copy in rights:
         copy.start()
-    for step in range(1, STEPS):
+    for step in (2, 3, 0):
         load(step, 0).start()
         load(step, 1).start()
     for copy in rights:
         copy.wait()
 
-    def one_step(step, _):
+    def one_step(step, target, finish):
         load(step, 0).wait()
         load(step, 1).wait()
         for yl in range(4):
@@ -121,33 +121,40 @@
                     lane = dd * 256 + cc * 128
                     for r in range(2):
                         b = yl * 2 + r
-                        prods[step, b * 64 : (b + 1) * 64, lane : lane + 128] = prod[
+                        target[b * 64 : (b + 1) * 64, lane : lane + 128] = prod[
                             dd * 64 : (dd + 1) * 64, r * 128 : (r + 1) * 128
                         ]
-            store(step, yl).start()
+            finish(yl)
+
+    def later(n, _):
+        one_step(n + 1, prods.at[n], lambda yl: store(n, yl).start())
         return 0
 
-    lax.fori_loop(0, STEPS, one_step, 0)
-    for step in range(STEPS):
+    lax.fori_loop(0, STEPS - 1, later, 0)
+    one_step(0, near_ref, lambda yl: None)
+    for n in range(STEPS - 1):
         for yl in range(4):
-            store(step, yl).wait()
+            store(n, yl).wait()
 
 
 def products(where, own, other, rights):
     anywhere = pl.BlockSpec(memory_space=pl.ANY)
-    shape = (STEPS, 512, DSTEP * 256)
+    shape = (STEPS - 1, 512, DSTEP * 256)
     return pl.pallas_call(
         product_kernel,
         in_specs=[pl.BlockSpec(memory_space=pltpu.SMEM)] + [anywhere] * 6,
-        out_specs=pl.BlockSpec(memory_space=pltpu.HBM),
-        out_shape=pltpu.HBM(shape, jnp.bfloat16),
+        out_specs=[pl.BlockSpec(memory_space=pltpu.VMEM), pl.BlockSpec(memory_space=pltpu.HBM)],
+        out_shape=[
+            jax.ShapeDtypeStruct(shape[1:], jnp.bfloat16),
+            pltpu.HBM(shape, jnp.bfloat16),
+        ],
         scratch_shapes=[
             pltpu.VMEM((2, STEPS, DSTEP, 64, 512), jnp.bfloat16),
             pltpu.VMEM((4, 16, 64, 128), jnp.bfloat16),
             pltpu.VMEM(shape, jnp.bfloat16),
             pltpu.SemaphoreType.DMA((2, STEPS)),
             pltpu.SemaphoreType.DMA((4,)),
-            pltpu.SemaphoreType.DMA((STEPS, 4)),
+            pltpu.SemaphoreType.DMA((STEPS - 1, 4)),
         ],
         compiler_params=pltpu.CompilerParams(vmem_limit_bytes=VMEM_A * 1024 * 1024),
         cost_estimate=pl.CostEstimate(
@@ -156,20 +163,20 @@
     )(where, own, other, *rights)
 
 
-def ladder_kernel(prod_ref, left_ref, out_ref, prods, sem):
+def ladder_kernel(near_ref, prod_ref, left_ref, out_ref, prods, sem):
     copies = [
-        pltpu.make_async_copy(prod_ref.at[step], prods.at[step], sem.at[step])
-        for step in range(STEPS)
+        pltpu.make_async_copy(prod_ref.at[n], prods.at[n], sem.at[n]) for n in range(STEPS - 1)
     ]
     for copy in copies:
         copy.start()
     total = jnp.zeros((64, 512), jnp.float32)
     width = DSTEP * 256
     for step in range(STEPS):
-        copies[step].wait()
+        if step > 0:
+            copies[step - 1].wait()
         total += lax.dot_general(
             left_ref[:, step * width : (step + 1) * width],
-            prods[step],
+            near_ref[...] if step == 0 else prods[step - 1],
             (((1,), (1,)), ((), ())),
             preferred_element_type=jnp.float32,
         )
@@ -180,24 +187,25 @@
             ]
 
 
-def ladder_parts(prods, left):
+def ladder_parts(near, prods, left):
     return pl.pallas_call(
         ladder_kernel,
         in_specs=[
+            pl.BlockSpec(memory_space=pltpu.VMEM),
             pl.BlockSpec(memory_space=pltpu.HBM),
             pl.BlockSpec(memory_space=pltpu.VMEM),
         ],
         out_specs=pl.BlockSpec(memory_space=pltpu.VMEM),
         out_shape=jax.ShapeDtypeStruct((256, 128), jnp.float32),
         scratch_shapes=[
-            pltpu.VMEM((STEPS, 512, DSTEP * 256), jnp.bfloat16),
-            pltpu.SemaphoreType.DMA((STEPS,)),
+            pltpu.VMEM((STEPS - 1, 512, DSTEP * 256), jnp.bfloat16),
+            pltpu.SemaphoreType.DMA((STEPS - 1,)),
         ],
         compiler_params=pltpu.CompilerParams(vmem_limit_bytes=VMEM_B * 1024 * 1024),
         cost_estimate=pl.CostEstimate(
             flops=2 * 64 * 64 * 8 * 8192, bytes_accessed=9 * 1024 * 1024, transcendentals=0
         ),
-    )(prods, left)
+    )(near, prods, left)
 
 
 def both_kernel(own_ref, crossed_ref, pairing_ref, out_ref, turned):
@@ -274,7 +282,7 @@
     rights = [rows] + [
         lax.ppermute(rows, "x", [(i, (i + s) % 4) for i in range(4)]) for s in (1, 3, 2)
     ]
-    ladder = ladder_parts(products(where, amps, amps_other, rights), left)
+    ladder = ladder_parts(*products(where, amps, amps_other, rights), left)
     crossed = lax.all_to_all(ladder.reshape(8, 32, 128), "z", 0, 0, tiled=True)
     parts = both_orders(ladder, crossed.reshape(256, 128), pairing)
     parts = lax.all_to_all(parts, GROUP, 0, 0, tiled=True)

time: 104 us -> 103 us (level)
  Pallas kernels: 17.2 us -> 15.7 us
  transfers between devices with their start and end apart: 8 -> 8, of which waited for: 5 -> 5; matrix products, arithmetic and copies ran while one was open for 7% -> 7% of each run, Pallas kernels for 9% -> 8%
where the time goes in v10:
time: 103 us; the launch traced here: 102 us
  starting transfers between devices  41.3 us (40%)
  waiting for transfers between devices  37.6 us (37%)
  Pallas kernels  15.7 us (15%)
  local copies, waits for them, and re-layouts  6.16 us (6%)
  other arithmetic  1.28 us (1%)
    all_to_all x1, waiting for transfers between devices, per_device(): rows = lax.all_to_all(eighths, ('yh', 'yl', 'c'), 0, 0, tiled=True)  11.7 us
    all_to_all x1, waiting for transfers between devices, per_device(): parts = lax.all_to_all(parts, GROUP, 0, 0, tiled=True)  10.1 us
    ppermute x3, starting transfers between devices, per_device(): lax.ppermute(rows, 'x', [(i, (i + s) % 4) for i in range(4)])  9.93 us
    ppermute x1, starting transfers between devices, per_device(): other = lax.ppermute(amplitudes, 'c', [(0, 1), (1, 0)])  8.78 us
    all_to_all x1, starting transfers between devices, per_device(): lax.all_to_all(for_each_plane(where, rows), 'z', 0, 0, tiled=True)  8.42 us
    all_to_all x1, waiting for transfers between devices, per_device(): crossed = lax.all_to_all(ladder.reshape(8, 32, 128), 'z', 0, 0, tiled=True)  7.53 us
    all_to_all x1, starting transfers between devices, per_device(): parts = lax.all_to_all(parts, GROUP, 0, 0, tiled=True)  7.23 us
    pallas_call x1, Pallas kernels, products(): pl.pallas_call(product_kernel, in_specs=[pl.BlockSpec(memory_space=pltpu....  6.19 us
  transfers between devices with their start and end apart: 8, of which 5 were waited for; matrix products, arithmetic and copies ran while one was open for 7% of the time, Pallas kernels for 8%

profile of v10, /device:TPU:1, one launch (start us, length us, event | category | flops | bytes accessed | tf_op | source)
XLA Modules:
  0.0 102.3 jit_solution(2367292659000455511)
XLA Ops:
  0.0 8.8 %collective-permute-start = (bf16[64,32,512]{2,1,0:T(8,128)(2,1)}, bf16[64,32,512]{2,1,0:T(8,128)(2,1)}, u32[]{:S(2)}, u32[]{:S(2)}) collective-permute-start(bf16[64,32,512]{2,1,0:T(8,128)(2,1)} %param.7), channel_id=1, source_target_pairs={{0,1},{1,0},{2,3},{3,2},{4,5},{5,4},{6,7},{7,6},{8,9},{9,8},{10,11... | collective-permute-start | bytes 6291464 | tf_op jit(solution)/shard_map/ppermute | solution.py:277
  8.8 0.9 copy.13
  9.7 0.0 copy-start.2
  9.8 0.0 copy-start.3
  9.8 0.0 copy-start.1
  9.8 0.8 broadcast_in_dim.46
  10.5 0.0 copy-start
  10.5 3.6 %all-to-all-start = ((bf16[16,64,128]{2,1,0:T(8,128)(2,1)}), bf16[16,64,128]{2,1,0:T(8,128)(2,1)S(1)}, u32[]{:S(2)}, u32[]{:S(2)}) async-start(bf16[16,64,128]{2,1,0:T(8,128)(2,1)} %bitcast.8), calls=%async_computation | async-start | bytes 524288 | tf_op jit(solution)/shard_map/all_to_all | solution.py:276
  14.1 0.1 pad_add_fusion.where_ref
  14.2 11.7 %all-to-all-done.r0_ref.rows_ref = bf16[16,64,128]{2,1,0:T(8,128)(2,1)S(1)} async-done(((bf16[16,64,128]{2,1,0:T(8,128)(2,1)}), bf16[16,64,128]{2,1,0:T(8,128)(2,1)S(1)}, u32[]{:S(2)}, u32[]{:S(2)}) %all-to-all-start) | async-done | bytes 262176 | tf_op jit(solution)/shard_map/all_to_all | solution.py:276
  25.9 1.9 %shard_map.65 = bf16[8,8,8192]{2,1,0:T(8,128)(2,1)} custom-call(s32[3]{0:T(128)S(1)} %pad_add_fusion.where_ref, bf16[16,64,128]{2,1,0:T(8,128)(2,1)S(1)} %all-to-all-done.r0_ref.rows_ref), custom_call_target="tpu_custom_call" | custom-call | tf_op jit(solution)/shard_map/pallas_call | solution.py:53
  27.7 8.4 %all-to-all-start.1 = ((bf16[8,8,8192]{2,1,0:T(8,128)(2,1)}), bf16[8,8,8192]{2,1,0:T(8,128)(2,1)S(1)}, u32[]{:S(2)}, u32[]{:S(2)}) async-start(bf16[8,8,8192]{2,1,0:T(8,128)(2,1)} %shard_map.65), calls=%async_computation.1 | async-start | bytes 2097152 | tf_op jit(solution)/shard_map/all_to_all | solution.py:281
  36.2 0.0 copy-done.2
  36.2 0.0 copy-done.3
  36.2 0.7 select_reduce_fusion
  36.8 0.0 copy-done.1
  36.8 0.1 compare_convert_fusion
  36.9 3.1 %collective-permute-start.1 = (bf16[16,64,128]{2,1,0:T(8,128)(2,1)S(1)}, bf16[16,64,128]{2,1,0:T(8,128)(2,1)S(1)}, u32[]{:S(2)}, u32[]{:S(2)}) collective-permute-start(bf16[16,64,128]{2,1,0:T(8,128)(2,1)S(1)} %all-to-all-done.r0_ref.rows_ref), channel_id=1, source_target_pairs={{0,2},{2,4},{4,6},{6,0},{1,3},{3,5},{5,7},{7,1},{8,10},{10,12},{12... | collective-permute-start | bytes 786440 | tf_op jit(solution)/shard_map/ppermute | solution.py:283
  40.0 3.4 %collective-permute-start.2 = (bf16[16,64,128]{2,1,0:T(8,128)(2,1)S(1)}, bf16[16,64,128]{2,1,0:T(8,128)(2,1)S(1)}, u32[]{:S(2)}, u32[]{:S(2)}) collective-permute-start(bf16[16,64,128]{2,1,0:T(8,128)(2,1)S(1)} %all-to-all-done.r0_ref.rows_ref), channel_id=1, source_target_pairs={{0,6},{2,0},{4,2},{6,4},{1,7},{3,1},{5,3},{7,5},{8,14},{10,8},{12,... | collective-permute-start | bytes 786440 | tf_op jit(solution)/shard_map/ppermute | solution.py:283
  43.4 3.4 %collective-permute-start.3 = (bf16[16,64,128]{2,1,0:T(8,128)(2,1)S(1)}, bf16[16,64,128]{2,1,0:T(8,128)(2,1)S(1)}, u32[]{:S(2)}, u32[]{:S(2)}) collective-permute-start(bf16[16,64,128]{2,1,0:T(8,128)(2,1)S(1)} %all-to-all-done.r0_ref.rows_ref), channel_id=1, source_target_pairs={{0,4},{2,6},{4,0},{6,2},{1,5},{3,7},{5,1},{7,3},{8,12},{10,14},{12... | collective-permute-start | bytes 786440 | tf_op jit(solution)/shard_map/ppermute | solution.py:283
  46.9 0.0 copy-done
  46.9 1.2 %copy.10 = bf16[32,64,512]{2,1,0:T(8,128)(2,1)S(1)} copy(bf16[32,64,512]{2,0,1:T(8,128)(2,1)S(1)} %bitcast.20) | data formatting | bytes 4194304 | tf_op jit(solution)/shard_map/transpose | solution.py:279
  48.1 0.1 broadcast_multiply_fusion
  48.2 0.0 collective-permute-done
  48.2 2.8 %copy.11 = bf16[32,64,512]{2,1,0:T(8,128)(2,1)S(1)} copy(bf16[32,64,512]{2,0,1:T(8,128)(2,1)} %bitcast.5) | data formatting | bytes 4194304 | tf_op jit(solution)/shard_map/transpose | solution.py:279
  50.9 0.0 collective-permute-done.1.rp_ref
  50.9 0.0 collective-permute-done.2.rm_ref
  51.0 3.3 %collective-permute-done.3.rt_ref = bf16[16,64,128]{2,1,0:T(8,128)(2,1)S(1)} collective-permute-done((bf16[16,64,128]{2,1,0:T(8,128)(2,1)S(1)}, bf16[16,64,128]{2,1,0:T(8,128)(2,1)S(1)}, u32[]{:S(2)}, u32[]{:S(2)}) %collective-permute-start.3) | collective-permute-done | bytes 262176 | tf_op jit(solution)/shard_map/ppermute | solution.py:283
  54.3 6.2 %shard_map.64 = (bf16[512,2048]{1,0:T(8,128)(2,1)S(1)}, bf16[3,512,2048]{2,1,0:T(8,128)(2,1)}) custom-call(s32[3]{0:T(128)S(1)} %pad_add_fusion.where_ref, bf16[4,8,64,512]{3,2,1,0:T(8,128)(2,1)S(1)} %bitcast.17, bf16[4,8,64,512]{3,2,1,0:T(8,128)(2,1)S(1)} %bitcast.18, bf16[16,64,128]{2,1,0:T(8,128)(2,1)S(1)} %all-to-all-done.r0_ref.rows_ref, ...), custom_call_target="tpu_custom_call" | custom-call | flops 4294967296 | bytes 14680064 | tf_op jit(solution)/shard_map/pallas_call | solution.py:143
  60.5 5.0 %all-to-all-done.1 = bf16[8,8,8192]{2,1,0:T(8,128)(2,1)S(1)} async-done(((bf16[8,8,8192]{2,1,0:T(8,128)(2,1)}), bf16[8,8,8192]{2,1,0:T(8,128)(2,1)S(1)}, u32[]{:S(2)}, u32[]{:S(2)}) %all-to-all-start.1) | async-done | bytes 1048608 | tf_op jit(solution)/shard_map/all_to_all | solution.py:281
  65.5 0.0 copy-start.4
  65.5 0.0 copy-start.5
  65.5 5.0 %shard_map.66.own_ref = f32[256,128]{1,0:T(8,128)} custom-call(bf16[512,2048]{1,0:T(8,128)(2,1)S(1)} %get-tuple-element.7.near_ref, bf16[3,512,2048]{2,1,0:T(8,128)(2,1)} %get-tuple-element.8.prod_ref, bf16[64,8192]{1,0:T(8,128)(2,1)S(1)} %bitcast.16), custom_call_target="tpu_custom_call" | custom-call | flops 536870912 | bytes 9437184 | tf_op jit(solution)/shard_map/pallas_call | solution.py:191
  70.5 3.4 %all-to-all-start.2 = ((f32[8,32,128]{2,1,0:T(8,128)}), f32[8,32,128]{2,1,0:T(8,128)S(1)}, u32[]{:S(2)}, u32[]{:S(2)}) async-start(f32[8,32,128]{2,1,0:T(8,128)} %bitcast.10), calls=%async_computation.2 | async-start | bytes 262144 | tf_op jit(solution)/shard_map/all_to_all | solution.py:286
  73.9 0.0 copy-done.4
  73.9 0.2 select_reduce_fusion.3
  74.1 0.1 mul.47.pairing_ref
  74.2 0.0 copy-done.5
  74.2 0.1 dynamic_slice.7
  74.3 0.1 dynamic_slice.6
  74.4 0.1 broadcast_add_fusion
  74.4 7.5 %all-to-all-done.2 = f32[8,32,128]{2,1,0:T(8,128)S(1)} async-done(((f32[8,32,128]{2,1,0:T(8,128)}), f32[8,32,128]{2,1,0:T(8,128)S(1)}, u32[]{:S(2)}, u32[]{:S(2)}) %all-to-all-start.2) | async-done | bytes 131104 | tf_op jit(solution)/shard_map/all_to_all | solution.py:286
  82.0 2.0 %shard_map.67 = f32[64,4,128]{2,1,0:T(4,128)} custom-call(f32[256,128]{1,0:T(8,128)} %shard_map.66.own_ref, f32[256,128]{1,0:T(8,128)S(1)} %bitcast.19, f32[128,128]{1,0:T(8,128)S(1)} %mul.47.pairing_ref), custom_call_target="tpu_custom_call" | custom-call | tf_op jit(solution)/shard_map/pallas_call | solution.py:232
  83.9 7.2 %all-to-all-start.3 = ((f32[64,4,128]{2,1,0:T(4,128)}), f32[64,4,128]{2,1,0:T(4,128)S(1)}, u32[]{:S(2)}, u32[]{:S(2)}) async-start(f32[64,4,128]{2,1,0:T(4,128)} %shard_map.67), calls=%async_computation.3 | async-start | bytes 262144 | tf_op jit(solution)/shard_map/all_to_all | solution.py:288
  91.1 0.1 select_reduce_fusion.1
  91.2 0.1 sub.29
  91.3 0.1 sub.30
  91.4 0.1 sub.32
  91.5 10.1 %all-to-all-done.3.parts_ref = f32[64,4,128]{2,1,0:T(4,128)S(1)} async-done(((f32[64,4,128]{2,1,0:T(4,128)}), f32[64,4,128]{2,1,0:T(4,128)S(1)}, u32[]{:S(2)}, u32[]{:S(2)}) %all-to-all-start.3) | async-done | bytes 131104 | tf_op jit(solution)/shard_map/all_to_all | solution.py:288
  101.6 0.7 shard_map.68
  (7 shorter events, 0.1 us)
Async XLA Ops:
  0.0 48.2 %collective-permute-start = (bf16[64,32,512]{2,1,0:T(8,128)(2,1)}, bf16[64,32,512]{2,1,0:T(8,128)(2,1)}, u32[]{:S(2)}, u32[]{:S(2)}) collective-permute-start(bf16[64,32,512]{2,1,0:T(8,128)(2,1)} %param.7), channel_id=1, source_target_pairs={{0,1},{1,0},{2,3},{3,2},{4,5},{5,4},{6,7},{7,6},{8,9},{9,8},{10,11... | collective-permute-start | bytes 6291464 | tf_op jit(solution)/shard_map/ppermute | solution.py:277
  9.7 26.4 %copy-start.2 = (s32[64]{0:T(128)S(1)}, s32[64]{0:T(128)}, u32[]{:S(2)}) copy-start(s32[64]{0:T(128)} %param.10) | copy-start | bytes 772
  9.8 26.4 %copy-start.3 = (f32[128]{0:T(128)S(1)}, f32[128]{0:T(128)}, u32[]{:S(2)}) copy-start(f32[128]{0:T(128)} %param.11) | copy-start | bytes 1540
  9.8 27.1 %copy-start.1 = (s32[64]{0:T(128)S(1)}, s32[64]{0:T(128)}, u32[]{:S(2)}) copy-start(s32[64]{0:T(128)} %param.8) | copy-start | bytes 772
  10.5 36.4 %copy-start = (bf16[64,32,512]{2,1,0:T(8,128)(2,1)S(1)}, bf16[64,32,512]{2,1,0:T(8,128)(2,1)}, u32[]{:S(2)}) copy-start(bf16[64,32,512]{2,1,0:T(8,128)(2,1)} %param.7) | copy-start | bytes 6291460
  10.5 15.3 %all-to-all-start = ((bf16[16,64,128]{2,1,0:T(8,128)(2,1)}), bf16[16,64,128]{2,1,0:T(8,128)(2,1)S(1)}, u32[]{:S(2)}, u32[]{:S(2)}) async-start(bf16[16,64,128]{2,1,0:T(8,128)(2,1)} %bitcast.8), calls=%async_computation | async-start | bytes 524288 | tf_op jit(solution)/shard_map/all_to_all | solution.py:276
  27.7 37.8 %all-to-all-start.1 = ((bf16[8,8,8192]{2,1,0:T(8,128)(2,1)}), bf16[8,8,8192]{2,1,0:T(8,128)(2,1)S(1)}, u32[]{:S(2)}, u32[]{:S(2)}) async-start(bf16[8,8,8192]{2,1,0:T(8,128)(2,1)} %shard_map.65), calls=%async_computation.1 | async-start | bytes 2097152 | tf_op jit(solution)/shard_map/all_to_all | solution.py:281
  36.9 14.0 %collective-permute-start.1 = (bf16[16,64,128]{2,1,0:T(8,128)(2,1)S(1)}, bf16[16,64,128]{2,1,0:T(8,128)(2,1)S(1)}, u32[]{:S(2)}, u32[]{:S(2)}) collective-permute-start(bf16[16,64,128]{2,1,0:T(8,128)(2,1)S(1)} %all-to-all-done.r0_ref.rows_ref), channel_id=1, source_target_pairs={{0,2},{2,4},{4,6},{6,0},{1,3},{3,5},{5,7},{7,1},{8,10},{10,12},{12... | collective-permute-start | bytes 786440 | tf_op jit(solution)/shard_map/ppermute | solution.py:283
  40.0 10.9 %collective-permute-start.2 = (bf16[16,64,128]{2,1,0:T(8,128)(2,1)S(1)}, bf16[16,64,128]{2,1,0:T(8,128)(2,1)S(1)}, u32[]{:S(2)}, u32[]{:S(2)}) collective-permute-start(bf16[16,64,128]{2,1,0:T(8,128)(2,1)S(1)} %all-to-all-done.r0_ref.rows_ref), channel_id=1, source_target_pairs={{0,6},{2,0},{4,2},{6,4},{1,7},{3,1},{5,3},{7,5},{8,14},{10,8},{12,... | collective-permute-start | bytes 786440 | tf_op jit(solution)/shard_map/ppermute | solution.py:283
  43.4 10.9 %collective-permute-start.3 = (bf16[16,64,128]{2,1,0:T(8,128)(2,1)S(1)}, bf16[16,64,128]{2,1,0:T(8,128)(2,1)S(1)}, u32[]{:S(2)}, u32[]{:S(2)}) collective-permute-start(bf16[16,64,128]{2,1,0:T(8,128)(2,1)S(1)} %all-to-all-done.r0_ref.rows_ref), channel_id=1, source_target_pairs={{0,4},{2,6},{4,0},{6,2},{1,5},{3,7},{5,1},{7,3},{8,12},{10,14},{12... | collective-permute-start | bytes 786440 | tf_op jit(solution)/shard_map/ppermute | solution.py:283
  65.5 8.4 %copy-start.4 = (s32[8]{0:T(128)S(1)}, s32[8]{0:T(128)}, u32[]{:S(2)}) copy-start(s32[8]{0:T(128)} %param.9) | copy-start | bytes 100
  65.5 8.7 %copy-start.5 = (f32[64]{0:T(128)S(1)}, f32[64]{0:T(128)}, u32[]{:S(2)}) copy-start(f32[64]{0:T(128)} %select_reduce_fusion) | copy-start | bytes 772
  70.5 11.5 %all-to-all-start.2 = ((f32[8,32,128]{2,1,0:T(8,128)}), f32[8,32,128]{2,1,0:T(8,128)S(1)}, u32[]{:S(2)}, u32[]{:S(2)}) async-start(f32[8,32,128]{2,1,0:T(8,128)} %bitcast.10), calls=%async_computation.2 | async-start | bytes 262144 | tf_op jit(solution)/shard_map/all_to_all | solution.py:286
  83.9 17.7 %all-to-all-start.3 = ((f32[64,4,128]{2,1,0:T(4,128)}), f32[64,4,128]{2,1,0:T(4,128)S(1)}, u32[]{:S(2)}, u32[]{:S(2)}) async-start(f32[64,4,128]{2,1,0:T(4,128)} %shard_map.67), calls=%async_computation.3 | async-start | bytes 262144 | tf_op jit(solution)/shard_map/all_to_all | solution.py:288

commit v11 on v10

--- a/solution.py
+++ b/solution.py
@@ -32,14 +32,15 @@
     first = where_ref[2] * 8
     for n in range(8):
         wide[n * 64 : (n + 1) * 64, :] = rows_ref[first + n].astype(jnp.float32)
-    for dd in range(32):
+    for dd in range(16):
         for c in range(2):
             tile = dd * 2 + c
-            for r in range(2):
-                tiles[pl.ds(tile * 8 + r, 4, stride=2), :] = wide[
-                    pl.ds(c * 64 + r * 32 + dd, 4, stride=128), :
-                ]
-            packed[:, tile * 128 : (tile + 1) * 128] = tiles[tile * 8 : (tile + 1) * 8, :].astype(
+            for h in range(2):
+                for r in range(2):
+                    tiles[pl.ds(tile * 16 + h * 8 + r, 4, stride=2), :] = wide[
+                        pl.ds(c * 64 + r * 32 + h * 16 + dd, 4, stride=128), :
+                    ]
+            packed[:, tile * 128 : (tile + 1) * 128] = tiles[tile * 16 : (tile + 1) * 16, :].astype(
                 jnp.bfloat16
             )
     copies = [pltpu.make_async_copy(packed, out_ref.at[z], sem.at[z]) for z in range(8)]
@@ -57,11 +58,11 @@
             pl.BlockSpec(memory_space=pltpu.VMEM),
         ],
         out_specs=pl.BlockSpec(memory_space=pl.ANY),
-        out_shape=jax.ShapeDtypeStruct((8, 8, 8192), jnp.bfloat16),
+        out_shape=jax.ShapeDtypeStruct((8, 16, 4096), jnp.bfloat16),
         scratch_shapes=[
             pltpu.VMEM((512, 128), jnp.float32),
             pltpu.VMEM((512, 128), jnp.float32),
-            pltpu.VMEM((8, 8192), jnp.bfloat16),
+            pltpu.VMEM((16, 4096), jnp.bfloat16),
             pltpu.SemaphoreType.DMA((8,)),
         ],
         compiler_params=pltpu.CompilerParams(vmem_limit_bytes=8 * 1024 * 1024),
@@ -174,11 +175,15 @@
     for step in range(STEPS):
         if step > 0:
             copies[step - 1].wait()
-        total += lax.dot_general(
-            left_ref[:, step * width : (step + 1) * width],
+        half, lane = divmod(step * width, 4096)
+        both = lax.dot_general(
+            left_ref[:, lane : lane + width],
             near_ref[...] if step == 0 else prods[step - 1],
             (((1,), (1,)), ((), ())),
             preferred_element_type=jnp.float32,
+        )
+        total += jnp.concatenate(
+            [both[(z * 2 + half) * 8 : (z * 2 + half + 1) * 8] for z in range(8)], axis=0
         )
     for yl in range(4):
         for z in range(8):
@@ -278,7 +283,7 @@
     amps, amps_other = (
         t.transpose(1, 0, 2).reshape(STEPS, DSTEP, 64, 512) for t in (amplitudes, other)
     )
-    left = lax.all_to_all(for_each_plane(where, rows), "z", 0, 0, tiled=True).reshape(64, 8192)
+    left = lax.all_to_all(for_each_plane(where, rows), "z", 0, 0, tiled=True).reshape(128, 4096)
     rights = [rows] + [
         lax.ppermute(rows, "x", [(i, (i + s) % 4) for i in range(4)]) for s in (1, 3, 2)
     ]

time: 103 us -> 103 us (level)
  no operation moved by 1% of the time
where the time goes in v11:
time: 103 us; the launch traced here: 102 us
  starting transfers between devices  41.3 us (40%)
  waiting for transfers between devices  37.6 us (37%)
  Pallas kernels  15.5 us (15%)
  local copies, waits for them, and re-layouts  6.16 us (6%)
  other arithmetic  1.28 us (1%)
    all_to_all x1, waiting for transfers between devices, per_device(): rows = lax.all_to_all(eighths, ('yh', 'yl', 'c'), 0, 0, tiled=True)  11.7 us
    all_to_all x1, waiting for transfers between devices, per_device(): parts = lax.all_to_all(parts, GROUP, 0, 0, tiled=True)  10.1 us
    ppermute x3, starting transfers between devices, per_device(): lax.ppermute(rows, 'x', [(i, (i + s) % 4) for i in range(4)])  9.93 us
    ppermute x1, starting transfers between devices, per_device(): other = lax.ppermute(amplitudes, 'c', [(0, 1), (1, 0)])  8.78 us
    all_to_all x1, starting transfers between devices, per_device(): lax.all_to_all(for_each_plane(where, rows), 'z', 0, 0, tiled=True)  8.42 us
    all_to_all x1, waiting for transfers between devices, per_device(): crossed = lax.all_to_all(ladder.reshape(8, 32, 128), 'z', 0, 0, tiled=True)  7.54 us
    all_to_all x1, starting transfers between devices, per_device(): parts = lax.all_to_all(parts, GROUP, 0, 0, tiled=True)  7.21 us
    pallas_call x1, Pallas kernels, products(): pl.pallas_call(product_kernel, in_specs=[pl.BlockSpec(memory_space=pltpu....  6.19 us
  transfers between devices with their start and end apart: 8, of which 5 were waited for; matrix products, arithmetic and copies ran while one was open for 7% of the time, Pallas kernels for 8%

profile of v11, /device:TPU:1, one launch (start us, length us, event | category | flops | bytes accessed | tf_op | source)
XLA Modules:
  0.0 102.1 jit_solution(6263887794949986533)
XLA Ops:
  0.0 8.8 %collective-permute-start = (bf16[64,32,512]{2,1,0:T(8,128)(2,1)}, bf16[64,32,512]{2,1,0:T(8,128)(2,1)}, u32[]{:S(2)}, u32[]{:S(2)}) collective-permute-start(bf16[64,32,512]{2,1,0:T(8,128)(2,1)} %param.7), channel_id=1, source_target_pairs={{0,1},{1,0},{2,3},{3,2},{4,5},{5,4},{6,7},{7,6},{8,9},{9,8},{10,11... | collective-permute-start | bytes 6291464 | tf_op jit(solution)/shard_map/ppermute | solution.py:282
  8.8 0.9 copy.13
  9.7 0.0 copy-start.2
  9.8 0.0 copy-start.3
  9.8 0.0 copy-start.1
  9.8 0.8 broadcast_in_dim.46
  10.5 0.0 copy-start
  10.5 3.6 %all-to-all-start = ((bf16[16,64,128]{2,1,0:T(8,128)(2,1)}), bf16[16,64,128]{2,1,0:T(8,128)(2,1)S(1)}, u32[]{:S(2)}, u32[]{:S(2)}) async-start(bf16[16,64,128]{2,1,0:T(8,128)(2,1)} %bitcast.8), calls=%async_computation | async-start | bytes 524288 | tf_op jit(solution)/shard_map/all_to_all | solution.py:281
  14.1 0.1 pad_add_fusion.where_ref
  14.2 11.7 %all-to-all-done.r0_ref.rows_ref = bf16[16,64,128]{2,1,0:T(8,128)(2,1)S(1)} async-done(((bf16[16,64,128]{2,1,0:T(8,128)(2,1)}), bf16[16,64,128]{2,1,0:T(8,128)(2,1)S(1)}, u32[]{:S(2)}, u32[]{:S(2)}) %all-to-all-start) | async-done | bytes 262176 | tf_op jit(solution)/shard_map/all_to_all | solution.py:281
  25.9 1.9 %shard_map.65 = bf16[8,16,4096]{2,1,0:T(8,128)(2,1)} custom-call(s32[3]{0:T(128)S(1)} %pad_add_fusion.where_ref, bf16[16,64,128]{2,1,0:T(8,128)(2,1)S(1)} %all-to-all-done.r0_ref.rows_ref), custom_call_target="tpu_custom_call" | custom-call | tf_op jit(solution)/shard_map/pallas_call | solution.py:54
  27.7 8.4 %all-to-all-start.1 = ((bf16[8,16,4096]{2,1,0:T(8,128)(2,1)}), bf16[8,16,4096]{2,1,0:T(8,128)(2,1)S(1)}, u32[]{:S(2)}, u32[]{:S(2)}) async-start(bf16[8,16,4096]{2,1,0:T(8,128)(2,1)} %shard_map.65), calls=%async_computation.1 | async-start | bytes 2097152 | tf_op jit(solution)/shard_map/all_to_all | solution.py:286
  36.1 0.0 copy-done.2
  36.1 0.0 copy-done.3
  36.2 0.7 select_reduce_fusion
  36.8 0.0 copy-done.1
  36.8 0.1 compare_convert_fusion
  36.9 3.1 %collective-permute-start.1 = (bf16[16,64,128]{2,1,0:T(8,128)(2,1)S(1)}, bf16[16,64,128]{2,1,0:T(8,128)(2,1)S(1)}, u32[]{:S(2)}, u32[]{:S(2)}) collective-permute-start(bf16[16,64,128]{2,1,0:T(8,128)(2,1)S(1)} %all-to-all-done.r0_ref.rows_ref), channel_id=1, source_target_pairs={{0,2},{2,4},{4,6},{6,0},{1,3},{3,5},{5,7},{7,1},{8,10},{10,12},{12... | collective-permute-start | bytes 786440 | tf_op jit(solution)/shard_map/ppermute | solution.py:288
  40.0 3.4 %collective-permute-start.2 = (bf16[16,64,128]{2,1,0:T(8,128)(2,1)S(1)}, bf16[16,64,128]{2,1,0:T(8,128)(2,1)S(1)}, u32[]{:S(2)}, u32[]{:S(2)}) collective-permute-start(bf16[16,64,128]{2,1,0:T(8,128)(2,1)S(1)} %all-to-all-done.r0_ref.rows_ref), channel_id=1, source_target_pairs={{0,6},{2,0},{4,2},{6,4},{1,7},{3,1},{5,3},{7,5},{8,14},{10,8},{12,... | collective-permute-start | bytes 786440 | tf_op jit(solution)/shard_map/ppermute | solution.py:288
  43.4 3.4 %collective-permute-start.3 = (bf16[16,64,128]{2,1,0:T(8,128)(2,1)S(1)}, bf16[16,64,128]{2,1,0:T(8,128)(2,1)S(1)}, u32[]{:S(2)}, u32[]{:S(2)}) collective-permute-start(bf16[16,64,128]{2,1,0:T(8,128)(2,1)S(1)} %all-to-all-done.r0_ref.rows_ref), channel_id=1, source_target_pairs={{0,4},{2,6},{4,0},{6,2},{1,5},{3,7},{5,1},{7,3},{8,12},{10,14},{12... | collective-permute-start | bytes 786440 | tf_op jit(solution)/shard_map/ppermute | solution.py:288
  46.9 0.0 copy-done
  46.9 1.2 %copy.10 = bf16[32,64,512]{2,1,0:T(8,128)(2,1)S(1)} copy(bf16[32,64,512]{2,0,1:T(8,128)(2,1)S(1)} %bitcast.20) | data formatting | bytes 4194304 | tf_op jit(solution)/shard_map/transpose | solution.py:284
  48.1 0.1 broadcast_multiply_fusion
  48.2 0.0 collective-permute-done
  48.2 2.8 %copy.11 = bf16[32,64,512]{2,1,0:T(8,128)(2,1)S(1)} copy(bf16[32,64,512]{2,0,1:T(8,128)(2,1)} %bitcast.5) | data formatting | bytes 4194304 | tf_op jit(solution)/shard_map/transpose | solution.py:284
  50.9 0.0 collective-permute-done.1.rp_ref
  50.9 0.0 collective-permute-done.2.rm_ref
  50.9 3.3 %collective-permute-done.3.rt_ref = bf16[16,64,128]{2,1,0:T(8,128)(2,1)S(1)} collective-permute-done((bf16[16,64,128]{2,1,0:T(8,128)(2,1)S(1)}, bf16[16,64,128]{2,1,0:T(8,128)(2,1)S(1)}, u32[]{:S(2)}, u32[]{:S(2)}) %collective-permute-start.3) | collective-permute-done | bytes 262176 | tf_op jit(solution)/shard_map/ppermute | solution.py:288
  54.3 6.2 %shard_map.64 = (bf16[512,2048]{1,0:T(8,128)(2,1)S(1)}, bf16[3,512,2048]{2,1,0:T(8,128)(2,1)}) custom-call(s32[3]{0:T(128)S(1)} %pad_add_fusion.where_ref, bf16[4,8,64,512]{3,2,1,0:T(8,128)(2,1)S(1)} %bitcast.17, bf16[4,8,64,512]{3,2,1,0:T(8,128)(2,1)S(1)} %bitcast.18, bf16[16,64,128]{2,1,0:T(8,128)(2,1)S(1)} %all-to-all-done.r0_ref.rows_ref, ...), custom_call_target="tpu_custom_call" | custom-call | flops 4294967296 | bytes 14680064 | tf_op jit(solution)/shard_map/pallas_call | solution.py:144
  60.5 5.0 %all-to-all-done.1 = bf16[8,16,4096]{2,1,0:T(8,128)(2,1)S(1)} async-done(((bf16[8,16,4096]{2,1,0:T(8,128)(2,1)}), bf16[8,16,4096]{2,1,0:T(8,128)(2,1)S(1)}, u32[]{:S(2)}, u32[]{:S(2)}) %all-to-all-start.1) | async-done | bytes 1048608 | tf_op jit(solution)/shard_map/all_to_all | solution.py:286
  65.5 0.0 copy-start.4
  65.5 0.0 copy-start.5
  65.5 4.8 %shard_map.66.own_ref = f32[256,128]{1,0:T(8,128)} custom-call(bf16[512,2048]{1,0:T(8,128)(2,1)S(1)} %get-tuple-element.7.near_ref, bf16[3,512,2048]{2,1,0:T(8,128)(2,1)} %get-tuple-element.8.prod_ref, bf16[128,4096]{1,0:T(8,128)(2,1)S(1)} %bitcast.16), custom_call_target="tpu_custom_call" | custom-call | flops 536870912 | bytes 9437184 | tf_op jit(solution)/shard_map/pallas_call | solution.py:196
  70.3 3.4 %all-to-all-start.2 = ((f32[8,32,128]{2,1,0:T(8,128)}), f32[8,32,128]{2,1,0:T(8,128)S(1)}, u32[]{:S(2)}, u32[]{:S(2)}) async-start(f32[8,32,128]{2,1,0:T(8,128)} %bitcast.10), calls=%async_computation.2 | async-start | bytes 262144 | tf_op jit(solution)/shard_map/all_to_all | solution.py:291
  73.7 0.0 copy-done.4
  73.7 0.2 select_reduce_fusion.3
  73.9 0.1 mul.47.pairing_ref
  74.0 0.0 copy-done.5
  74.0 0.1 dynamic_slice.7
  74.1 0.1 dynamic_slice.6
  74.1 0.1 broadcast_add_fusion
  74.2 7.5 %all-to-all-done.2 = f32[8,32,128]{2,1,0:T(8,128)S(1)} async-done(((f32[8,32,128]{2,1,0:T(8,128)}), f32[8,32,128]{2,1,0:T(8,128)S(1)}, u32[]{:S(2)}, u32[]{:S(2)}) %all-to-all-start.2) | async-done | bytes 131104 | tf_op jit(solution)/shard_map/all_to_all | solution.py:291
  81.8 2.0 %shard_map.67 = f32[64,4,128]{2,1,0:T(4,128)} custom-call(f32[256,128]{1,0:T(8,128)} %shard_map.66.own_ref, f32[256,128]{1,0:T(8,128)S(1)} %bitcast.19, f32[128,128]{1,0:T(8,128)S(1)} %mul.47.pairing_ref), custom_call_target="tpu_custom_call" | custom-call | tf_op jit(solution)/shard_map/pallas_call | solution.py:237
  83.7 7.2 %all-to-all-start.3 = ((f32[64,4,128]{2,1,0:T(4,128)}), f32[64,4,128]{2,1,0:T(4,128)S(1)}, u32[]{:S(2)}, u32[]{:S(2)}) async-start(f32[64,4,128]{2,1,0:T(4,128)} %shard_map.67), calls=%async_computation.3 | async-start | bytes 262144 | tf_op jit(solution)/shard_map/all_to_all | solution.py:293
  90.9 0.1 select_reduce_fusion.1
  91.0 0.1 sub.29
  91.1 0.1 sub.30
  91.2 0.1 sub.32
  91.3 10.1 %all-to-all-done.3.parts_ref = f32[64,4,128]{2,1,0:T(4,128)S(1)} async-done(((f32[64,4,128]{2,1,0:T(4,128)}), f32[64,4,128]{2,1,0:T(4,128)S(1)}, u32[]{:S(2)}, u32[]{:S(2)}) %all-to-all-start.3) | async-done | bytes 131104 | tf_op jit(solution)/shard_map/all_to_all | solution.py:293
  101.4 0.7 shard_map.68
  (7 shorter events, 0.1 us)
Async XLA Ops:
  0.0 48.2 %collective-permute-start = (bf16[64,32,512]{2,1,0:T(8,128)(2,1)}, bf16[64,32,512]{2,1,0:T(8,128)(2,1)}, u32[]{:S(2)}, u32[]{:S(2)}) collective-permute-start(bf16[64,32,512]{2,1,0:T(8,128)(2,1)} %param.7), channel_id=1, source_target_pairs={{0,1},{1,0},{2,3},{3,2},{4,5},{5,4},{6,7},{7,6},{8,9},{9,8},{10,11... | collective-permute-start | bytes 6291464 | tf_op jit(solution)/shard_map/ppermute | solution.py:282
  9.7 26.4 %copy-start.2 = (s32[64]{0:T(128)S(1)}, s32[64]{0:T(128)}, u32[]{:S(2)}) copy-start(s32[64]{0:T(128)} %param.10) | copy-start | bytes 772
  9.8 26.4 %copy-start.3 = (f32[128]{0:T(128)S(1)}, f32[128]{0:T(128)}, u32[]{:S(2)}) copy-start(f32[128]{0:T(128)} %param.11) | copy-start | bytes 1540
  9.8 27.1 %copy-start.1 = (s32[64]{0:T(128)S(1)}, s32[64]{0:T(128)}, u32[]{:S(2)}) copy-start(s32[64]{0:T(128)} %param.8) | copy-start | bytes 772
  10.5 36.3 %copy-start = (bf16[64,32,512]{2,1,0:T(8,128)(2,1)S(1)}, bf16[64,32,512]{2,1,0:T(8,128)(2,1)}, u32[]{:S(2)}) copy-start(bf16[64,32,512]{2,1,0:T(8,128)(2,1)} %param.7) | copy-start | bytes 6291460
  10.5 15.3 %all-to-all-start = ((bf16[16,64,128]{2,1,0:T(8,128)(2,1)}), bf16[16,64,128]{2,1,0:T(8,128)(2,1)S(1)}, u32[]{:S(2)}, u32[]{:S(2)}) async-start(bf16[16,64,128]{2,1,0:T(8,128)(2,1)} %bitcast.8), calls=%async_computation | async-start | bytes 524288 | tf_op jit(solution)/shard_map/all_to_all | solution.py:281
  27.7 37.8 %all-to-all-start.1 = ((bf16[8,16,4096]{2,1,0:T(8,128)(2,1)}), bf16[8,16,4096]{2,1,0:T(8,128)(2,1)S(1)}, u32[]{:S(2)}, u32[]{:S(2)}) async-start(bf16[8,16,4096]{2,1,0:T(8,128)(2,1)} %shard_map.65), calls=%async_computation.1 | async-start | bytes 2097152 | tf_op jit(solution)/shard_map/all_to_all | solution.py:286
  36.9 14.0 %collective-permute-start.1 = (bf16[16,64,128]{2,1,0:T(8,128)(2,1)S(1)}, bf16[16,64,128]{2,1,0:T(8,128)(2,1)S(1)}, u32[]{:S(2)}, u32[]{:S(2)}) collective-permute-start(bf16[16,64,128]{2,1,0:T(8,128)(2,1)S(1)} %all-to-all-done.r0_ref.rows_ref), channel_id=1, source_target_pairs={{0,2},{2,4},{4,6},{6,0},{1,3},{3,5},{5,7},{7,1},{8,10},{10,12},{12... | collective-permute-start | bytes 786440 | tf_op jit(solution)/shard_map/ppermute | solution.py:288
  40.0 10.9 %collective-permute-start.2 = (bf16[16,64,128]{2,1,0:T(8,128)(2,1)S(1)}, bf16[16,64,128]{2,1,0:T(8,128)(2,1)S(1)}, u32[]{:S(2)}, u32[]{:S(2)}) collective-permute-start(bf16[16,64,128]{2,1,0:T(8,128)(2,1)S(1)} %all-to-all-done.r0_ref.rows_ref), channel_id=1, source_target_pairs={{0,6},{2,0},{4,2},{6,4},{1,7},{3,1},{5,3},{7,5},{8,14},{10,8},{12,... | collective-permute-start | bytes 786440 | tf_op jit(solution)/shard_map/ppermute | solution.py:288
  43.4 10.9 %collective-permute-start.3 = (bf16[16,64,128]{2,1,0:T(8,128)(2,1)S(1)}, bf16[16,64,128]{2,1,0:T(8,128)(2,1)S(1)}, u32[]{:S(2)}, u32[]{:S(2)}) collective-permute-start(bf16[16,64,128]{2,1,0:T(8,128)(2,1)S(1)} %all-to-all-done.r0_ref.rows_ref), channel_id=1, source_target_pairs={{0,4},{2,6},{4,0},{6,2},{1,5},{3,7},{5,1},{7,3},{8,12},{10,14},{12... | collective-permute-start | bytes 786440 | tf_op jit(solution)/shard_map/ppermute | solution.py:288
  65.5 8.2 %copy-start.4 = (s32[8]{0:T(128)S(1)}, s32[8]{0:T(128)}, u32[]{:S(2)}) copy-start(s32[8]{0:T(128)} %param.9) | copy-start | bytes 100
  65.5 8.5 %copy-start.5 = (f32[64]{0:T(128)S(1)}, f32[64]{0:T(128)}, u32[]{:S(2)}) copy-start(f32[64]{0:T(128)} %select_reduce_fusion) | copy-start | bytes 772
  70.3 11.5 %all-to-all-start.2 = ((f32[8,32,128]{2,1,0:T(8,128)}), f32[8,32,128]{2,1,0:T(8,128)S(1)}, u32[]{:S(2)}, u32[]{:S(2)}) async-start(f32[8,32,128]{2,1,0:T(8,128)} %bitcast.10), calls=%async_computation.2 | async-start | bytes 262144 | tf_op jit(solution)/shard_map/all_to_all | solution.py:291
  83.7 17.6 %all-to-all-start.3 = ((f32[64,4,128]{2,1,0:T(4,128)}), f32[64,4,128]{2,1,0:T(4,128)S(1)}, u32[]{:S(2)}, u32[]{:S(2)}) async-start(f32[64,4,128]{2,1,0:T(4,128)} %shard_map.67), calls=%async_computation.3 | async-start | bytes 262144 | tf_op jit(solution)/shard_map/all_to_all | solution.py:293

commit v12 on v11

--- a/solution.py
+++ b/solution.py
@@ -218,17 +218,23 @@
         rows = [crossed_ref[pl.ds(yl * 2 + r, 32, stride=8), :] for r in range(2)]
         for r in range(2):
             half = slice(r * 64, (r + 1) * 64)
-            turned[pl.ds(r, 32, stride=2), :] = jnp.concatenate(
+            turned[pl.ds(yl * 64 + r, 32, stride=2), :] = jnp.concatenate(
                 [rows[0][:, half], rows[1][:, half]], axis=1
             )
-        partnered = jnp.dot(
-            turned[...],
-            pairing_ref[...],
-            precision=lax.Precision.HIGHEST,
-            preferred_element_type=jnp.float32,
-        )
+    rest, parts = turned[...], []
+    for _ in range(3):
+        parts.append(rest.astype(jnp.bfloat16))
+        rest = rest - parts[-1].astype(jnp.float32)
+    three = jnp.dot(
+        jnp.concatenate(parts, axis=0),
+        pairing_ref[...].astype(jnp.bfloat16),
+        preferred_element_type=jnp.float32,
+    )
+    partnered = three[:256] + three[256:512] + three[512:]
+    for yl in range(4):
         for z in range(8):
-            total = own_ref[z * 32 + yl * 8 : z * 32 + yl * 8 + 8, :] + partnered[z * 8 : z * 8 + 8]
+            row = yl * 64 + z * 8
+            total = own_ref[z * 32 + yl * 8 : z * 32 + yl * 8 + 8, :] + partnered[row : row + 8]
             out_ref[(yl * 8 + z) * 2] = total[:4]
             out_ref[(yl * 8 + z) * 2 + 1] = total[4:]
 
@@ -237,7 +243,7 @@
     return pl.pallas_call(
         both_kernel,
         out_shape=jax.ShapeDtypeStruct((64, 4, 128), jnp.float32),
-        scratch_shapes=[pltpu.VMEM((64, 128), jnp.float32)],
+        scratch_shapes=[pltpu.VMEM((256, 128), jnp.float32)],
         compiler_params=pltpu.CompilerParams(vmem_limit_bytes=8 * 1024 * 1024),
     )(own, crossed, pairing)
 

time: 103 us -> 103 us (level)
  no operation moved by 1% of the time
where the time goes in v12:
time: 103 us; the launch traced here: 102 us
  starting transfers between devices  41.3 us (40%)
  waiting for transfers between devices  37.6 us (37%)
  Pallas kernels  15.4 us (15%)
  local copies, waits for them, and re-layouts  6.16 us (6%)
  other arithmetic  1.28 us (1%)
    all_to_all x1, waiting for transfers between devices, per_device(): rows = lax.all_to_all(eighths, ('yh', 'yl', 'c'), 0, 0, tiled=True)  11.7 us
    all_to_all x1, waiting for transfers between devices, per_device(): parts = lax.all_to_all(parts, GROUP, 0, 0, tiled=True)  10.1 us
    ppermute x3, starting transfers between devices, per_device(): lax.ppermute(rows, 'x', [(i, (i + s) % 4) for i in range(4)])  9.93 us
    ppermute x1, starting transfers between devices, per_device(): other = lax.ppermute(amplitudes, 'c', [(0, 1), (1, 0)])  8.78 us
    all_to_all x1, starting transfers between devices, per_device(): lax.all_to_all(for_each_plane(where, rows), 'z', 0, 0, tiled=True)  8.42 us
    all_to_all x1, waiting for transfers between devices, per_device(): crossed = lax.all_to_all(ladder.reshape(8, 32, 128), 'z', 0, 0, tiled=True)  7.54 us
    all_to_all x1, starting transfers between devices, per_device(): parts = lax.all_to_all(parts, GROUP, 0, 0, tiled=True)  7.21 us
    pallas_call x1, Pallas kernels, products(): pl.pallas_call(product_kernel, in_specs=[pl.BlockSpec(memory_space=pltpu....  6.19 us
  transfers between devices with their start and end apart: 8, of which 5 were waited for; matrix products, arithmetic and copies ran while one was open for 7% of the time, Pallas kernels for 8%

profile of v12, /device:TPU:1, one launch (start us, length us, event | category | flops | bytes accessed | tf_op | source)
XLA Modules:
  0.0 102.0 jit_solution(182394240580409836)
XLA Ops:
  0.0 8.8 %collective-permute-start = (bf16[64,32,512]{2,1,0:T(8,128)(2,1)}, bf16[64,32,512]{2,1,0:T(8,128)(2,1)}, u32[]{:S(2)}, u32[]{:S(2)}) collective-permute-start(bf16[64,32,512]{2,1,0:T(8,128)(2,1)} %param.7), channel_id=1, source_target_pairs={{0,1},{1,0},{2,3},{3,2},{4,5},{5,4},{6,7},{7,6},{8,9},{9,8},{10,11... | collective-permute-start | bytes 6291464 | tf_op jit(solution)/shard_map/ppermute | solution.py:288
  8.8 0.9 copy.13
  9.7 0.0 copy-start.2
  9.8 0.0 copy-start.3
  9.8 0.0 copy-start.1
  9.8 0.8 broadcast_in_dim.46
  10.5 0.0 copy-start
  10.5 3.6 %all-to-all-start = ((bf16[16,64,128]{2,1,0:T(8,128)(2,1)}), bf16[16,64,128]{2,1,0:T(8,128)(2,1)S(1)}, u32[]{:S(2)}, u32[]{:S(2)}) async-start(bf16[16,64,128]{2,1,0:T(8,128)(2,1)} %bitcast.8), calls=%async_computation | async-start | bytes 524288 | tf_op jit(solution)/shard_map/all_to_all | solution.py:287
  14.1 0.1 pad_add_fusion.where_ref
  14.2 11.7 %all-to-all-done.r0_ref.rows_ref = bf16[16,64,128]{2,1,0:T(8,128)(2,1)S(1)} async-done(((bf16[16,64,128]{2,1,0:T(8,128)(2,1)}), bf16[16,64,128]{2,1,0:T(8,128)(2,1)S(1)}, u32[]{:S(2)}, u32[]{:S(2)}) %all-to-all-start) | async-done | bytes 262176 | tf_op jit(solution)/shard_map/all_to_all | solution.py:287
  25.9 1.9 %shard_map.65 = bf16[8,16,4096]{2,1,0:T(8,128)(2,1)} custom-call(s32[3]{0:T(128)S(1)} %pad_add_fusion.where_ref, bf16[16,64,128]{2,1,0:T(8,128)(2,1)S(1)} %all-to-all-done.r0_ref.rows_ref), custom_call_target="tpu_custom_call" | custom-call | tf_op jit(solution)/shard_map/pallas_call | solution.py:54
  27.7 8.4 %all-to-all-start.1 = ((bf16[8,16,4096]{2,1,0:T(8,128)(2,1)}), bf16[8,16,4096]{2,1,0:T(8,128)(2,1)S(1)}, u32[]{:S(2)}, u32[]{:S(2)}) async-start(bf16[8,16,4096]{2,1,0:T(8,128)(2,1)} %shard_map.65), calls=%async_computation.1 | async-start | bytes 2097152 | tf_op jit(solution)/shard_map/all_to_all | solution.py:292
  36.1 0.0 copy-done.2
  36.1 0.0 copy-done.3
  36.2 0.7 select_reduce_fusion
  36.8 0.0 copy-done.1
  36.8 0.1 compare_convert_fusion
  36.9 3.1 %collective-permute-start.1 = (bf16[16,64,128]{2,1,0:T(8,128)(2,1)S(1)}, bf16[16,64,128]{2,1,0:T(8,128)(2,1)S(1)}, u32[]{:S(2)}, u32[]{:S(2)}) collective-permute-start(bf16[16,64,128]{2,1,0:T(8,128)(2,1)S(1)} %all-to-all-done.r0_ref.rows_ref), channel_id=1, source_target_pairs={{0,2},{2,4},{4,6},{6,0},{1,3},{3,5},{5,7},{7,1},{8,10},{10,12},{12... | collective-permute-start | bytes 786440 | tf_op jit(solution)/shard_map/ppermute | solution.py:294
  40.0 3.4 %collective-permute-start.2 = (bf16[16,64,128]{2,1,0:T(8,128)(2,1)S(1)}, bf16[16,64,128]{2,1,0:T(8,128)(2,1)S(1)}, u32[]{:S(2)}, u32[]{:S(2)}) collective-permute-start(bf16[16,64,128]{2,1,0:T(8,128)(2,1)S(1)} %all-to-all-done.r0_ref.rows_ref), channel_id=1, source_target_pairs={{0,6},{2,0},{4,2},{6,4},{1,7},{3,1},{5,3},{7,5},{8,14},{10,8},{12,... | collective-permute-start | bytes 786440 | tf_op jit(solution)/shard_map/ppermute | solution.py:294
  43.4 3.4 %collective-permute-start.3 = (bf16[16,64,128]{2,1,0:T(8,128)(2,1)S(1)}, bf16[16,64,128]{2,1,0:T(8,128)(2,1)S(1)}, u32[]{:S(2)}, u32[]{:S(2)}) collective-permute-start(bf16[16,64,128]{2,1,0:T(8,128)(2,1)S(1)} %all-to-all-done.r0_ref.rows_ref), channel_id=1, source_target_pairs={{0,4},{2,6},{4,0},{6,2},{1,5},{3,7},{5,1},{7,3},{8,12},{10,14},{12... | collective-permute-start | bytes 786440 | tf_op jit(solution)/shard_map/ppermute | solution.py:294
  46.9 0.0 copy-done
  46.9 1.2 %copy.10 = bf16[32,64,512]{2,1,0:T(8,128)(2,1)S(1)} copy(bf16[32,64,512]{2,0,1:T(8,128)(2,1)S(1)} %bitcast.20) | data formatting | bytes 4194304 | tf_op jit(solution)/shard_map/transpose | solution.py:290
  48.1 0.1 broadcast_multiply_fusion
  48.2 0.0 collective-permute-done
  48.2 2.8 %copy.11 = bf16[32,64,512]{2,1,0:T(8,128)(2,1)S(1)} copy(bf16[32,64,512]{2,0,1:T(8,128)(2,1)} %bitcast.5) | data formatting | bytes 4194304 | tf_op jit(solution)/shard_map/transpose | solution.py:290
  50.9 0.0 collective-permute-done.1.rp_ref
  50.9 0.0 collective-permute-done.2.rm_ref
  50.9 3.3 %collective-permute-done.3.rt_ref = bf16[16,64,128]{2,1,0:T(8,128)(2,1)S(1)} collective-permute-done((bf16[16,64,128]{2,1,0:T(8,128)(2,1)S(1)}, bf16[16,64,128]{2,1,0:T(8,128)(2,1)S(1)}, u32[]{:S(2)}, u32[]{:S(2)}) %collective-permute-start.3) | collective-permute-done | bytes 262176 | tf_op jit(solution)/shard_map/ppermute | solution.py:294
  54.3 6.2 %shard_map.64 = (bf16[512,2048]{1,0:T(8,128)(2,1)S(1)}, bf16[3,512,2048]{2,1,0:T(8,128)(2,1)}) custom-call(s32[3]{0:T(128)S(1)} %pad_add_fusion.where_ref, bf16[4,8,64,512]{3,2,1,0:T(8,128)(2,1)S(1)} %bitcast.17, bf16[4,8,64,512]{3,2,1,0:T(8,128)(2,1)S(1)} %bitcast.18, bf16[16,64,128]{2,1,0:T(8,128)(2,1)S(1)} %all-to-all-done.r0_ref.rows_ref, ...), custom_call_target="tpu_custom_call" | custom-call | flops 4294967296 | bytes 14680064 | tf_op jit(solution)/shard_map/pallas_call | solution.py:144
  60.5 5.0 %all-to-all-done.1 = bf16[8,16,4096]{2,1,0:T(8,128)(2,1)S(1)} async-done(((bf16[8,16,4096]{2,1,0:T(8,128)(2,1)}), bf16[8,16,4096]{2,1,0:T(8,128)(2,1)S(1)}, u32[]{:S(2)}, u32[]{:S(2)}) %all-to-all-start.1) | async-done | bytes 1048608 | tf_op jit(solution)/shard_map/all_to_all | solution.py:292
  65.5 0.0 copy-start.4
  65.5 0.0 copy-start.5
  65.5 4.8 %shard_map.66.own_ref = f32[256,128]{1,0:T(8,128)} custom-call(bf16[512,2048]{1,0:T(8,128)(2,1)S(1)} %get-tuple-element.7.near_ref, bf16[3,512,2048]{2,1,0:T(8,128)(2,1)} %get-tuple-element.8.prod_ref, bf16[128,4096]{1,0:T(8,128)(2,1)S(1)} %bitcast.16), custom_call_target="tpu_custom_call" | custom-call | flops 536870912 | bytes 9437184 | tf_op jit(solution)/shard_map/pallas_call | solution.py:196
  70.3 3.4 %all-to-all-start.2 = ((f32[8,32,128]{2,1,0:T(8,128)}), f32[8,32,128]{2,1,0:T(8,128)S(1)}, u32[]{:S(2)}, u32[]{:S(2)}) async-start(f32[8,32,128]{2,1,0:T(8,128)} %bitcast.10), calls=%async_computation.2 | async-start | bytes 262144 | tf_op jit(solution)/shard_map/all_to_all | solution.py:297
  73.7 0.0 copy-done.4
  73.7 0.2 select_reduce_fusion.3
  73.9 0.1 mul.47.pairing_ref
  74.0 0.0 copy-done.5
  74.0 0.1 dynamic_slice.7
  74.1 0.1 dynamic_slice.6
  74.1 0.1 broadcast_add_fusion
  74.2 7.5 %all-to-all-done.2 = f32[8,32,128]{2,1,0:T(8,128)S(1)} async-done(((f32[8,32,128]{2,1,0:T(8,128)}), f32[8,32,128]{2,1,0:T(8,128)S(1)}, u32[]{:S(2)}, u32[]{:S(2)}) %all-to-all-start.2) | async-done | bytes 131104 | tf_op jit(solution)/shard_map/all_to_all | solution.py:297
  81.8 1.8 %shard_map.67 = f32[64,4,128]{2,1,0:T(4,128)} custom-call(f32[256,128]{1,0:T(8,128)} %shard_map.66.own_ref, f32[256,128]{1,0:T(8,128)S(1)} %bitcast.19, f32[128,128]{1,0:T(8,128)S(1)} %mul.47.pairing_ref), custom_call_target="tpu_custom_call" | custom-call | tf_op jit(solution)/shard_map/pallas_call | solution.py:243
  83.6 7.2 %all-to-all-start.3 = ((f32[64,4,128]{2,1,0:T(4,128)}), f32[64,4,128]{2,1,0:T(4,128)S(1)}, u32[]{:S(2)}, u32[]{:S(2)}) async-start(f32[64,4,128]{2,1,0:T(4,128)} %shard_map.67), calls=%async_computation.3 | async-start | bytes 262144 | tf_op jit(solution)/shard_map/all_to_all | solution.py:299
  90.8 0.1 select_reduce_fusion.1
  90.9 0.1 sub.29
  91.0 0.1 sub.30
  91.1 0.1 sub.32
  91.2 10.1 %all-to-all-done.3.parts_ref = f32[64,4,128]{2,1,0:T(4,128)S(1)} async-done(((f32[64,4,128]{2,1,0:T(4,128)}), f32[64,4,128]{2,1,0:T(4,128)S(1)}, u32[]{:S(2)}, u32[]{:S(2)}) %all-to-all-start.3) | async-done | bytes 131104 | tf_op jit(solution)/shard_map/all_to_all | solution.py:299
  101.2 0.7 shard_map.68
  (7 shorter events, 0.1 us)
Async XLA Ops:
  0.0 48.2 %collective-permute-start = (bf16[64,32,512]{2,1,0:T(8,128)(2,1)}, bf16[64,32,512]{2,1,0:T(8,128)(2,1)}, u32[]{:S(2)}, u32[]{:S(2)}) collective-permute-start(bf16[64,32,512]{2,1,0:T(8,128)(2,1)} %param.7), channel_id=1, source_target_pairs={{0,1},{1,0},{2,3},{3,2},{4,5},{5,4},{6,7},{7,6},{8,9},{9,8},{10,11... | collective-permute-start | bytes 6291464 | tf_op jit(solution)/shard_map/ppermute | solution.py:288
  9.7 26.4 %copy-start.2 = (s32[64]{0:T(128)S(1)}, s32[64]{0:T(128)}, u32[]{:S(2)}) copy-start(s32[64]{0:T(128)} %param.10) | copy-start | bytes 772
  9.8 26.4 %copy-start.3 = (f32[128]{0:T(128)S(1)}, f32[128]{0:T(128)}, u32[]{:S(2)}) copy-start(f32[128]{0:T(128)} %param.11) | copy-start | bytes 1540
  9.8 27.1 %copy-start.1 = (s32[64]{0:T(128)S(1)}, s32[64]{0:T(128)}, u32[]{:S(2)}) copy-start(s32[64]{0:T(128)} %param.8) | copy-start | bytes 772
  10.5 36.3 %copy-start = (bf16[64,32,512]{2,1,0:T(8,128)(2,1)S(1)}, bf16[64,32,512]{2,1,0:T(8,128)(2,1)}, u32[]{:S(2)}) copy-start(bf16[64,32,512]{2,1,0:T(8,128)(2,1)} %param.7) | copy-start | bytes 6291460
  10.5 15.3 %all-to-all-start = ((bf16[16,64,128]{2,1,0:T(8,128)(2,1)}), bf16[16,64,128]{2,1,0:T(8,128)(2,1)S(1)}, u32[]{:S(2)}, u32[]{:S(2)}) async-start(bf16[16,64,128]{2,1,0:T(8,128)(2,1)} %bitcast.8), calls=%async_computation | async-start | bytes 524288 | tf_op jit(solution)/shard_map/all_to_all | solution.py:287
  27.7 37.8 %all-to-all-start.1 = ((bf16[8,16,4096]{2,1,0:T(8,128)(2,1)}), bf16[8,16,4096]{2,1,0:T(8,128)(2,1)S(1)}, u32[]{:S(2)}, u32[]{:S(2)}) async-start(bf16[8,16,4096]{2,1,0:T(8,128)(2,1)} %shard_map.65), calls=%async_computation.1 | async-start | bytes 2097152 | tf_op jit(solution)/shard_map/all_to_all | solution.py:292
  36.9 14.0 %collective-permute-start.1 = (bf16[16,64,128]{2,1,0:T(8,128)(2,1)S(1)}, bf16[16,64,128]{2,1,0:T(8,128)(2,1)S(1)}, u32[]{:S(2)}, u32[]{:S(2)}) collective-permute-start(bf16[16,64,128]{2,1,0:T(8,128)(2,1)S(1)} %all-to-all-done.r0_ref.rows_ref), channel_id=1, source_target_pairs={{0,2},{2,4},{4,6},{6,0},{1,3},{3,5},{5,7},{7,1},{8,10},{10,12},{12... | collective-permute-start | bytes 786440 | tf_op jit(solution)/shard_map/ppermute | solution.py:294
  40.0 10.9 %collective-permute-start.2 = (bf16[16,64,128]{2,1,0:T(8,128)(2,1)S(1)}, bf16[16,64,128]{2,1,0:T(8,128)(2,1)S(1)}, u32[]{:S(2)}, u32[]{:S(2)}) collective-permute-start(bf16[16,64,128]{2,1,0:T(8,128)(2,1)S(1)} %all-to-all-done.r0_ref.rows_ref), channel_id=1, source_target_pairs={{0,6},{2,0},{4,2},{6,4},{1,7},{3,1},{5,3},{7,5},{8,14},{10,8},{12,... | collective-permute-start | bytes 786440 | tf_op jit(solution)/shard_map/ppermute | solution.py:294
  43.4 10.9 %collective-permute-start.3 = (bf16[16,64,128]{2,1,0:T(8,128)(2,1)S(1)}, bf16[16,64,128]{2,1,0:T(8,128)(2,1)S(1)}, u32[]{:S(2)}, u32[]{:S(2)}) collective-permute-start(bf16[16,64,128]{2,1,0:T(8,128)(2,1)S(1)} %all-to-all-done.r0_ref.rows_ref), channel_id=1, source_target_pairs={{0,4},{2,6},{4,0},{6,2},{1,5},{3,7},{5,1},{7,3},{8,12},{10,14},{12... | collective-permute-start | bytes 786440 | tf_op jit(solution)/shard_map/ppermute | solution.py:294
  65.5 8.2 %copy-start.4 = (s32[8]{0:T(128)S(1)}, s32[8]{0:T(128)}, u32[]{:S(2)}) copy-start(s32[8]{0:T(128)} %param.9) | copy-start | bytes 100
  65.5 8.5 %copy-start.5 = (f32[64]{0:T(128)S(1)}, f32[64]{0:T(128)}, u32[]{:S(2)}) copy-start(f32[64]{0:T(128)} %select_reduce_fusion) | copy-start | bytes 772
  70.3 11.5 %all-to-all-start.2 = ((f32[8,32,128]{2,1,0:T(8,128)}), f32[8,32,128]{2,1,0:T(8,128)S(1)}, u32[]{:S(2)}, u32[]{:S(2)}) async-start(f32[8,32,128]{2,1,0:T(8,128)} %bitcast.10), calls=%async_computation.2 | async-start | bytes 262144 | tf_op jit(solution)/shard_map/all_to_all | solution.py:297
  83.6 17.6 %all-to-all-start.3 = ((f32[64,4,128]{2,1,0:T(4,128)}), f32[64,4,128]{2,1,0:T(4,128)S(1)}, u32[]{:S(2)}, u32[]{:S(2)}) async-start(f32[64,4,128]{2,1,0:T(4,128)} %shard_map.67), calls=%async_computation.3 | async-start | bytes 262144 | tf_op jit(solution)/shard_map/all_to_all | solution.py:299

commit v13 on v12

--- a/solution.py
+++ b/solution.py
@@ -285,11 +285,12 @@
     eighths = factors.reshape(64, 8, 128).transpose(1, 0, 2)
     eighths = jnp.broadcast_to(eighths[None], (2, 8, 64, 128)).reshape(16, 64, 128)
     rows = lax.all_to_all(eighths, ("yh", "yl", "c"), 0, 0, tiled=True)
-    other = lax.ppermute(amplitudes, "c", [(0, 1), (1, 0)])
+    planes, sent = lax.optimization_barrier((for_each_plane(where, rows), amplitudes))
+    left = lax.all_to_all(planes, "z", 0, 0, tiled=True).reshape(128, 4096)
+    other = lax.ppermute(sent, "c", [(0, 1), (1, 0)])
     amps, amps_other = (
         t.transpose(1, 0, 2).reshape(STEPS, DSTEP, 64, 512) for t in (amplitudes, other)
     )
-    left = lax.all_to_all(for_each_plane(where, rows), "z", 0, 0, tiled=True).reshape(128, 4096)
     rights = [rows] + [
         lax.ppermute(rows, "x", [(i, (i + s) % 4) for i in range(4)]) for s in (1, 3, 2)
     ]

time: 103 us -> 103 us (level)
    ppermute x1, starting transfers between devices: 8.78 us -> 1.92 us  [per_device(): other = lax.ppermute(sent, 'c', [(0, 1), (1, 0)])]
    all_to_all x1, starting transfers between devices: 3.56 us -> 10.2 us  [per_device(): rows = lax.all_to_all(eighths, ('yh', 'yl', 'c'), 0, 0, tiled=True)]
  transfers between devices with their start and end apart: 8 -> 8, of which waited for: 5 -> 5; matrix products, arithmetic and copies ran while one was open for 7% -> 6% of each run, Pallas kernels for 8% -> 6%
where the time goes in v13:
time: 103 us; the launch traced here: 102 us
  starting transfers between devices  41.6 us (40%)
  waiting for transfers between devices  37.6 us (37%)
  Pallas kernels  15.4 us (15%)
  local copies, waits for them, and re-layouts  6.31 us (6%)
  other arithmetic  1.28 us (1%)
    all_to_all x1, waiting for transfers between devices, per_device(): rows = lax.all_to_all(eighths, ('yh', 'yl', 'c'), 0, 0, tiled=True)  11.8 us
    all_to_all x1, starting transfers between devices, per_device(): rows = lax.all_to_all(eighths, ('yh', 'yl', 'c'), 0, 0, tiled=True)  10.2 us
    all_to_all x1, waiting for transfers between devices, per_device(): parts = lax.all_to_all(parts, GROUP, 0, 0, tiled=True)  10.1 us
    ppermute x3, starting transfers between devices, per_device(): lax.ppermute(rows, 'x', [(i, (i + s) % 4) for i in range(4)])  9.93 us
    all_to_all x1, starting transfers between devices, per_device(): left = lax.all_to_all(planes, 'z', 0, 0, tiled=True).reshape(128, 4096)  8.32 us
    all_to_all x1, starting transfers between devices, per_device(): parts = lax.all_to_all(parts, GROUP, 0, 0, tiled=True)  7.82 us
    all_to_all x1, waiting for transfers between devices, per_device(): crossed = lax.all_to_all(ladder.reshape(8, 32, 128), 'z', 0, 0, tiled=True)  7.51 us
    pallas_call x1, Pallas kernels, products(): pl.pallas_call(product_kernel, in_specs=[pl.BlockSpec(memory_space=pltpu....  6.19 us
  transfers between devices with their start and end apart: 8, of which 5 were waited for; matrix products, arithmetic and copies ran while one was open for 6% of the time, Pallas kernels for 6%

profile of v13, /device:TPU:1, one launch (start us, length us, event | category | flops | bytes accessed | tf_op | source)
XLA Modules:
  0.0 102.3 jit_solution(15934384619037904275)
XLA Ops:
  0.0 0.0 copy-start
  0.0 1.1 %copy.13 = bf16[8,8,8,128]{3,2,1,0:T(8,128)(2,1)S(1)} copy(bf16[8,8,8,128]{3,1,2,0:T(8,128)(2,1)} %bitcast.22) | data formatting | bytes 262144
  1.1 0.0 copy-start.2
  1.1 0.0 copy-start.3
  1.1 0.0 copy-start.1
  1.1 0.8 broadcast_in_dim.46
  1.9 10.2 %all-to-all-start = ((bf16[16,64,128]{2,1,0:T(8,128)(2,1)}), bf16[16,64,128]{2,1,0:T(8,128)(2,1)S(1)}, u32[]{:S(2)}, u32[]{:S(2)}) async-start(bf16[16,64,128]{2,1,0:T(8,128)(2,1)} %bitcast.6), calls=%async_computation | async-start | bytes 524288 | tf_op jit(solution)/shard_map/all_to_all | solution.py:287
  12.1 0.1 pad_add_fusion.where_ref
  12.2 11.8 %all-to-all-done.rows_ref.r0_ref = bf16[16,64,128]{2,1,0:T(8,128)(2,1)S(1)} async-done(((bf16[16,64,128]{2,1,0:T(8,128)(2,1)}), bf16[16,64,128]{2,1,0:T(8,128)(2,1)S(1)}, u32[]{:S(2)}, u32[]{:S(2)}) %all-to-all-start) | async-done | bytes 262176 | tf_op jit(solution)/shard_map/all_to_all | solution.py:287
  24.0 1.9 %shard_map.64 = bf16[8,16,4096]{2,1,0:T(8,128)(2,1)} custom-call(s32[3]{0:T(128)S(1)} %pad_add_fusion.where_ref, bf16[16,64,128]{2,1,0:T(8,128)(2,1)S(1)} %all-to-all-done.rows_ref.r0_ref), custom_call_target="tpu_custom_call" | custom-call | tf_op jit(solution)/shard_map/pallas_call | solution.py:54
  25.8 0.0 copy-done
  25.8 1.9 %collective-permute-start = (bf16[64,32,512]{2,1,0:T(8,128)(2,1)S(1)}, bf16[64,32,512]{2,1,0:T(8,128)(2,1)}, u32[]{:S(2)}, u32[]{:S(2)}) collective-permute-start(bf16[64,32,512]{2,1,0:T(8,128)(2,1)S(1)} %copy-done), channel_id=1, source_target_pairs={{0,1},{1,0},{2,3},{3,2},{4,5},{5,4},{6,7},{7,6},{8,9},{9,8},{10,11... | collective-permute-start | bytes 6291464 | tf_op jit(solution)/shard_map/ppermute | solution.py:290
  27.8 8.3 %all-to-all-start.1 = ((bf16[8,16,4096]{2,1,0:T(8,128)(2,1)}), bf16[8,16,4096]{2,1,0:T(8,128)(2,1)S(1)}, u32[]{:S(2)}, u32[]{:S(2)}) async-start(bf16[8,16,4096]{2,1,0:T(8,128)(2,1)} %shard_map.64), calls=%async_computation.1 | async-start | bytes 2097152 | tf_op jit(solution)/shard_map/all_to_all | solution.py:289
  36.1 0.0 copy-done.2
  36.1 0.0 copy-done.3
  36.1 0.7 select_reduce_fusion
  36.8 0.0 copy-done.1
  36.8 0.1 compare_convert_fusion
  36.8 3.1 %collective-permute-start.1 = (bf16[16,64,128]{2,1,0:T(8,128)(2,1)S(1)}, bf16[16,64,128]{2,1,0:T(8,128)(2,1)S(1)}, u32[]{:S(2)}, u32[]{:S(2)}) collective-permute-start(bf16[16,64,128]{2,1,0:T(8,128)(2,1)S(1)} %all-to-all-done.rows_ref.r0_ref), channel_id=1, source_target_pairs={{0,2},{2,4},{4,6},{6,0},{1,3},{3,5},{5,7},{7,1},{8,10},{10,12},{12... | collective-permute-start | bytes 786440 | tf_op jit(solution)/shard_map/ppermute | solution.py:295
  40.0 3.4 %collective-permute-start.2 = (bf16[16,64,128]{2,1,0:T(8,128)(2,1)S(1)}, bf16[16,64,128]{2,1,0:T(8,128)(2,1)S(1)}, u32[]{:S(2)}, u32[]{:S(2)}) collective-permute-start(bf16[16,64,128]{2,1,0:T(8,128)(2,1)S(1)} %all-to-all-done.rows_ref.r0_ref), channel_id=1, source_target_pairs={{0,6},{2,0},{4,2},{6,4},{1,7},{3,1},{5,3},{7,5},{8,14},{10,8},{12,... | collective-permute-start | bytes 786440 | tf_op jit(solution)/shard_map/ppermute | solution.py:295
  43.3 3.4 %collective-permute-start.3 = (bf16[16,64,128]{2,1,0:T(8,128)(2,1)S(1)}, bf16[16,64,128]{2,1,0:T(8,128)(2,1)S(1)}, u32[]{:S(2)}, u32[]{:S(2)}) collective-permute-start(bf16[16,64,128]{2,1,0:T(8,128)(2,1)S(1)} %all-to-all-done.rows_ref.r0_ref), channel_id=1, source_target_pairs={{0,4},{2,6},{4,0},{6,2},{1,5},{3,7},{5,1},{7,3},{8,12},{10,14},{12... | collective-permute-start | bytes 786440 | tf_op jit(solution)/shard_map/ppermute | solution.py:295
  46.8 1.2 %copy.10 = bf16[32,64,512]{2,1,0:T(8,128)(2,1)S(1)} copy(bf16[32,64,512]{2,0,1:T(8,128)(2,1)S(1)} %bitcast.20) | data formatting | bytes 4194304 | tf_op jit(solution)/shard_map/transpose | solution.py:292
  48.0 0.1 broadcast_multiply_fusion
  48.1 0.0 collective-permute-done
  48.1 2.8 %copy.12 = bf16[32,64,512]{2,1,0:T(8,128)(2,1)S(1)} copy(bf16[32,64,512]{2,0,1:T(8,128)(2,1)} %bitcast.7) | data formatting | bytes 4194304 | tf_op jit(solution)/shard_map/transpose | solution.py:292
  50.9 0.0 collective-permute-done.1.rp_ref
  50.9 0.0 collective-permute-done.2.rm_ref
  50.9 2.3 %collective-permute-done.3.rt_ref = bf16[16,64,128]{2,1,0:T(8,128)(2,1)S(1)} collective-permute-done((bf16[16,64,128]{2,1,0:T(8,128)(2,1)S(1)}, bf16[16,64,128]{2,1,0:T(8,128)(2,1)S(1)}, u32[]{:S(2)}, u32[]{:S(2)}) %collective-permute-start.3) | collective-permute-done | bytes 262176 | tf_op jit(solution)/shard_map/ppermute | solution.py:295
  53.2 6.2 %shard_map.65 = (bf16[512,2048]{1,0:T(8,128)(2,1)S(1)}, bf16[3,512,2048]{2,1,0:T(8,128)(2,1)}) custom-call(s32[3]{0:T(128)S(1)} %pad_add_fusion.where_ref, bf16[4,8,64,512]{3,2,1,0:T(8,128)(2,1)S(1)} %bitcast.17, bf16[4,8,64,512]{3,2,1,0:T(8,128)(2,1)S(1)} %bitcast.18, bf16[16,64,128]{2,1,0:T(8,128)(2,1)S(1)} %all-to-all-done.rows_ref.r0_ref, ...), custom_call_target="tpu_custom_call" | custom-call | flops 4294967296 | bytes 14680064 | tf_op jit(solution)/shard_map/pallas_call | solution.py:144
  59.4 5.9 %all-to-all-done.1 = bf16[8,16,4096]{2,1,0:T(8,128)(2,1)S(1)} async-done(((bf16[8,16,4096]{2,1,0:T(8,128)(2,1)}), bf16[8,16,4096]{2,1,0:T(8,128)(2,1)S(1)}, u32[]{:S(2)}, u32[]{:S(2)}) %all-to-all-start.1) | async-done | bytes 1048608 | tf_op jit(solution)/shard_map/all_to_all | solution.py:289
  65.3 0.0 copy-start.4
  65.3 0.0 copy-start.5
  65.3 4.8 %shard_map.66.own_ref = f32[256,128]{1,0:T(8,128)} custom-call(bf16[512,2048]{1,0:T(8,128)(2,1)S(1)} %get-tuple-element.10.near_ref, bf16[3,512,2048]{2,1,0:T(8,128)(2,1)} %get-tuple-element.11.prod_ref, bf16[128,4096]{1,0:T(8,128)(2,1)S(1)} %bitcast.16), custom_call_target="tpu_custom_call" | custom-call | flops 536870912 | bytes 9437184 | tf_op jit(solution)/shard_map/pallas_call | solution.py:196
  70.1 3.4 %all-to-all-start.2 = ((f32[8,32,128]{2,1,0:T(8,128)}), f32[8,32,128]{2,1,0:T(8,128)S(1)}, u32[]{:S(2)}, u32[]{:S(2)}) async-start(f32[8,32,128]{2,1,0:T(8,128)} %bitcast.10), calls=%async_computation.2 | async-start | bytes 262144 | tf_op jit(solution)/shard_map/all_to_all | solution.py:298
  73.5 0.0 copy-done.4
  73.5 0.2 select_reduce_fusion.3
  73.7 0.1 mul.47.pairing_ref
  73.8 0.0 copy-done.5
  73.8 0.1 dynamic_slice.7
  73.9 0.1 dynamic_slice.6
  74.0 0.1 broadcast_add_fusion
  74.0 7.5 %all-to-all-done.2 = f32[8,32,128]{2,1,0:T(8,128)S(1)} async-done(((f32[8,32,128]{2,1,0:T(8,128)}), f32[8,32,128]{2,1,0:T(8,128)S(1)}, u32[]{:S(2)}, u32[]{:S(2)}) %all-to-all-start.2) | async-done | bytes 131104 | tf_op jit(solution)/shard_map/all_to_all | solution.py:298
  81.5 1.8 %shard_map.67 = f32[64,4,128]{2,1,0:T(4,128)} custom-call(f32[256,128]{1,0:T(8,128)} %shard_map.66.own_ref, f32[256,128]{1,0:T(8,128)S(1)} %bitcast.19, f32[128,128]{1,0:T(8,128)S(1)} %mul.47.pairing_ref), custom_call_target="tpu_custom_call" | custom-call | tf_op jit(solution)/shard_map/pallas_call | solution.py:243
  83.4 7.8 %all-to-all-start.3 = ((f32[64,4,128]{2,1,0:T(4,128)}), f32[64,4,128]{2,1,0:T(4,128)S(1)}, u32[]{:S(2)}, u32[]{:S(2)}) async-start(f32[64,4,128]{2,1,0:T(4,128)} %shard_map.67), calls=%async_computation.3 | async-start | bytes 262144 | tf_op jit(solution)/shard_map/all_to_all | solution.py:300
  91.2 0.1 select_reduce_fusion.1
  91.3 0.1 sub.29
  91.4 0.1 sub.30
  91.5 0.1 sub.32
  91.5 10.1 %all-to-all-done.3.parts_ref = f32[64,4,128]{2,1,0:T(4,128)S(1)} async-done(((f32[64,4,128]{2,1,0:T(4,128)}), f32[64,4,128]{2,1,0:T(4,128)S(1)}, u32[]{:S(2)}, u32[]{:S(2)}) %all-to-all-start.3) | async-done | bytes 131104 | tf_op jit(solution)/shard_map/all_to_all | solution.py:300
  101.6 0.7 shard_map.68
  (7 shorter events, 0.1 us)
Async XLA Ops:
  0.0 25.8 %copy-start = (bf16[64,32,512]{2,1,0:T(8,128)(2,1)S(1)}, bf16[64,32,512]{2,1,0:T(8,128)(2,1)}, u32[]{:S(2)}) copy-start(bf16[64,32,512]{2,1,0:T(8,128)(2,1)} %param.7) | copy-start | bytes 6291460
  1.1 35.0 %copy-start.2 = (s32[64]{0:T(128)S(1)}, s32[64]{0:T(128)}, u32[]{:S(2)}) copy-start(s32[64]{0:T(128)} %param.10) | copy-start | bytes 772
  1.1 35.0 %copy-start.3 = (f32[128]{0:T(128)S(1)}, f32[128]{0:T(128)}, u32[]{:S(2)}) copy-start(f32[128]{0:T(128)} %param.11) | copy-start | bytes 1540
  1.1 35.6 %copy-start.1 = (s32[64]{0:T(128)S(1)}, s32[64]{0:T(128)}, u32[]{:S(2)}) copy-start(s32[64]{0:T(128)} %param.8) | copy-start | bytes 772
  1.9 22.1 %all-to-all-start = ((bf16[16,64,128]{2,1,0:T(8,128)(2,1)}), bf16[16,64,128]{2,1,0:T(8,128)(2,1)S(1)}, u32[]{:S(2)}, u32[]{:S(2)}) async-start(bf16[16,64,128]{2,1,0:T(8,128)(2,1)} %bitcast.6), calls=%async_computation | async-start | bytes 524288 | tf_op jit(solution)/shard_map/all_to_all | solution.py:287
  25.8 22.3 %collective-permute-start = (bf16[64,32,512]{2,1,0:T(8,128)(2,1)S(1)}, bf16[64,32,512]{2,1,0:T(8,128)(2,1)}, u32[]{:S(2)}, u32[]{:S(2)}) collective-permute-start(bf16[64,32,512]{2,1,0:T(8,128)(2,1)S(1)} %copy-done), channel_id=1, source_target_pairs={{0,1},{1,0},{2,3},{3,2},{4,5},{5,4},{6,7},{7,6},{8,9},{9,8},{10,11... | collective-permute-start | bytes 6291464 | tf_op jit(solution)/shard_map/ppermute | solution.py:290
  27.8 37.6 %all-to-all-start.1 = ((bf16[8,16,4096]{2,1,0:T(8,128)(2,1)}), bf16[8,16,4096]{2,1,0:T(8,128)(2,1)S(1)}, u32[]{:S(2)}, u32[]{:S(2)}) async-start(bf16[8,16,4096]{2,1,0:T(8,128)(2,1)} %shard_map.64), calls=%async_computation.1 | async-start | bytes 2097152 | tf_op jit(solution)/shard_map/all_to_all | solution.py:289
  36.8 14.0 %collective-permute-start.1 = (bf16[16,64,128]{2,1,0:T(8,128)(2,1)S(1)}, bf16[16,64,128]{2,1,0:T(8,128)(2,1)S(1)}, u32[]{:S(2)}, u32[]{:S(2)}) collective-permute-start(bf16[16,64,128]{2,1,0:T(8,128)(2,1)S(1)} %all-to-all-done.rows_ref.r0_ref), channel_id=1, source_target_pairs={{0,2},{2,4},{4,6},{6,0},{1,3},{3,5},{5,7},{7,1},{8,10},{10,12},{12... | collective-permute-start | bytes 786440 | tf_op jit(solution)/shard_map/ppermute | solution.py:295
  40.0 10.9 %collective-permute-start.2 = (bf16[16,64,128]{2,1,0:T(8,128)(2,1)S(1)}, bf16[16,64,128]{2,1,0:T(8,128)(2,1)S(1)}, u32[]{:S(2)}, u32[]{:S(2)}) collective-permute-start(bf16[16,64,128]{2,1,0:T(8,128)(2,1)S(1)} %all-to-all-done.rows_ref.r0_ref), channel_id=1, source_target_pairs={{0,6},{2,0},{4,2},{6,4},{1,7},{3,1},{5,3},{7,5},{8,14},{10,8},{12,... | collective-permute-start | bytes 786440 | tf_op jit(solution)/shard_map/ppermute | solution.py:295
  43.3 9.9 %collective-permute-start.3 = (bf16[16,64,128]{2,1,0:T(8,128)(2,1)S(1)}, bf16[16,64,128]{2,1,0:T(8,128)(2,1)S(1)}, u32[]{:S(2)}, u32[]{:S(2)}) collective-permute-start(bf16[16,64,128]{2,1,0:T(8,128)(2,1)S(1)} %all-to-all-done.rows_ref.r0_ref), channel_id=1, source_target_pairs={{0,4},{2,6},{4,0},{6,2},{1,5},{3,7},{5,1},{7,3},{8,12},{10,14},{12... | collective-permute-start | bytes 786440 | tf_op jit(solution)/shard_map/ppermute | solution.py:295
  65.3 8.2 %copy-start.4 = (s32[8]{0:T(128)S(1)}, s32[8]{0:T(128)}, u32[]{:S(2)}) copy-start(s32[8]{0:T(128)} %param.9) | copy-start | bytes 100
  65.3 8.5 %copy-start.5 = (f32[64]{0:T(128)S(1)}, f32[64]{0:T(128)}, u32[]{:S(2)}) copy-start(f32[64]{0:T(128)} %select_reduce_fusion) | copy-start | bytes 772
  70.1 11.5 %all-to-all-start.2 = ((f32[8,32,128]{2,1,0:T(8,128)}), f32[8,32,128]{2,1,0:T(8,128)S(1)}, u32[]{:S(2)}, u32[]{:S(2)}) async-start(f32[8,32,128]{2,1,0:T(8,128)} %bitcast.10), calls=%async_computation.2 | async-start | bytes 262144 | tf_op jit(solution)/shard_map/all_to_all | solution.py:298
  83.4 18.3 %all-to-all-start.3 = ((f32[64,4,128]{2,1,0:T(4,128)}), f32[64,4,128]{2,1,0:T(4,128)S(1)}, u32[]{:S(2)}, u32[]{:S(2)}) async-start(f32[64,4,128]{2,1,0:T(4,128)} %shard_map.67), calls=%async_computation.3 | async-start | bytes 262144 | tf_op jit(solution)/shard_map/all_to_all | solution.py:300

commit v14 on v12

--- a/solution.py
+++ b/solution.py
@@ -70,12 +70,12 @@
 
 
 def product_kernel(
-    where_ref, own_ref, other_ref, r0_ref, rp_ref, rm_ref, rt_ref, near_ref, out_ref, amps, bmat, prods, amps_sem, b_sem, out_sem
+    where_ref, own_ref, other_ref, r0_ref, rt_ref, rp_ref, rm_ref, near_ref, out_ref, amps, bmat, prods, amps_sem, b_sem, out_sem
 ):
     x, c = where_ref[0], where_ref[1]
     rights = [
         pltpu.make_async_copy(ref, bmat.at[(x + shift) & 3], b_sem.at[n])
-        for n, (ref, shift) in enumerate(((r0_ref, 0), (rp_ref, 3), (rm_ref, 1), (rt_ref, 2)))
+        for n, (ref, shift) in enumerate(((r0_ref, 0), (rt_ref, 2), (rp_ref, 3), (rm_ref, 1)))
     ]
 
     def load(step, half):
@@ -291,7 +291,7 @@
     )
     left = lax.all_to_all(for_each_plane(where, rows), "z", 0, 0, tiled=True).reshape(128, 4096)
     rights = [rows] + [
-        lax.ppermute(rows, "x", [(i, (i + s) % 4) for i in range(4)]) for s in (1, 3, 2)
+        lax.ppermute(rows, "x", [(i, (i + s) % 4) for i in range(4)]) for s in (2, 1, 3)
     ]
     ladder = ladder_parts(*products(where, amps, amps_other, rights), left)
     crossed = lax.all_to_all(ladder.reshape(8, 32, 128), "z", 0, 0, tiled=True)

time: 103 us -> 103 us (level)
  starting transfers between devices: 41.3 us -> 42.5 us
  waiting for transfers between devices: 37.6 us -> 36.4 us
    ppermute x3, waiting for transfers between devices: 3.32 us -> 2.04 us  [per_device(): lax.ppermute(rows, 'x', [(i, (i + s) % 4) for i in range(4)])]
    ppermute x3, starting transfers between devices: 9.93 us -> 11.1 us  [per_device(): lax.ppermute(rows, 'x', [(i, (i + s) % 4) for i in range(4)])]
where the time goes in v14:
time: 103 us; the launch traced here: 102 us
  starting transfers between devices  42.5 us (41%)
  waiting for transfers between devices  36.4 us (35%)
  Pallas kernels  15.4 us (15%)
  local copies, waits for them, and re-layouts  6.16 us (6%)
  other arithmetic  1.28 us (1%)
    all_to_all x1, waiting for transfers between devices, per_device(): rows = lax.all_to_all(eighths, ('yh', 'yl', 'c'), 0, 0, tiled=True)  11.7 us
    ppermute x3, starting transfers between devices, per_device(): lax.ppermute(rows, 'x', [(i, (i + s) % 4) for i in range(4)])  11.1 us
    all_to_all x1, waiting for transfers between devices, per_device(): parts = lax.all_to_all(parts, GROUP, 0, 0, tiled=True)  10.1 us
    ppermute x1, starting transfers between devices, per_device(): other = lax.ppermute(amplitudes, 'c', [(0, 1), (1, 0)])  8.78 us
    all_to_all x1, starting transfers between devices, per_device(): lax.all_to_all(for_each_plane(where, rows), 'z', 0, 0, tiled=True)  8.42 us
    all_to_all x1, waiting for transfers between devices, per_device(): crossed = lax.all_to_all(ladder.reshape(8, 32, 128), 'z', 0, 0, tiled=True)  7.54 us
    all_to_all x1, starting transfers between devices, per_device(): parts = lax.all_to_all(parts, GROUP, 0, 0, tiled=True)  7.21 us
    pallas_call x1, Pallas kernels, products(): pl.pallas_call(product_kernel, in_specs=[pl.BlockSpec(memory_space=pltpu....  6.19 us
  transfers between devices with their start and end apart: 8, of which 5 were waited for; matrix products, arithmetic and copies ran while one was open for 7% of the time, Pallas kernels for 8%

profile of v14, /device:TPU:1, one launch (start us, length us, event | category | flops | bytes accessed | tf_op | source)
XLA Modules:
  0.0 102.0 jit_solution(17315356492597956445)
XLA Ops:
  0.0 8.8 %collective-permute-start = (bf16[64,32,512]{2,1,0:T(8,128)(2,1)}, bf16[64,32,512]{2,1,0:T(8,128)(2,1)}, u32[]{:S(2)}, u32[]{:S(2)}) collective-permute-start(bf16[64,32,512]{2,1,0:T(8,128)(2,1)} %param.7), channel_id=1, source_target_pairs={{0,1},{1,0},{2,3},{3,2},{4,5},{5,4},{6,7},{7,6},{8,9},{9,8},{10,11... | collective-permute-start | bytes 6291464 | tf_op jit(solution)/shard_map/ppermute | solution.py:288
  8.8 0.9 copy.13
  9.7 0.0 copy-start.2
  9.8 0.0 copy-start.3
  9.8 0.0 copy-start.1
  9.8 0.8 broadcast_in_dim.46
  10.5 0.0 copy-start
  10.5 3.6 %all-to-all-start = ((bf16[16,64,128]{2,1,0:T(8,128)(2,1)}), bf16[16,64,128]{2,1,0:T(8,128)(2,1)S(1)}, u32[]{:S(2)}, u32[]{:S(2)}) async-start(bf16[16,64,128]{2,1,0:T(8,128)(2,1)} %bitcast.8), calls=%async_computation | async-start | bytes 524288 | tf_op jit(solution)/shard_map/all_to_all | solution.py:287
  14.1 0.1 pad_add_fusion.where_ref
  14.2 11.7 %all-to-all-done.r0_ref.rows_ref = bf16[16,64,128]{2,1,0:T(8,128)(2,1)S(1)} async-done(((bf16[16,64,128]{2,1,0:T(8,128)(2,1)}), bf16[16,64,128]{2,1,0:T(8,128)(2,1)S(1)}, u32[]{:S(2)}, u32[]{:S(2)}) %all-to-all-start) | async-done | bytes 262176 | tf_op jit(solution)/shard_map/all_to_all | solution.py:287
  25.9 1.9 %shard_map.65 = bf16[8,16,4096]{2,1,0:T(8,128)(2,1)} custom-call(s32[3]{0:T(128)S(1)} %pad_add_fusion.where_ref, bf16[16,64,128]{2,1,0:T(8,128)(2,1)S(1)} %all-to-all-done.r0_ref.rows_ref), custom_call_target="tpu_custom_call" | custom-call | tf_op jit(solution)/shard_map/pallas_call | solution.py:54
  27.7 8.4 %all-to-all-start.1 = ((bf16[8,16,4096]{2,1,0:T(8,128)(2,1)}), bf16[8,16,4096]{2,1,0:T(8,128)(2,1)S(1)}, u32[]{:S(2)}, u32[]{:S(2)}) async-start(bf16[8,16,4096]{2,1,0:T(8,128)(2,1)} %shard_map.65), calls=%async_computation.1 | async-start | bytes 2097152 | tf_op jit(solution)/shard_map/all_to_all | solution.py:292
  36.1 0.0 copy-done.2
  36.1 0.0 copy-done.3
  36.2 0.7 select_reduce_fusion
  36.8 0.0 copy-done.1
  36.8 0.1 compare_convert_fusion
  36.9 4.6 %collective-permute-start.1 = (bf16[16,64,128]{2,1,0:T(8,128)(2,1)S(1)}, bf16[16,64,128]{2,1,0:T(8,128)(2,1)S(1)}, u32[]{:S(2)}, u32[]{:S(2)}) collective-permute-start(bf16[16,64,128]{2,1,0:T(8,128)(2,1)S(1)} %all-to-all-done.r0_ref.rows_ref), channel_id=1, source_target_pairs={{0,4},{2,6},{4,0},{6,2},{1,5},{3,7},{5,1},{7,3},{8,12},{10,14},{12... | collective-permute-start | bytes 786440 | tf_op jit(solution)/shard_map/ppermute | solution.py:294
  41.6 2.2 %collective-permute-start.2 = (bf16[16,64,128]{2,1,0:T(8,128)(2,1)S(1)}, bf16[16,64,128]{2,1,0:T(8,128)(2,1)S(1)}, u32[]{:S(2)}, u32[]{:S(2)}) collective-permute-start(bf16[16,64,128]{2,1,0:T(8,128)(2,1)S(1)} %all-to-all-done.r0_ref.rows_ref), channel_id=1, source_target_pairs={{0,2},{2,4},{4,6},{6,0},{1,3},{3,5},{5,7},{7,1},{8,10},{10,12},{12... | collective-permute-start | bytes 786440 | tf_op jit(solution)/shard_map/ppermute | solution.py:294
  43.8 4.3 %collective-permute-start.3 = (bf16[16,64,128]{2,1,0:T(8,128)(2,1)S(1)}, bf16[16,64,128]{2,1,0:T(8,128)(2,1)S(1)}, u32[]{:S(2)}, u32[]{:S(2)}) collective-permute-start(bf16[16,64,128]{2,1,0:T(8,128)(2,1)S(1)} %all-to-all-done.r0_ref.rows_ref), channel_id=1, source_target_pairs={{0,6},{2,0},{4,2},{6,4},{1,7},{3,1},{5,3},{7,5},{8,14},{10,8},{12,... | collective-permute-start | bytes 786440 | tf_op jit(solution)/shard_map/ppermute | solution.py:294
  48.1 0.0 copy-done
  48.1 1.2 %copy.10 = bf16[32,64,512]{2,1,0:T(8,128)(2,1)S(1)} copy(bf16[32,64,512]{2,0,1:T(8,128)(2,1)S(1)} %bitcast.20) | data formatting | bytes 4194304 | tf_op jit(solution)/shard_map/transpose | solution.py:290
  49.3 0.1 broadcast_multiply_fusion
  49.4 0.0 collective-permute-done
  49.4 2.8 %copy.11 = bf16[32,64,512]{2,1,0:T(8,128)(2,1)S(1)} copy(bf16[32,64,512]{2,0,1:T(8,128)(2,1)} %bitcast.5) | data formatting | bytes 4194304 | tf_op jit(solution)/shard_map/transpose | solution.py:290
  52.1 0.0 collective-permute-done.1.rt_ref
  52.1 2.0 %collective-permute-done.2.rp_ref = bf16[16,64,128]{2,1,0:T(8,128)(2,1)S(1)} collective-permute-done((bf16[16,64,128]{2,1,0:T(8,128)(2,1)S(1)}, bf16[16,64,128]{2,1,0:T(8,128)(2,1)S(1)}, u32[]{:S(2)}, u32[]{:S(2)}) %collective-permute-start.2) | collective-permute-done | bytes 262176 | tf_op jit(solution)/shard_map/ppermute | solution.py:294
  54.2 0.0 collective-permute-done.3.rm_ref
  54.2 6.2 %shard_map.64 = (bf16[512,2048]{1,0:T(8,128)(2,1)S(1)}, bf16[3,512,2048]{2,1,0:T(8,128)(2,1)}) custom-call(s32[3]{0:T(128)S(1)} %pad_add_fusion.where_ref, bf16[4,8,64,512]{3,2,1,0:T(8,128)(2,1)S(1)} %bitcast.17, bf16[4,8,64,512]{3,2,1,0:T(8,128)(2,1)S(1)} %bitcast.18, bf16[16,64,128]{2,1,0:T(8,128)(2,1)S(1)} %all-to-all-done.r0_ref.rows_ref, ...), custom_call_target="tpu_custom_call" | custom-call | flops 4294967296 | bytes 14680064 | tf_op jit(solution)/shard_map/pallas_call | solution.py:144
  60.4 5.1 %all-to-all-done.1 = bf16[8,16,4096]{2,1,0:T(8,128)(2,1)S(1)} async-done(((bf16[8,16,4096]{2,1,0:T(8,128)(2,1)}), bf16[8,16,4096]{2,1,0:T(8,128)(2,1)S(1)}, u32[]{:S(2)}, u32[]{:S(2)}) %all-to-all-start.1) | async-done | bytes 1048608 | tf_op jit(solution)/shard_map/all_to_all | solution.py:292
  65.5 0.0 copy-start.4
  65.5 0.0 copy-start.5
  65.5 4.8 %shard_map.66.own_ref = f32[256,128]{1,0:T(8,128)} custom-call(bf16[512,2048]{1,0:T(8,128)(2,1)S(1)} %get-tuple-element.7.near_ref, bf16[3,512,2048]{2,1,0:T(8,128)(2,1)} %get-tuple-element.8.prod_ref, bf16[128,4096]{1,0:T(8,128)(2,1)S(1)} %bitcast.16), custom_call_target="tpu_custom_call" | custom-call | flops 536870912 | bytes 9437184 | tf_op jit(solution)/shard_map/pallas_call | solution.py:196
  70.3 3.4 %all-to-all-start.2 = ((f32[8,32,128]{2,1,0:T(8,128)}), f32[8,32,128]{2,1,0:T(8,128)S(1)}, u32[]{:S(2)}, u32[]{:S(2)}) async-start(f32[8,32,128]{2,1,0:T(8,128)} %bitcast.10), calls=%async_computation.2 | async-start | bytes 262144 | tf_op jit(solution)/shard_map/all_to_all | solution.py:297
  73.7 0.0 copy-done.4
  73.7 0.2 select_reduce_fusion.3
  73.9 0.1 mul.47.pairing_ref
  74.0 0.0 copy-done.5
  74.0 0.1 dynamic_slice.7
  74.1 0.1 dynamic_slice.6
  74.1 0.1 broadcast_add_fusion
  74.2 7.5 %all-to-all-done.2 = f32[8,32,128]{2,1,0:T(8,128)S(1)} async-done(((f32[8,32,128]{2,1,0:T(8,128)}), f32[8,32,128]{2,1,0:T(8,128)S(1)}, u32[]{:S(2)}, u32[]{:S(2)}) %all-to-all-start.2) | async-done | bytes 131104 | tf_op jit(solution)/shard_map/all_to_all | solution.py:297
  81.8 1.8 %shard_map.67 = f32[64,4,128]{2,1,0:T(4,128)} custom-call(f32[256,128]{1,0:T(8,128)} %shard_map.66.own_ref, f32[256,128]{1,0:T(8,128)S(1)} %bitcast.19, f32[128,128]{1,0:T(8,128)S(1)} %mul.47.pairing_ref), custom_call_target="tpu_custom_call" | custom-call | tf_op jit(solution)/shard_map/pallas_call | solution.py:243
  83.6 7.2 %all-to-all-start.3 = ((f32[64,4,128]{2,1,0:T(4,128)}), f32[64,4,128]{2,1,0:T(4,128)S(1)}, u32[]{:S(2)}, u32[]{:S(2)}) async-start(f32[64,4,128]{2,1,0:T(4,128)} %shard_map.67), calls=%async_computation.3 | async-start | bytes 262144 | tf_op jit(solution)/shard_map/all_to_all | solution.py:299
  90.8 0.1 select_reduce_fusion.1
  90.9 0.1 sub.29
  91.0 0.1 sub.30
  91.1 0.1 sub.32
  91.2 10.1 %all-to-all-done.3.parts_ref = f32[64,4,128]{2,1,0:T(4,128)S(1)} async-done(((f32[64,4,128]{2,1,0:T(4,128)}), f32[64,4,128]{2,1,0:T(4,128)S(1)}, u32[]{:S(2)}, u32[]{:S(2)}) %all-to-all-start.3) | async-done | bytes 131104 | tf_op jit(solution)/shard_map/all_to_all | solution.py:299
  101.2 0.7 shard_map.68
  (7 shorter events, 0.1 us)
Async XLA Ops:
  0.0 49.4 %collective-permute-start = (bf16[64,32,512]{2,1,0:T(8,128)(2,1)}, bf16[64,32,512]{2,1,0:T(8,128)(2,1)}, u32[]{:S(2)}, u32[]{:S(2)}) collective-permute-start(bf16[64,32,512]{2,1,0:T(8,128)(2,1)} %param.7), channel_id=1, source_target_pairs={{0,1},{1,0},{2,3},{3,2},{4,5},{5,4},{6,7},{7,6},{8,9},{9,8},{10,11... | collective-permute-start | bytes 6291464 | tf_op jit(solution)/shard_map/ppermute | solution.py:288
  9.7 26.4 %copy-start.2 = (s32[64]{0:T(128)S(1)}, s32[64]{0:T(128)}, u32[]{:S(2)}) copy-start(s32[64]{0:T(128)} %param.10) | copy-start | bytes 772
  9.8 26.4 %copy-start.3 = (f32[128]{0:T(128)S(1)}, f32[128]{0:T(128)}, u32[]{:S(2)}) copy-start(f32[128]{0:T(128)} %param.11) | copy-start | bytes 1540
  9.8 27.1 %copy-start.1 = (s32[64]{0:T(128)S(1)}, s32[64]{0:T(128)}, u32[]{:S(2)}) copy-start(s32[64]{0:T(128)} %param.8) | copy-start | bytes 772
  10.5 37.6 %copy-start = (bf16[64,32,512]{2,1,0:T(8,128)(2,1)S(1)}, bf16[64,32,512]{2,1,0:T(8,128)(2,1)}, u32[]{:S(2)}) copy-start(bf16[64,32,512]{2,1,0:T(8,128)(2,1)} %param.7) | copy-start | bytes 6291460
  10.5 15.3 %all-to-all-start = ((bf16[16,64,128]{2,1,0:T(8,128)(2,1)}), bf16[16,64,128]{2,1,0:T(8,128)(2,1)S(1)}, u32[]{:S(2)}, u32[]{:S(2)}) async-start(bf16[16,64,128]{2,1,0:T(8,128)(2,1)} %bitcast.8), calls=%async_computation | async-start | bytes 524288 | tf_op jit(solution)/shard_map/all_to_all | solution.py:287
  27.7 37.8 %all-to-all-start.1 = ((bf16[8,16,4096]{2,1,0:T(8,128)(2,1)}), bf16[8,16,4096]{2,1,0:T(8,128)(2,1)S(1)}, u32[]{:S(2)}, u32[]{:S(2)}) async-start(bf16[8,16,4096]{2,1,0:T(8,128)(2,1)} %shard_map.65), calls=%async_computation.1 | async-start | bytes 2097152 | tf_op jit(solution)/shard_map/all_to_all | solution.py:292
  36.9 15.2 %collective-permute-start.1 = (bf16[16,64,128]{2,1,0:T(8,128)(2,1)S(1)}, bf16[16,64,128]{2,1,0:T(8,128)(2,1)S(1)}, u32[]{:S(2)}, u32[]{:S(2)}) collective-permute-start(bf16[16,64,128]{2,1,0:T(8,128)(2,1)S(1)} %all-to-all-done.r0_ref.rows_ref), channel_id=1, source_target_pairs={{0,4},{2,6},{4,0},{6,2},{1,5},{3,7},{5,1},{7,3},{8,12},{10,14},{12... | collective-permute-start | bytes 786440 | tf_op jit(solution)/shard_map/ppermute | solution.py:294
  41.6 12.6 %collective-permute-start.2 = (bf16[16,64,128]{2,1,0:T(8,128)(2,1)S(1)}, bf16[16,64,128]{2,1,0:T(8,128)(2,1)S(1)}, u32[]{:S(2)}, u32[]{:S(2)}) collective-permute-start(bf16[16,64,128]{2,1,0:T(8,128)(2,1)S(1)} %all-to-all-done.r0_ref.rows_ref), channel_id=1, source_target_pairs={{0,2},{2,4},{4,6},{6,0},{1,3},{3,5},{5,7},{7,1},{8,10},{10,12},{12... | collective-permute-start | bytes 786440 | tf_op jit(solution)/shard_map/ppermute | solution.py:294
  43.8 10.4 %collective-permute-start.3 = (bf16[16,64,128]{2,1,0:T(8,128)(2,1)S(1)}, bf16[16,64,128]{2,1,0:T(8,128)(2,1)S(1)}, u32[]{:S(2)}, u32[]{:S(2)}) collective-permute-start(bf16[16,64,128]{2,1,0:T(8,128)(2,1)S(1)} %all-to-all-done.r0_ref.rows_ref), channel_id=1, source_target_pairs={{0,6},{2,0},{4,2},{6,4},{1,7},{3,1},{5,3},{7,5},{8,14},{10,8},{12,... | collective-permute-start | bytes 786440 | tf_op jit(solution)/shard_map/ppermute | solution.py:294
  65.5 8.2 %copy-start.4 = (s32[8]{0:T(128)S(1)}, s32[8]{0:T(128)}, u32[]{:S(2)}) copy-start(s32[8]{0:T(128)} %param.9) | copy-start | bytes 100
  65.5 8.5 %copy-start.5 = (f32[64]{0:T(128)S(1)}, f32[64]{0:T(128)}, u32[]{:S(2)}) copy-start(f32[64]{0:T(128)} %select_reduce_fusion) | copy-start | bytes 772
  70.3 11.5 %all-to-all-start.2 = ((f32[8,32,128]{2,1,0:T(8,128)}), f32[8,32,128]{2,1,0:T(8,128)S(1)}, u32[]{:S(2)}, u32[]{:S(2)}) async-start(f32[8,32,128]{2,1,0:T(8,128)} %bitcast.10), calls=%async_computation.2 | async-start | bytes 262144 | tf_op jit(solution)/shard_map/all_to_all | solution.py:297
  83.6 17.6 %all-to-all-start.3 = ((f32[64,4,128]{2,1,0:T(4,128)}), f32[64,4,128]{2,1,0:T(4,128)S(1)}, u32[]{:S(2)}, u32[]{:S(2)}) async-start(f32[64,4,128]{2,1,0:T(4,128)} %shard_map.67), calls=%async_computation.3 | async-start | bytes 262144 | tf_op jit(solution)/shard_map/all_to_all | solution.py:299
